TPU v7x, 256 devices: a whole 4x4x8 slice. The times are simulated.
256 devices in a mesh: fsdp: 64 (over z, y, core), tp: 4 (over x).
Axes of the slice: x: 4, y: 4, z: 8, core: 2. Of those that a mesh axis runs over, the one named last changes fastest.
Arguments:
- gradient: bfloat16 [8192, 22528], P('fsdp', 'tp'), may hold values from -6 to 6
- momentum: float32 [8192, 22528], P('fsdp', 'tp'), may hold values from -140 to 140, as said below
- weight: float32 [8192, 22528], P('fsdp', 'tp'), may hold values from -0.12 to 0.12
- basis: float32 [22528, 256], P(('tp', 'fsdp')), may hold values from -6 to 6
Outputs:
- new_momentum: float32 [8192, 22528], P('fsdp', 'tp')
- new_weight: float32 [8192, 22528], P('fsdp', 'tp')
- new_basis: float32 [22528, 256], P(('tp', 'fsdp'))
Inputs may be any that keep to these rules, and one draw needn't show every extreme that they name: Real-valued momentum, rows and columns of differing scales.
All inputs are finite; a program needn't handle non-finite values.
Results may differ from a plain program's by a relative error of at most 0.0003.
Values sent between devices are 32-bit elements; how exact they have to be, the bound alone decides.
No kernel may reach another device: no remote copies, remote signals or barrier semaphores. Data moves between devices by JAX's collectives and lax.ppermute only.
A program may use at most 128 MiB of HBM per device.

v0:
```python
import math

import jax
import jax.numpy as jnp
from jax import lax
from jax.experimental import pallas as pl
from jax.experimental.pallas import tpu as pltpu
from jax.sharding import Mesh, PartitionSpec as P

D = 8192
FF = 22528
RANK = 256
NZ, NY, NC, NX = 8, 4, 2, 4


epsilon = 1e-06
feedback_keep = 0.05
step_rate = 0.1
weight_decay = 0.1

VMEM_BYTES = 50 * 1024 * 1024
HIGHEST = lax.Precision.HIGHEST


def dot(left, right, left_dim, right_dim, precision=lax.Precision.HIGH):
    return lax.dot_general(
        left,
        right,
        (((left_dim,), (right_dim,)), ((), ())),
        precision=precision,
        preferred_element_type=jnp.float32,
    )


def gather(block, axes, count):
    copies = jnp.broadcast_to(block[None], (count,) + block.shape)
    return lax.all_to_all(copies, axes, 0, 0)


def scatter_sum(blocks, axes):
    return jnp.sum(lax.all_to_all(blocks, axes, 0, 0), axis=0)


def swap(block):
    return lax.ppermute(block, "c", [(0, 1), (1, 0)])


def shift(block, axis, size, step):
    return lax.ppermute(block, axis, [(i, (i + step) % size) for i in range(size)])


def halves(value):
    high = value.astype(jnp.bfloat16)
    low = (value - high.astype(jnp.float32)).astype(jnp.bfloat16)
    return high, low


def dot_halves(left, right, left_dim, right_dim):
    def one(a, b):
        return lax.dot_general(
            a,
            b,
            (((left_dim,), (right_dim,)), ((), ())),
            preferred_element_type=jnp.float32,
        )

    (lh, ll), (rh, rl) = left, right
    return one(lh, rh) + (one(lh, rl) + one(ll, rh))


def params():
    return pltpu.CompilerParams(vmem_limit_bytes=VMEM_BYTES)


def cost(flops, size):
    return pl.CostEstimate(flops=flops, bytes_accessed=size, transcendentals=0)


def smem():
    return pl.BlockSpec(memory_space=pltpu.SMEM)


def split_kernel(pos, grad, mom, out0, out1, out2, out3, turned):
    y = pos[0]
    turned[...] = (mom[...] + grad[...].astype(jnp.float32)).T
    size = out0.shape[1]
    for d, out in enumerate((out0, out1, out2, out3)):
        owner = lax.rem(y + d, NY)
        for part in range(out.shape[0]):
            start = pl.multiple_of((part * NY + owner) * size, 8)
            out[part] = turned[pl.ds(start, size), :]


def split_columns(pos, gradient, momentum):
    rows, cols = momentum.shape
    wide = 2 * cols // NZ
    size = wide // (2 * NY)
    block = pl.BlockSpec((rows, wide), lambda i: (0, i))
    piece = pl.BlockSpec((2, size, rows), lambda i: (i, 0, 0))
    return pl.pallas_call(
        split_kernel,
        grid=(NZ // 2,),
        in_specs=[smem(), block, block],
        out_specs=[piece] * NY,
        out_shape=[jax.ShapeDtypeStruct((NZ, size, rows), jnp.float32)] * NY,
        scratch_shapes=[pltpu.VMEM((wide, rows), jnp.float32)],
        compiler_params=params(),
        cost_estimate=cost(0, rows * cols * 10),
    )(pos, gradient, momentum)


def project_kernel(pos, s0, s1, s2, s3, mine, other, out, full):
    y, core = pos[0], pos[1]
    half = mine.shape[1]
    for z in range(NZ):
        start = pl.multiple_of(z * 2 * half + core * half, 8)
        full[pl.ds(start, half), :] = mine[z]
        start = pl.multiple_of(z * 2 * half + (1 - core) * half, 8)
        full[pl.ds(start, half), :] = other[z]
    right = halves(full[...])
    for d, strip in enumerate((s0, s1, s2, s3)):
        left = halves(strip[...])
        out[lax.rem(y + NY - d, NY)] = dot_halves(left, right, 0, 0)


def project(pos, strips, mine, other):
    cols, rows = strips[0].shape
    return pl.pallas_call(
        project_kernel,
        in_specs=[smem()] + [pl.BlockSpec(memory_space=pltpu.VMEM)] * 6,
        out_specs=pl.BlockSpec(memory_space=pltpu.VMEM),
        out_shape=jax.ShapeDtypeStruct((NY, rows, RANK), jnp.float32),
        scratch_shapes=[pltpu.VMEM((cols, RANK), jnp.float32)],
        compiler_params=params(),
        cost_estimate=cost(6 * NY * rows * cols * RANK, NY * rows * cols * 8),
    )(pos, *strips, mine, other)


def feedback_kernel(pos, s0, s1, s2, s3, proj, gram, mine, other, low, high, full):
    y, core = pos[0], pos[1]
    rows = s0.shape[2]
    half = mine.shape[1] - gram.shape[0]

    @pl.when(pl.program_id(0) == 0)
    def _():
        for d in range(NY):
            top, rest = halves(proj[lax.rem(y + NY - d, NY)])
            high[d * rows : (d + 1) * rows] = top
            low[d * rows : (d + 1) * rows] = rest

    strip = jnp.concatenate([s0[0], s1[0], s2[0], s3[0]], axis=1)
    full[...] = dot_halves(halves(strip), (high[...], low[...]), 1, 0)
    mine[0, :half] = full[pl.ds(pl.multiple_of(core * half, 8), half), :]
    other[0, :half] = full[pl.ds(pl.multiple_of((1 - core) * half, 8), half), :]
    mine[0, half:] = gram[...]
    other[0, half:] = gram[...]


def raw_feedback(pos, strips, proj, gram):
    _, size, rows = strips[0].shape
    part = gram.shape[0]
    strip = pl.BlockSpec((1, size, rows), lambda z: (z, 0, 0))
    whole = lambda shape: pl.BlockSpec(shape, lambda z: (0,) * len(shape))
    out = pl.BlockSpec((1, size // 2 + part, RANK), lambda z: (z, 0, 0))
    return pl.pallas_call(
        feedback_kernel,
        grid=(NZ,),
        in_specs=[smem()] + [strip] * NY + [whole(proj.shape), whole(gram.shape)],
        out_specs=[out] * 2,
        out_shape=[jax.ShapeDtypeStruct((NZ, size // 2 + part, RANK), jnp.float32)] * 2,
        scratch_shapes=[
            pltpu.VMEM((NY * rows, RANK), jnp.bfloat16),
            pltpu.VMEM((NY * rows, RANK), jnp.bfloat16),
            pltpu.VMEM((size, RANK), jnp.float32),
        ],
        compiler_params=params(),
        cost_estimate=cost(6 * NY * rows * NZ * size * RANK, NZ * size * rows * 24),
    )(pos, *strips, proj, gram)


BLOCK = 64


def small_inverse(block):
    rows = lax.broadcasted_iota(jnp.int32, (BLOCK, BLOCK), 0)
    cols = lax.broadcasted_iota(jnp.int32, (BLOCK, BLOCK), 1)
    unit = (rows == cols).astype(jnp.float32)
    wide = jnp.concatenate([block, unit], axis=1)
    tiles = [wide[8 * t : 8 * t + 8] for t in range(BLOCK // 8)]
    place = lax.broadcasted_iota(jnp.int32, (8, 2 * BLOCK), 0)
    scale = [jnp.zeros((8, 2 * BLOCK), jnp.float32) for _ in tiles]
    for j in range(BLOCK):
        tile, row = divmod(j, 8)
        line = jnp.broadcast_to(tiles[tile][row : row + 1], (8, 2 * BLOCK))
        pivot = jnp.broadcast_to(line[:, j : j + 1], (8, 2 * BLOCK))
        line = line * (1.0 / pivot)
        scale[tile] = jnp.where(place == row, pivot, scale[tile])
        for t in range(tile, BLOCK // 8):
            factor = jnp.broadcast_to(tiles[t][:, j : j + 1], (8, 2 * BLOCK))
            if t == tile:
                factor = jnp.where(place > row, factor, 0.0)
            tiles[t] = tiles[t] - factor * line
    tiles = [t * (1.0 / jnp.sqrt(s)) for t, s in zip(tiles, scale)]
    return jnp.concatenate(tiles, axis=0)[:, BLOCK:]


def inverse_kernel(gram, out, work, lower):
    work[...] = gram[...]
    out[...] = jnp.zeros_like(out)
    count = RANK // BLOCK
    for k in range(count):
        at, end = k * BLOCK, (k + 1) * BLOCK
        small = small_inverse(work[at:end, at:end])
        if k + 1 < count:
            panel = dot(work[end:, at:end], small, 1, 1, HIGHEST)
            lower[end:, at:end] = panel
            work[end:, end:] = work[end:, end:] - dot(panel, panel, 1, 1, HIGHEST)
        if k:
            above = dot(lower[at:end, :at], out[:at, :at], 1, 0, HIGHEST)
            out[at:end, :at] = -dot(small, above, 1, 0, HIGHEST)
        out[at:end, at:end] = small


def factor_inverse(gram):
    return pl.pallas_call(
        inverse_kernel,
        in_specs=[pl.BlockSpec(memory_space=pltpu.VMEM)],
        out_specs=pl.BlockSpec(memory_space=pltpu.VMEM),
        out_shape=jax.ShapeDtypeStruct((RANK, RANK), jnp.float32),
        scratch_shapes=[pltpu.VMEM((RANK, RANK), jnp.float32)] * 2,
        compiler_params=params(),
        cost_estimate=cost(10_000_000_000, 1_000_000),
    )(gram)


def update_kernel(pos, left, grad, mom, wgt, *refs):
    mine, other = refs[0:5], refs[5:10]
    new_mom, new_wgt, full = refs[10:]
    y, core, i = pos[0], pos[1], pl.program_id(0)
    half = mine[0].shape[1]

    def place(ref, d, first):
        owner = lax.rem(y + NY - d, NY)
        for part in range(2):
            start = ((part * NY + owner) * 2 + first) * half
            full[pl.ds(pl.multiple_of(start, 8), half), :] = ref[part]

    for group, first in ((mine, core), (other, 1 - core)):
        place(group[0], 0, first)
        place(group[1], 1, first)
        place(group[2], 3, first)

        @pl.when(i < 2)
        def _():
            place(group[3], 2, first)

        @pl.when(i >= 2)
        def _():
            place(group[4], 2, first)

    rows = mom.shape[0]
    both = dot_halves(halves(left[...]), halves(full[...]), 1, 1)
    coeff = step_rate * math.sqrt(D / RANK) / math.sqrt(FF)
    keep = 1.0 - step_rate * weight_decay
    summed = mom[...] + grad[...].astype(jnp.float32)
    new_mom[...] = summed - feedback_keep * both[:rows]
    new_wgt[...] = keep * wgt[...] - coeff * both[rows:]


def update(pos, left, gradient, momentum, weight, mine, other):
    rows, cols = momentum.shape
    wide = 2 * cols // NZ
    half = mine[0].shape[1]
    block = pl.BlockSpec((rows, wide), lambda i: (0, i))
    piece = pl.BlockSpec((2, half, RANK), lambda i: (i, 0, 0))
    early = pl.BlockSpec((2, half, RANK), lambda i: (jnp.minimum(i, 1), 0, 0))
    late = pl.BlockSpec((2, half, RANK), lambda i: (jnp.maximum(i - 2, 0), 0, 0))
    pieces = [piece] * 3 + [early, late]
    whole = pl.BlockSpec(left.shape, lambda i: (0, 0))
    return pl.pallas_call(
        update_kernel,
        grid=(NZ // 2,),
        in_specs=[smem(), whole, block, block, block] + pieces + pieces,
        out_specs=[block, block],
        out_shape=[jax.ShapeDtypeStruct(momentum.shape, jnp.float32)] * 2,
        scratch_shapes=[pltpu.VMEM((wide, RANK), jnp.float32)],
        compiler_params=params(),
        cost_estimate=cost(12 * rows * cols * RANK, rows * cols * 18),
    )(pos, left, gradient, momentum, weight, *mine, *other)


def body(gradient, momentum, weight, basis):
    core, y, x = lax.axis_index("c"), lax.axis_index("y"), lax.axis_index("x")
    pos = jnp.stack([y, core]).astype(jnp.int32)
    rows, cols = momentum.shape
    shard = basis.shape[0]

    basis_z = gather(basis, "z", NZ)

    sent = split_columns(pos, gradient, momentum)
    strips = [sent[0]] + [shift(sent[d], "y", NY, d) for d in range(1, NY)]
    flat = [strip.reshape(NZ * NC * shard, rows) for strip in strips]

    partial_proj = project(pos, flat, basis_z, swap(basis_z))
    few = rows // NX
    few_rows = scatter_sum(partial_proj.reshape(NY * NX, few, RANK), ("y", "x"))
    group_proj = gather(few_rows, ("y", "x"), NY * NX).reshape(NY, rows, RANK)
    projected = lax.dynamic_index_in_dim(group_proj, y, 0, keepdims=False)

    part = RANK // (NY * NX)
    all_rows = group_proj.reshape(NY * rows, RANK)
    gram_group = dot(all_rows, all_rows, 0, 0, HIGHEST)
    gram_part = lax.dynamic_slice_in_dim(gram_group, (y * NX + x) * part, part, 0)

    mine, other = raw_feedback(pos, strips, group_proj, gram_part)
    reduced = scatter_sum(mine + swap(other), "z")
    raw_shard, gram_part = reduced[:shard], reduced[shard:]

    raw = gather(raw_shard, "z", NZ)
    ahead = shift(raw, "y", NY, 1)
    behind = shift(raw, "y", NY, NY - 1)
    ahead2 = shift(ahead[: NZ // 2], "y", NY, 1)
    behind2 = shift(behind[NZ // 2 :], "y", NY, NY - 1)
    own = [raw, ahead, behind, ahead2, behind2]
    paired = [swap(block) for block in own]

    by_y = jnp.stack([gram_part] + [shift(gram_part, "y", NY, d) for d in range(1, NY)])
    by_x = jnp.stack([by_y] + [shift(by_y, "x", NX, d) for d in range(1, NX)])
    by_x = jnp.flip(jnp.concatenate([by_x, by_x], 0), 0)
    by_x = lax.dynamic_slice_in_dim(by_x, NX - 1 - x, NX, 0)
    by_y = jnp.flip(jnp.concatenate([by_x, by_x], 1), 1)
    by_y = lax.dynamic_slice_in_dim(by_y, NY - 1 - y, NY, 1)
    gram_matrix = jnp.swapaxes(by_y, 0, 1).reshape(RANK, RANK)
    inverse = factor_inverse(gram_matrix)

    orthonormal = dot(projected, inverse, 1, 1, HIGHEST)
    strip_feedback = dot(raw.reshape(NZ * shard, RANK), inverse, 1, 1)
    squares = jnp.sum(strip_feedback * strip_feedback, axis=0, keepdims=True)
    squares = squares + swap(squares)
    squares = jnp.sum(gather(squares, ("y", "x"), NY * NX), axis=0)
    scales = math.sqrt(FF) / (jnp.sqrt(squares) + epsilon)

    left = jnp.concatenate([orthonormal, orthonormal * scales], axis=0)
    left = dot(left, inverse, 1, 0, HIGHEST)
    new_momentum, new_weight = update(
        pos, left, gradient, momentum, weight, own, paired
    )
    new_basis = dot(raw_shard, inverse, 1, 1) * scales
    return (new_momentum, new_weight, new_basis)


def solution(mesh):
    fine = Mesh(mesh.devices.reshape(NZ, NY, NC, NX), ("z", "y", "c", "x"))
    matrix = P(("z", "y", "c"), "x")
    tall = P(("x", "z", "y", "c"), None)
    return jax.shard_map(
        body,
        mesh=fine,
        in_specs=(matrix, matrix, matrix, tall),
        out_specs=(matrix, matrix, tall),
        check_vma=False,
    )
```

profile of v0, /device:TPU:1, one launch (start us, length us, event | category | flops | bytes accessed | tf_op | source)
XLA Modules:
  0.0 236.7 jit_solution(17267933188710993095)
XLA Ops:
  0.6 1.8 broadcast_in_dim.12
  2.5 9.0 %all-to-all-start = ((f32[8,88,256]{2,1,0:T(8,128)}), f32[8,88,256]{2,1,0:T(8,128)}, u32[]{:S(2)}, u32[]{:S(2)}) async-start(f32[8,88,256]{2,1,0:T(8,128)} %broadcast_in_dim.12), calls=%async_computation | async-start | bytes 1441792 | tf_op jit(solution)/shard_map/all_to_all | solution.py:37
  11.5 0.1 pad_add_fusion.pos
  11.5 4.8 %shard_map.67 = (f32[8,176,128]{2,1,0:T(8,128)S(1)}, f32[8,176,128]{2,1,0:T(8,128)}, f32[8,176,128]{2,1,0:T(8,128)}, f32[8,176,128]{2,1,0:T(8,128)}) custom-call(s32[2]{0:T(128)S(1)} %pad_add_fusion.pos, bf16[128,5632]{1,0:T(8,128)(2,1)} %grad.3, f32[128,5632]{1,0:T(8,128)} %mom.3), custom_call_target="tpu_custom_call" | custom-call | bytes 7208960 | tf_op jit(solution)/shard_map/pallas_call | solution.py:100
  16.4 1.3 collective-permute-start
  17.7 2.6 %collective-permute-start.1 = (f32[8,176,128]{2,1,0:T(8,128)}, f32[8,176,128]{2,1,0:T(8,128)S(1)}, u32[]{:S(2)}, u32[]{:S(2)}) collective-permute-start(f32[8,176,128]{2,1,0:T(8,128)} %get-tuple-element.13), channel_id=1, source_target_pairs={{0,16},{8,24},{16,0},{24,8},{1,17},{9,25},{17,1},{25,9},{2,18},{10... | collective-permute-start | bytes 2162696 | tf_op jit(solution)/shard_map/ppermute | solution.py:49
  20.3 1.1 collective-permute-start.2
  21.4 12.4 %all-to-all-done.mine = f32[8,88,256]{2,1,0:T(8,128)} async-done(((f32[8,88,256]{2,1,0:T(8,128)}), f32[8,88,256]{2,1,0:T(8,128)}, u32[]{:S(2)}, u32[]{:S(2)}) %all-to-all-start) | async-done | bytes 720928 | tf_op jit(solution)/shard_map/all_to_all | solution.py:37
  33.7 0.5 collective-permute-start.3
  34.2 0.4 collective-permute-done.s1
  34.7 16.5 %collective-permute-done.1.s2 = f32[8,176,128]{2,1,0:T(8,128)S(1)} collective-permute-done((f32[8,176,128]{2,1,0:T(8,128)}, f32[8,176,128]{2,1,0:T(8,128)S(1)}, u32[]{:S(2)}, u32[]{:S(2)}) %collective-permute-start.1) | collective-permute-done | bytes 720928 | tf_op jit(solution)/shard_map/ppermute | solution.py:49
  51.2 0.0 collective-permute-done.3.other
  51.2 0.0 copy-start.2
  51.2 0.9 copy-done.2
  52.1 2.9 %shard_map.68 = f32[4,128,256]{2,1,0:T(8,128)S(1)} custom-call(s32[2]{0:T(128)S(1)} %pad_add_fusion.pos, f32[1408,128]{1,0:T(8,128)S(1)} %bitcast.49, f32[1408,128]{1,0:T(8,128)S(1)} %bitcast.50, f32[1408,128]{1,0:T(8,128)S(1)} %bitcast.51, f32[1408,128]{1,0:T(8,128)S(1)} %bitcast.52, f32[8,88,256]{2,1,0:T(8,128)} %all-to-all-done.mine, f32[8,88,256]{2,1,0:T(8,128)} %copy-done.2), custom_call_target="tpu_custom_call" | custom-call | flops 1107296256 | bytes 5767168 | tf_op jit(solution)/shard_map/pallas_call | solution.py:128
  55.0 17.4 %all_to_all.30 = f32[16,32,256]{2,1,0:T(8,128)} all-to-all(f32[16,32,256]{2,1,0:T(8,128)S(1)} %bitcast.46), channel_id=1, replica_groups=mesh['z'=8,'y'=4,'c'=2,'x'=4] {'y','x'}, dimensions={0} | all-to-all | bytes 1048576 | tf_op jit(solution)/shard_map/all_to_all | solution.py:41
  72.4 1.1 reduce_sum.36
  73.4 0.8 broadcast_in_dim.13
  74.3 3.6 %all-to-all-start.2 = ((f32[16,32,256]{2,1,0:T(8,128)}), f32[16,32,256]{2,1,0:T(8,128)S(1)}, u32[]{:S(2)}, u32[]{:S(2)}) async-start(f32[16,32,256]{2,1,0:T(8,128)} %broadcast_in_dim.13), calls=%async_computation.2 | async-start | bytes 1048576 | tf_op jit(solution)/shard_map/all_to_all | solution.py:37
  77.9 9.5 %all-to-all-done.2 = f32[16,32,256]{2,1,0:T(8,128)S(1)} async-done(((f32[16,32,256]{2,1,0:T(8,128)}), f32[16,32,256]{2,1,0:T(8,128)S(1)}, u32[]{:S(2)}, u32[]{:S(2)}) %all-to-all-start.2) | async-done | bytes 524320 | tf_op jit(solution)/shard_map/all_to_all | solution.py:37
  87.4 1.0 convolution_bitcast_fusion
  88.4 0.0 copy-start.1
  88.5 1.1 copy-done.1
  89.6 5.1 %shard_map.69 = (f32[8,104,256]{2,1,0:T(8,128)}, f32[8,104,256]{2,1,0:T(8,128)}) custom-call(s32[2]{0:T(128)S(1)} %pad_add_fusion.pos, f32[8,176,128]{2,1,0:T(8,128)S(1)} %get-tuple-element.11.s0, f32[8,176,128]{2,1,0:T(8,128)S(1)} %collective-permute-done.s1, f32[8,176,128]{2,1,0:T(8,128)S(1)} %collective-permute-done.1.s2, f32[8,176,128]{2,1,0:T(8,128)S(1)} %copy-done.1, ...), custom_call_target="tpu_custom_call" | custom-call | flops 1107296256 | bytes 4325376 | tf_op jit(solution)/shard_map/pallas_call | solution.py:165
  94.6 3.0 %collective-permute-start.4 = (f32[8,104,256]{2,1,0:T(8,128)}, f32[8,104,256]{2,1,0:T(8,128)S(1)}, u32[]{:S(2)}, u32[]{:S(2)}) collective-permute-start(f32[8,104,256]{2,1,0:T(8,128)} %get-tuple-element.16), channel_id=1, source_target_pairs={{0,4},{4,0},{1,5},{5,1},{2,6},{6,2},{3,7},{7,3},{8,12},{12,8},{9,1... | collective-permute-start | bytes 2555912 | tf_op jit(solution)/shard_map/ppermute | solution.py:45
  97.6 2.2 collective-permute-done.4
  99.8 1.3 add.38
  101.2 30.5 %all_to_all.31 = f32[8,104,256]{2,1,0:T(8,128)S(1)} all-to-all(f32[8,104,256]{2,1,0:T(8,128)S(1)} %add.38), channel_id=1, replica_groups=mesh['z'=8,'y'=4,'c'=2,'x'=4] {'z'}, dimensions={0} | all-to-all | bytes 1703936 | tf_op jit(solution)/shard_map/all_to_all | solution.py:41
  131.6 0.1 reduce_sum.37
  131.7 0.6 collective-permute-start.6
  132.3 0.6 collective-permute-start.5
  132.9 2.1 collective-permute-start.7
  135.0 0.9 broadcast_in_dim.14
  135.9 3.5 %all-to-all-start.4 = ((f32[8,88,256]{2,1,0:T(8,128)}), f32[8,88,256]{2,1,0:T(8,128)S(1)}, u32[]{:S(2)}, u32[]{:S(2)}) async-start(f32[8,88,256]{2,1,0:T(8,128)} %broadcast_in_dim.14), calls=%async_computation.4 | async-start | bytes 1441792 | tf_op jit(solution)/shard_map/all_to_all | solution.py:37
  139.5 1.3 collective-permute-start.9
  140.8 0.4 collective-permute-start.8
  141.1 2.3 collective-permute-start.10
  143.4 1.6 collective-permute-done.8
  145.1 0.2 collective-permute-done.10
  145.5 0.1 pad_maximum_fusion
  145.7 13.6 %all-to-all-done.4.refs_0_ = f32[8,88,256]{2,1,0:T(8,128)S(1)} async-done(((f32[8,88,256]{2,1,0:T(8,128)}), f32[8,88,256]{2,1,0:T(8,128)S(1)}, u32[]{:S(2)}, u32[]{:S(2)}) %all-to-all-start.4) | async-done | bytes 720928 | tf_op jit(solution)/shard_map/all_to_all | solution.py:37
  159.3 0.1 collective-permute-start.13
  159.4 1.3 collective-permute-start.12
  160.7 35.9 %shard_map.70 = f32[256,256]{1,0:T(8,128)S(1)} custom-call(f32[256,256]{1,0:T(8,128)S(1)} %bitcast.53), custom_call_target="tpu_custom_call" | custom-call | flops 10000000000 | bytes 1000000 | tf_op jit(solution)/shard_map/pallas_call | solution.py:225
  196.7 0.5 fusion
  197.2 3.4 %collective-permute-start.11 = (f32[1,256]{1,0:T(1,128)S(1)}, f32[1,256]{1,0:T(1,128)S(1)}, u32[]{:S(2)}, u32[]{:S(2)}) collective-permute-start(f32[1,256]{1,0:T(1,128)S(1)} %bitcast.63), channel_id=1, source_target_pairs={{0,4},{4,0},{1,5},{5,1},{2,6},{6,2},{3,7},{7,3},{8,12},{12,8},{9,1... | collective-permute-start | bytes 3080 | tf_op jit(solution)/shard_map/ppermute | solution.py:45
  200.6 0.8 collective-permute-done.11
  201.4 0.6 broadcast_in_dim.34
  202.0 3.8 %all-to-all-start.5 = ((f32[16,1,256]{2,1,0:T(1,128)}), f32[16,1,256]{2,1,0:T(1,128)S(1)}, u32[]{:S(2)}, u32[]{:S(2)}) async-start(f32[16,1,256]{2,1,0:T(1,128)} %broadcast_in_dim.34), calls=%async_computation.5 | async-start | bytes 32768 | tf_op jit(solution)/shard_map/all_to_all | solution.py:37
  205.8 0.7 collective-permute-start.16
  206.5 5.7 %all-to-all-done.5 = f32[16,1,256]{2,1,0:T(1,128)S(1)} async-done(((f32[16,1,256]{2,1,0:T(1,128)}), f32[16,1,256]{2,1,0:T(1,128)S(1)}, u32[]{:S(2)}, u32[]{:S(2)}) %all-to-all-start.5) | async-done | bytes 16416 | tf_op jit(solution)/shard_map/all_to_all | solution.py:37
  212.4 1.0 collective-permute-start.15
  213.3 0.7 collective-permute-start.14
  214.0 2.3 collective-permute-start.18
  216.3 0.0 collective-permute-start.17
  216.3 0.4 broadcast_multiply_fusion
  216.7 3.8 %collective-permute-done.15.refs_4_ = f32[4,88,256]{2,1,0:T(8,128)S(1)} collective-permute-done((f32[4,88,256]{2,1,0:T(8,128)S(1)}, f32[4,88,256]{2,1,0:T(8,128)S(1)}, u32[]{:S(2)}, u32[]{:S(2)}) %collective-permute-start.15) | collective-permute-done | bytes 360480 | tf_op jit(solution)/shard_map/ppermute | solution.py:49
  220.6 2.7 %collective-permute-start.20 = (f32[4,88,256]{2,1,0:T(8,128)S(1)}, f32[4,88,256]{2,1,0:T(8,128)S(1)}, u32[]{:S(2)}, u32[]{:S(2)}) collective-permute-start(f32[4,88,256]{2,1,0:T(8,128)S(1)} %collective-permute-done.15.refs_4_), channel_id=1, source_target_pairs={{0,4},{4,0},{1,5},{5,1},{2,6},{6,2},{3,7},{7,3},{8,12},{12,8},{9,1... | collective-permute-start | bytes 1081352 | tf_op jit(solution)/shard_map/ppermute | solution.py:45
  223.3 2.2 collective-permute-start.19
  225.5 0.9 convolution_multiply_fusion.1
  226.4 0.4 fusion.1.left
  226.8 0.8 copy-done.3
  227.7 0.9 copy-done.4
  228.6 8.2 %shard_map.71 = (f32[128,5632]{1,0:T(8,128)}, f32[128,5632]{1,0:T(8,128)}) custom-call(s32[2]{0:T(128)S(1)} %pad_add_fusion.pos, f32[256,256]{1,0:T(8,128)S(1)} %fusion.1.left, bf16[128,5632]{1,0:T(8,128)(2,1)} %grad.3, f32[128,5632]{1,0:T(8,128)} %mom.3, f32[128,5632]{1,0:T(8,128)} %wgt.1, f32[8,88,256]{2,1,0:T(8,128)S(1)} %all-to-all-done.4.refs_0_, ...), custom_call_target="tpu_custom_call" | custom-call | flops 2214592512 | bytes 12976128 | tf_op jit(solution)/shard_map/pallas_call | solution.py:280
  (39 shorter events, 0.4 us)
Async XLA Ops:
  2.5 31.3 %all-to-all-start = ((f32[8,88,256]{2,1,0:T(8,128)}), f32[8,88,256]{2,1,0:T(8,128)}, u32[]{:S(2)}, u32[]{:S(2)}) async-start(f32[8,88,256]{2,1,0:T(8,128)} %broadcast_in_dim.12), calls=%async_computation | async-start | bytes 1441792 | tf_op jit(solution)/shard_map/all_to_all | solution.py:37
  16.4 18.3 %collective-permute-start = (f32[8,176,128]{2,1,0:T(8,128)}, f32[8,176,128]{2,1,0:T(8,128)S(1)}, u32[]{:S(2)}, u32[]{:S(2)}) collective-permute-start(f32[8,176,128]{2,1,0:T(8,128)} %get-tuple-element.12), channel_id=1, source_target_pairs={{0,8},{8,16},{16,24},{24,0},{1,9},{9,17},{17,25},{25,1},{2,10},{10... | collective-permute-start | bytes 2162696 | tf_op jit(solution)/shard_map/ppermute | solution.py:49
  17.7 33.5 %collective-permute-start.1 = (f32[8,176,128]{2,1,0:T(8,128)}, f32[8,176,128]{2,1,0:T(8,128)S(1)}, u32[]{:S(2)}, u32[]{:S(2)}) collective-permute-start(f32[8,176,128]{2,1,0:T(8,128)} %get-tuple-element.13), channel_id=1, source_target_pairs={{0,16},{8,24},{16,0},{24,8},{1,17},{9,25},{17,1},{25,9},{2,18},{10... | collective-permute-start | bytes 2162696 | tf_op jit(solution)/shard_map/ppermute | solution.py:49
  20.3 30.9 %collective-permute-start.2 = (f32[8,176,128]{2,1,0:T(8,128)}, f32[8,176,128]{2,1,0:T(8,128)S(1)}, u32[]{:S(2)}, u32[]{:S(2)}) collective-permute-start(f32[8,176,128]{2,1,0:T(8,128)} %get-tuple-element.14), channel_id=1, source_target_pairs={{0,24},{8,0},{16,8},{24,16},{1,25},{9,1},{17,9},{25,17},{2,26},{10... | collective-permute-start | bytes 2162696 | tf_op jit(solution)/shard_map/ppermute | solution.py:49
  33.7 17.5 %collective-permute-start.3 = (f32[8,88,256]{2,1,0:T(8,128)}, f32[8,88,256]{2,1,0:T(8,128)S(1)}, u32[]{:S(2)}, u32[]{:S(2)}) collective-permute-start(f32[8,88,256]{2,1,0:T(8,128)} %all-to-all-done.mine), channel_id=1, source_target_pairs={{0,4},{4,0},{1,5},{5,1},{2,6},{6,2},{3,7},{7,3},{8,12},{12,8},{9,1... | collective-permute-start | bytes 2162696 | tf_op jit(solution)/shard_map/ppermute | solution.py:45
  51.2 21.2 %copy-start = (f32[8,176,128]{2,1,0:T(8,128)}, f32[8,176,128]{2,1,0:T(8,128)S(1)}, u32[]{:S(2)}) copy-start(f32[8,176,128]{2,1,0:T(8,128)S(1)} %collective-permute-done.2.s3) | copy-start | bytes 2162692
  51.2 0.9 copy-start.2
  74.3 13.1 %all-to-all-start.2 = ((f32[16,32,256]{2,1,0:T(8,128)}), f32[16,32,256]{2,1,0:T(8,128)S(1)}, u32[]{:S(2)}, u32[]{:S(2)}) async-start(f32[16,32,256]{2,1,0:T(8,128)} %broadcast_in_dim.13), calls=%async_computation.2 | async-start | bytes 1048576 | tf_op jit(solution)/shard_map/all_to_all | solution.py:37
  88.4 1.1 copy-start.1
  94.6 5.2 %collective-permute-start.4 = (f32[8,104,256]{2,1,0:T(8,128)}, f32[8,104,256]{2,1,0:T(8,128)S(1)}, u32[]{:S(2)}, u32[]{:S(2)}) collective-permute-start(f32[8,104,256]{2,1,0:T(8,128)} %get-tuple-element.16), channel_id=1, source_target_pairs={{0,4},{4,0},{1,5},{5,1},{2,6},{6,2},{3,7},{7,3},{8,12},{12,8},{9,1... | collective-permute-start | bytes 2555912 | tf_op jit(solution)/shard_map/ppermute | solution.py:45
  131.7 7.8 %collective-permute-start.6 = (f32[16,256]{1,0:T(8,128)S(1)}, f32[16,256]{1,0:T(8,128)S(1)}, u32[]{:S(2)}, u32[]{:S(2)}) collective-permute-start(f32[16,256]{1,0:T(8,128)S(1)} %get-tuple-element.20), channel_id=1, source_target_pairs={{0,16},{8,24},{16,0},{24,8},{1,17},{9,25},{17,1},{25,9},{2,18},{10... | collective-permute-start | bytes 49160 | tf_op jit(solution)/shard_map/ppermute | solution.py:49
  132.3 7.2 %collective-permute-start.5 = (f32[16,256]{1,0:T(8,128)S(1)}, f32[16,256]{1,0:T(8,128)S(1)}, u32[]{:S(2)}, u32[]{:S(2)}) collective-permute-start(f32[16,256]{1,0:T(8,128)S(1)} %get-tuple-element.20), channel_id=1, source_target_pairs={{0,8},{8,16},{16,24},{24,0},{1,9},{9,17},{17,25},{25,1},{2,10},{10... | collective-permute-start | bytes 49160 | tf_op jit(solution)/shard_map/ppermute | solution.py:49
  132.9 6.6 %collective-permute-start.7 = (f32[16,256]{1,0:T(8,128)S(1)}, f32[16,256]{1,0:T(8,128)S(1)}, u32[]{:S(2)}, u32[]{:S(2)}) collective-permute-start(f32[16,256]{1,0:T(8,128)S(1)} %get-tuple-element.20), channel_id=1, source_target_pairs={{0,24},{8,0},{16,8},{24,16},{1,25},{9,1},{17,9},{25,17},{2,26},{10... | collective-permute-start | bytes 49160 | tf_op jit(solution)/shard_map/ppermute | solution.py:49
  135.9 23.4 %all-to-all-start.4 = ((f32[8,88,256]{2,1,0:T(8,128)}), f32[8,88,256]{2,1,0:T(8,128)S(1)}, u32[]{:S(2)}, u32[]{:S(2)}) async-start(f32[8,88,256]{2,1,0:T(8,128)} %broadcast_in_dim.14), calls=%async_computation.4 | async-start | bytes 1441792 | tf_op jit(solution)/shard_map/all_to_all | solution.py:37
  139.5 5.6 %collective-permute-start.9 = (f32[4,16,256]{2,1,0:T(8,128)S(1)}, f32[4,16,256]{2,1,0:T(8,128)S(1)}, u32[]{:S(2)}, u32[]{:S(2)}) collective-permute-start(f32[4,16,256]{2,1,0:T(8,128)S(1)} %pad_maximum_fusion.1), channel_id=1, source_target_pairs={{0,2},{1,3},{2,0},{3,1},{4,6},{5,7},{6,4},{7,5},{8,10},{9,11},{10,... | collective-permute-start | bytes 196616 | tf_op jit(solution)/shard_map/ppermute | solution.py:49
  140.8 4.3 %collective-permute-start.8 = (f32[4,16,256]{2,1,0:T(8,128)S(1)}, f32[4,16,256]{2,1,0:T(8,128)S(1)}, u32[]{:S(2)}, u32[]{:S(2)}) collective-permute-start(f32[4,16,256]{2,1,0:T(8,128)S(1)} %pad_maximum_fusion.1), channel_id=1, source_target_pairs={{0,1},{1,2},{2,3},{3,0},{4,5},{5,6},{6,7},{7,4},{8,9},{9,10},{10,1... | collective-permute-start | bytes 196616 | tf_op jit(solution)/shard_map/ppermute | solution.py:49
  141.1 4.2 %collective-permute-start.10 = (f32[4,16,256]{2,1,0:T(8,128)S(1)}, f32[4,16,256]{2,1,0:T(8,128)S(1)}, u32[]{:S(2)}, u32[]{:S(2)}) collective-permute-start(f32[4,16,256]{2,1,0:T(8,128)S(1)} %pad_maximum_fusion.1), channel_id=1, source_target_pairs={{0,3},{1,0},{2,1},{3,2},{4,7},{5,4},{6,5},{7,6},{8,11},{9,8},{10,9... | collective-permute-start | bytes 196616 | tf_op jit(solution)/shard_map/ppermute | solution.py:49
  159.3 53.0 %collective-permute-start.13 = (f32[8,88,256]{2,1,0:T(8,128)S(1)}, f32[8,88,256]{2,1,0:T(8,128)S(1)}, u32[]{:S(2)}, u32[]{:S(2)}) collective-permute-start(f32[8,88,256]{2,1,0:T(8,128)S(1)} %all-to-all-done.4.refs_0_), channel_id=1, source_target_pairs={{0,24},{8,0},{16,8},{24,16},{1,25},{9,1},{17,9},{25,17},{2,26},{10... | collective-permute-start | bytes 2162696 | tf_op jit(solution)/shard_map/ppermute | solution.py:49
  159.4 53.9 %collective-permute-start.12 = (f32[8,88,256]{2,1,0:T(8,128)S(1)}, f32[8,88,256]{2,1,0:T(8,128)S(1)}, u32[]{:S(2)}, u32[]{:S(2)}) collective-permute-start(f32[8,88,256]{2,1,0:T(8,128)S(1)} %all-to-all-done.4.refs_0_), channel_id=1, source_target_pairs={{0,8},{8,16},{16,24},{24,0},{1,9},{9,17},{17,25},{25,1},{2,10},{10... | collective-permute-start | bytes 2162696 | tf_op jit(solution)/shard_map/ppermute | solution.py:49
  197.2 4.2 %collective-permute-start.11 = (f32[1,256]{1,0:T(1,128)S(1)}, f32[1,256]{1,0:T(1,128)S(1)}, u32[]{:S(2)}, u32[]{:S(2)}) collective-permute-start(f32[1,256]{1,0:T(1,128)S(1)} %bitcast.63), channel_id=1, source_target_pairs={{0,4},{4,0},{1,5},{5,1},{2,6},{6,2},{3,7},{7,3},{8,12},{12,8},{9,1... | collective-permute-start | bytes 3080 | tf_op jit(solution)/shard_map/ppermute | solution.py:45
  202.0 10.2 %all-to-all-start.5 = ((f32[16,1,256]{2,1,0:T(1,128)}), f32[16,1,256]{2,1,0:T(1,128)S(1)}, u32[]{:S(2)}, u32[]{:S(2)}) async-start(f32[16,1,256]{2,1,0:T(1,128)} %broadcast_in_dim.34), calls=%async_computation.5 | async-start | bytes 32768 | tf_op jit(solution)/shard_map/all_to_all | solution.py:37
  205.8 20.9 %collective-permute-start.16 = (f32[8,88,256]{2,1,0:T(8,128)S(1)}, f32[8,88,256]{2,1,0:T(8,128)}, u32[]{:S(2)}, u32[]{:S(2)}) collective-permute-start(f32[8,88,256]{2,1,0:T(8,128)S(1)} %all-to-all-done.4.refs_0_), channel_id=1, source_target_pairs={{0,4},{4,0},{1,5},{5,1},{2,6},{6,2},{3,7},{7,3},{8,12},{12,8},{9,1... | collective-permute-start | bytes 2162696 | tf_op jit(solution)/shard_map/ppermute | solution.py:45
  212.4 8.2 %collective-permute-start.15 = (f32[4,88,256]{2,1,0:T(8,128)S(1)}, f32[4,88,256]{2,1,0:T(8,128)S(1)}, u32[]{:S(2)}, u32[]{:S(2)}) collective-permute-start(f32[4,88,256]{2,1,0:T(8,128)S(1)} %slice.19), channel_id=1, source_target_pairs={{0,24},{8,0},{16,8},{24,16},{1,25},{9,1},{17,9},{25,17},{2,26},{10... | collective-permute-start | bytes 1081352 | tf_op jit(solution)/shard_map/ppermute | solution.py:49
  213.3 9.9 %collective-permute-start.14 = (f32[4,88,256]{2,1,0:T(8,128)S(1)}, f32[4,88,256]{2,1,0:T(8,128)S(1)}, u32[]{:S(2)}, u32[]{:S(2)}) collective-permute-start(f32[4,88,256]{2,1,0:T(8,128)S(1)} %slice.18), channel_id=1, source_target_pairs={{0,8},{8,16},{16,24},{24,0},{1,9},{9,17},{17,25},{25,1},{2,10},{10... | collective-permute-start | bytes 1081352 | tf_op jit(solution)/shard_map/ppermute | solution.py:49
  214.0 12.8 %collective-permute-start.18 = (f32[8,88,256]{2,1,0:T(8,128)S(1)}, f32[8,88,256]{2,1,0:T(8,128)S(1)}, u32[]{:S(2)}, u32[]{:S(2)}) collective-permute-start(f32[8,88,256]{2,1,0:T(8,128)S(1)} %collective-permute-done.13.refs_2_), channel_id=1, source_target_pairs={{0,4},{4,0},{1,5},{5,1},{2,6},{6,2},{3,7},{7,3},{8,12},{12,8},{9,1... | collective-permute-start | bytes 2162696 | tf_op jit(solution)/shard_map/ppermute | solution.py:45
  216.3 10.5 %collective-permute-start.17 = (f32[8,88,256]{2,1,0:T(8,128)S(1)}, f32[8,88,256]{2,1,0:T(8,128)S(1)}, u32[]{:S(2)}, u32[]{:S(2)}) collective-permute-start(f32[8,88,256]{2,1,0:T(8,128)S(1)} %collective-permute-done.12.refs_1_), channel_id=1, source_target_pairs={{0,4},{4,0},{1,5},{5,1},{2,6},{6,2},{3,7},{7,3},{8,12},{12,8},{9,1... | collective-permute-start | bytes 2162696 | tf_op jit(solution)/shard_map/ppermute | solution.py:45
  220.6 6.2 %collective-permute-start.20 = (f32[4,88,256]{2,1,0:T(8,128)S(1)}, f32[4,88,256]{2,1,0:T(8,128)S(1)}, u32[]{:S(2)}, u32[]{:S(2)}) collective-permute-start(f32[4,88,256]{2,1,0:T(8,128)S(1)} %collective-permute-done.15.refs_4_), channel_id=1, source_target_pairs={{0,4},{4,0},{1,5},{5,1},{2,6},{6,2},{3,7},{7,3},{8,12},{12,8},{9,1... | collective-permute-start | bytes 1081352 | tf_op jit(solution)/shard_map/ppermute | solution.py:45
  223.3 3.5 %collective-permute-start.19 = (f32[4,88,256]{2,1,0:T(8,128)S(1)}, f32[4,88,256]{2,1,0:T(8,128)S(1)}, u32[]{:S(2)}, u32[]{:S(2)}) collective-permute-start(f32[4,88,256]{2,1,0:T(8,128)S(1)} %collective-permute-done.14.refs_3_), channel_id=1, source_target_pairs={{0,4},{4,0},{1,5},{5,1},{2,6},{6,2},{3,7},{7,3},{8,12},{12,8},{9,1... | collective-permute-start | bytes 1081352 | tf_op jit(solution)/shard_map/ppermute | solution.py:45
  226.8 0.9 copy-start.3
  227.7 0.9 copy-start.4
where the time goes:
time: 237 us
  waiting for transfers between devices  67 us (28%)
  Pallas kernels  56.9 us (24%)
  starting transfers between devices  50 us (21%)
  blocking collectives  47.8 us (20%)
  local copies, waits for them, and re-layouts  8.17 us (3%)
  matrix products  3.26 us (1%)
  other arithmetic  2.64 us (1%)
    all_to_all x2, blocking collectives, scatter_sum(): return jnp.sum(lax.all_to_all(blocks, axes, 0, 0), axis=0)  47.8 us
    all_to_all x4, waiting for transfers between devices, gather(): return lax.all_to_all(copies, axes, 0, 0)  41.2 us
    pallas_call x1, Pallas kernels, factor_inverse(): pl.pallas_call(inverse_kernel, in_specs=[pl.BlockSpec(memory_space=pltpu....  35.9 us
    ppermute x13, waiting for transfers between devices, shift(): lax.ppermute(block, axis, [(i, (i + step) % size) for i in range(size)])  22.7 us
    all_to_all x4, starting transfers between devices, gather(): return lax.all_to_all(copies, axes, 0, 0)  19.9 us
    ppermute x13, starting transfers between devices, shift(): lax.ppermute(block, axis, [(i, (i + step) % size) for i in range(size)])  15.3 us
    ppermute x8, starting transfers between devices, swap(): return lax.ppermute(block, 'c', [(0, 1), (1, 0)])  14.8 us
    pallas_call x1, Pallas kernels, update(): pl.pallas_call(update_kernel, grid=(NZ // 2,), in_specs=[smem(), whole, b...  8.17 us
  transfers between devices with their start and end apart: 25, of which 11 were waited for; matrix products, arithmetic and copies ran while one was open for 2% of the time, Pallas kernels for 17%

commit v1 on v0

--- a/solution.py
+++ b/solution.py
@@ -1,3 +1,4 @@
+import functools
 import math
 
 import jax
@@ -18,7 +19,7 @@
 step_rate = 0.1
 weight_decay = 0.1
 
-VMEM_BYTES = 50 * 1024 * 1024
+MIB = 1024 * 1024
 HIGHEST = lax.Precision.HIGHEST
 
 
@@ -68,8 +69,8 @@
     return one(lh, rh) + (one(lh, rl) + one(ll, rh))
 
 
-def params():
-    return pltpu.CompilerParams(vmem_limit_bytes=VMEM_BYTES)
+def params(mib):
+    return pltpu.CompilerParams(vmem_limit_bytes=mib * MIB)
 
 
 def cost(flops, size):
@@ -104,13 +105,15 @@
         out_specs=[piece] * NY,
         out_shape=[jax.ShapeDtypeStruct((NZ, size, rows), jnp.float32)] * NY,
         scratch_shapes=[pltpu.VMEM((wide, rows), jnp.float32)],
-        compiler_params=params(),
+        compiler_params=params(16),
         cost_estimate=cost(0, rows * cols * 10),
     )(pos, gradient, momentum)
 
 
-def project_kernel(pos, s0, s1, s2, s3, mine, other, out, full):
-    y, core = pos[0], pos[1]
+def project_kernel(count, pos, *refs):
+    core = pos[1]
+    mine, other = refs[count : count + 2]
+    full = refs[-1]
     half = mine.shape[1]
     for z in range(NZ):
         start = pl.multiple_of(z * 2 * half + core * half, 8)
@@ -118,67 +121,75 @@
         start = pl.multiple_of(z * 2 * half + (1 - core) * half, 8)
         full[pl.ds(start, half), :] = other[z]
     right = halves(full[...])
-    for d, strip in enumerate((s0, s1, s2, s3)):
-        left = halves(strip[...])
-        out[lax.rem(y + NY - d, NY)] = dot_halves(left, right, 0, 0)
+    for strip, out in zip(refs[:count], refs[count + 2 : -1]):
+        out[...] = dot_halves(halves(strip[...]), right, 0, 0)
 
 
 def project(pos, strips, mine, other):
     cols, rows = strips[0].shape
+    count = len(strips)
     return pl.pallas_call(
-        project_kernel,
-        in_specs=[smem()] + [pl.BlockSpec(memory_space=pltpu.VMEM)] * 6,
-        out_specs=pl.BlockSpec(memory_space=pltpu.VMEM),
-        out_shape=jax.ShapeDtypeStruct((NY, rows, RANK), jnp.float32),
+        functools.partial(project_kernel, count),
+        in_specs=[smem()] + [pl.BlockSpec(memory_space=pltpu.VMEM)] * (count + 2),
+        out_specs=[pl.BlockSpec(memory_space=pltpu.VMEM)] * count,
+        out_shape=[jax.ShapeDtypeStruct((rows, RANK), jnp.float32)] * count,
         scratch_shapes=[pltpu.VMEM((cols, RANK), jnp.float32)],
-        compiler_params=params(),
-        cost_estimate=cost(6 * NY * rows * cols * RANK, NY * rows * cols * 8),
+        compiler_params=params(24),
+        cost_estimate=cost(6 * count * rows * cols * RANK, count * rows * cols * 8),
     )(pos, *strips, mine, other)
 
 
-def feedback_kernel(pos, s0, s1, s2, s3, proj, gram, mine, other, low, high, full):
-    y, core = pos[0], pos[1]
+def feedback_kernel(pos, s0, s1, s2, s3, p0, p1, p2, p3, mine, other, low, high, full, gram):
+    core = pos[1]
     rows = s0.shape[2]
-    half = mine.shape[1] - gram.shape[0]
+    steps, size = s0.shape[:2]
+    half = size // 2
+    part = mine.shape[1] - half
 
     @pl.when(pl.program_id(0) == 0)
     def _():
-        for d in range(NY):
-            top, rest = halves(proj[lax.rem(y + NY - d, NY)])
-            high[d * rows : (d + 1) * rows] = top
-            low[d * rows : (d + 1) * rows] = rest
-
-    strip = jnp.concatenate([s0[0], s1[0], s2[0], s3[0]], axis=1)
-    full[...] = dot_halves(halves(strip), (high[...], low[...]), 1, 0)
-    mine[0, :half] = full[pl.ds(pl.multiple_of(core * half, 8), half), :]
-    other[0, :half] = full[pl.ds(pl.multiple_of((1 - core) * half, 8), half), :]
-    mine[0, half:] = gram[...]
-    other[0, half:] = gram[...]
-
-
-def raw_feedback(pos, strips, proj, gram):
+        proj = jnp.concatenate([p0[...], p1[...], p2[...], p3[...]], axis=0)
+        high[...], low[...] = halves(proj)
+        gram[...] = dot(proj, proj, 0, 0, HIGHEST)
+
+    mine_at = pl.multiple_of(core * half, 8)
+    other_at = pl.multiple_of((1 - core) * half, 8)
+    gram_rows = gram[pl.ds(pl.multiple_of(pos[2] * part, 8), part), :]
+    for z in range(steps):
+        strip = jnp.concatenate([s0[z], s1[z], s2[z], s3[z]], axis=1)
+        full[...] = dot_halves(halves(strip), (high[...], low[...]), 1, 0)
+        mine[z, :half] = full[pl.ds(mine_at, half), :]
+        other[z, :half] = full[pl.ds(other_at, half), :]
+        mine[z, half:] = gram_rows
+        other[z, half:] = gram_rows
+
+
+def raw_feedback(pos, strips, projs):
     _, size, rows = strips[0].shape
-    part = gram.shape[0]
-    strip = pl.BlockSpec((1, size, rows), lambda z: (z, 0, 0))
-    whole = lambda shape: pl.BlockSpec(shape, lambda z: (0,) * len(shape))
-    out = pl.BlockSpec((1, size // 2 + part, RANK), lambda z: (z, 0, 0))
+    part = RANK // (NY * NX)
+    steps = 2
+    strip = pl.BlockSpec((steps, size, rows), lambda z: (z, 0, 0))
+    proj = pl.BlockSpec((rows, RANK), lambda z: (0, 0))
+    out = pl.BlockSpec((steps, size // 2 + part, RANK), lambda z: (z, 0, 0))
     return pl.pallas_call(
         feedback_kernel,
-        grid=(NZ,),
-        in_specs=[smem()] + [strip] * NY + [whole(proj.shape), whole(gram.shape)],
+        grid=(NZ // steps,),
+        in_specs=[smem()] + [strip] * NY + [proj] * NY,
         out_specs=[out] * 2,
         out_shape=[jax.ShapeDtypeStruct((NZ, size // 2 + part, RANK), jnp.float32)] * 2,
         scratch_shapes=[
             pltpu.VMEM((NY * rows, RANK), jnp.bfloat16),
             pltpu.VMEM((NY * rows, RANK), jnp.bfloat16),
             pltpu.VMEM((size, RANK), jnp.float32),
+            pltpu.VMEM((RANK, RANK), jnp.float32),
         ],
-        compiler_params=params(),
+        compiler_params=params(24),
         cost_estimate=cost(6 * NY * rows * NZ * size * RANK, NZ * size * rows * 24),
-    )(pos, *strips, proj, gram)
+    )(pos, *strips, *projs)
 
 
 BLOCK = 64
+GROUP = 8
 
 
 def small_inverse(block):
@@ -186,20 +197,52 @@
     cols = lax.broadcasted_iota(jnp.int32, (BLOCK, BLOCK), 1)
     unit = (rows == cols).astype(jnp.float32)
     wide = jnp.concatenate([block, unit], axis=1)
+    full = (8, 2 * BLOCK)
     tiles = [wide[8 * t : 8 * t + 8] for t in range(BLOCK // 8)]
-    place = lax.broadcasted_iota(jnp.int32, (8, 2 * BLOCK), 0)
-    scale = [jnp.zeros((8, 2 * BLOCK), jnp.float32) for _ in tiles]
-    for j in range(BLOCK):
+    place = lax.broadcasted_iota(jnp.int32, full, 0)
+    scale = [jnp.zeros(full, jnp.float32) for _ in tiles]
+    for j in range(0, BLOCK, GROUP):
         tile, row = divmod(j, 8)
-        line = jnp.broadcast_to(tiles[tile][row : row + 1], (8, 2 * BLOCK))
-        pivot = jnp.broadcast_to(line[:, j : j + 1], (8, 2 * BLOCK))
-        line = line * (1.0 / pivot)
-        scale[tile] = jnp.where(place == row, pivot, scale[tile])
-        for t in range(tile, BLOCK // 8):
-            factor = jnp.broadcast_to(tiles[t][:, j : j + 1], (8, 2 * BLOCK))
+        cols = {
+            t: [jnp.broadcast_to(tiles[t][:, j + k : j + k + 1], full) for k in range(GROUP)]
+            for t in range(tile, BLOCK // 8)
+        }
+        lines = [
+            jnp.broadcast_to(tiles[tile][row + k : row + k + 1], full) for k in range(GROUP)
+        ]
+        heads = [
+            [
+                jnp.broadcast_to(cols[tile][m][row + k : row + k + 1], full)
+                for m in range(k + 1)
+            ]
+            for k in range(GROUP)
+        ]
+        pivots = []
+        for m in range(GROUP):
+            pivot = heads[m][m]
+            inverse = 1.0 / pivot
+            pivots.append((pivot, inverse))
+            for k in range(m + 1, GROUP):
+                ratio = heads[k][m] * inverse
+                lines[k] = lines[k] - ratio * lines[m]
+                for n in range(m + 1, k + 1):
+                    heads[k][n] = heads[k][n] - ratio * heads[n][m]
+                for t in cols:
+                    cols[t][k] = cols[t][k] - ratio * cols[t][m]
+        scaled = [line * inverse for line, (_, inverse) in zip(lines, pivots)]
+        for t in cols:
+            change = cols[t][0] * scaled[0]
+            for k in range(1, GROUP):
+                change = change + cols[t][k] * scaled[k]
             if t == tile:
-                factor = jnp.where(place > row, factor, 0.0)
-            tiles[t] = tiles[t] - factor * line
+                change = jnp.where(place >= row + GROUP, change, 0.0)
+                kept = tiles[t] - change
+                for k in range(GROUP):
+                    kept = jnp.where(place == row + k, lines[k], kept)
+                    scale[t] = jnp.where(place == row + k, pivots[k][0], scale[t])
+                tiles[t] = kept
+            else:
+                tiles[t] = tiles[t] - change
     tiles = [t * (1.0 / jnp.sqrt(s)) for t, s in zip(tiles, scale)]
     return jnp.concatenate(tiles, axis=0)[:, BLOCK:]
 
@@ -228,7 +271,7 @@
         out_specs=pl.BlockSpec(memory_space=pltpu.VMEM),
         out_shape=jax.ShapeDtypeStruct((RANK, RANK), jnp.float32),
         scratch_shapes=[pltpu.VMEM((RANK, RANK), jnp.float32)] * 2,
-        compiler_params=params(),
+        compiler_params=params(16),
         cost_estimate=cost(10_000_000_000, 1_000_000),
     )(gram)
 
@@ -284,46 +327,42 @@
         out_specs=[block, block],
         out_shape=[jax.ShapeDtypeStruct(momentum.shape, jnp.float32)] * 2,
         scratch_shapes=[pltpu.VMEM((wide, RANK), jnp.float32)],
-        compiler_params=params(),
+        compiler_params=params(28),
         cost_estimate=cost(12 * rows * cols * RANK, rows * cols * 18),
     )(pos, left, gradient, momentum, weight, *mine, *other)
 
 
 def body(gradient, momentum, weight, basis):
     core, y, x = lax.axis_index("c"), lax.axis_index("y"), lax.axis_index("x")
-    pos = jnp.stack([y, core]).astype(jnp.int32)
+    pos = jnp.stack([y, core, y * NX + x]).astype(jnp.int32)
     rows, cols = momentum.shape
     shard = basis.shape[0]
 
+    sent = split_columns(pos, gradient, momentum)
+    sent, basis = lax.optimization_barrier((sent, basis))
+    strips = [sent[0], None, None, None]
+    for d in (2, 1, 3):
+        strips[d] = shift(sent[d], "y", NY, d)
+    flat = [strip.reshape(NZ * NC * shard, rows) for strip in strips]
+
     basis_z = gather(basis, "z", NZ)
-
-    sent = split_columns(pos, gradient, momentum)
-    strips = [sent[0]] + [shift(sent[d], "y", NY, d) for d in range(1, NY)]
-    flat = [strip.reshape(NZ * NC * shard, rows) for strip in strips]
-
-    partial_proj = project(pos, flat, basis_z, swap(basis_z))
-    few = rows // NX
-    few_rows = scatter_sum(partial_proj.reshape(NY * NX, few, RANK), ("y", "x"))
-    group_proj = gather(few_rows, ("y", "x"), NY * NX).reshape(NY, rows, RANK)
-    projected = lax.dynamic_index_in_dim(group_proj, y, 0, keepdims=False)
-
-    part = RANK // (NY * NX)
-    all_rows = group_proj.reshape(NY * rows, RANK)
-    gram_group = dot(all_rows, all_rows, 0, 0, HIGHEST)
-    gram_part = lax.dynamic_slice_in_dim(gram_group, (y * NX + x) * part, part, 0)
-
-    mine, other = raw_feedback(pos, strips, group_proj, gram_part)
+    basis_other = swap(basis_z)
+    near, first, third = project(pos, [flat[0], flat[1], flat[3]], basis_z, basis_other)
+    (second,) = project(pos, [flat[2]], basis_z, basis_other)
+    projected = (
+        near
+        + shift(first, "y", NY, NY - 1)
+        + shift(third, "y", NY, 1)
+        + shift(second, "y", NY, 2)
+    )
+    projected = projected + sum(shift(projected, "x", NX, d) for d in range(1, NX))
+    projs = [projected] + [shift(projected, "y", NY, d) for d in range(1, NY)]
+
+    mine, other = raw_feedback(pos, strips, projs)
     reduced = scatter_sum(mine + swap(other), "z")
     raw_shard, gram_part = reduced[:shard], reduced[shard:]
 
     raw = gather(raw_shard, "z", NZ)
-    ahead = shift(raw, "y", NY, 1)
-    behind = shift(raw, "y", NY, NY - 1)
-    ahead2 = shift(ahead[: NZ // 2], "y", NY, 1)
-    behind2 = shift(behind[NZ // 2 :], "y", NY, NY - 1)
-    own = [raw, ahead, behind, ahead2, behind2]
-    paired = [swap(block) for block in own]
-
     by_y = jnp.stack([gram_part] + [shift(gram_part, "y", NY, d) for d in range(1, NY)])
     by_x = jnp.stack([by_y] + [shift(by_y, "x", NX, d) for d in range(1, NX)])
     by_x = jnp.flip(jnp.concatenate([by_x, by_x], 0), 0)
@@ -332,6 +371,14 @@
     by_y = lax.dynamic_slice_in_dim(by_y, NY - 1 - y, NY, 1)
     gram_matrix = jnp.swapaxes(by_y, 0, 1).reshape(RANK, RANK)
     inverse = factor_inverse(gram_matrix)
+
+    raw, inverse = lax.optimization_barrier((raw, inverse))
+    ahead = shift(raw, "y", NY, 1)
+    behind = shift(raw, "y", NY, NY - 1)
+    ahead2 = shift(ahead[: NZ // 2], "y", NY, 1)
+    behind2 = shift(behind[NZ // 2 :], "y", NY, NY - 1)
+    own = [raw, ahead, behind, ahead2, behind2]
+    paired = [swap(block) for block in own]
 
     orthonormal = dot(projected, inverse, 1, 1, HIGHEST)
     strip_feedback = dot(raw.reshape(NZ * shard, RANK), inverse, 1, 1)

time: 237 us -> 200 us (0.84)
  Pallas kernels: 56.9 us -> 26.9 us
  blocking collectives: 47.8 us -> 27.4 us
  starting transfers between devices: 50 us -> 59.2 us
  local copies, waits for them, and re-layouts: 8.17 us -> 11.5 us
  waiting for transfers between devices: 67 us -> 69.6 us
    pallas_call x1, Pallas kernels: 35.9 us -> 10.4 us  [factor_inverse(): pl.pallas_call(inverse_kernel, in_specs=[pl.BlockSpec(memory_space=pltpu....]
    all_to_all x2 -> x1, blocking collectives: 47.8 us -> 27.4 us  [scatter_sum(): return jnp.sum(lax.all_to_all(blocks, axes, 0, 0), axis=0)]
    ppermute x13 -> x22, starting transfers between devices: 15.3 us -> 27.5 us  [shift(): lax.ppermute(block, axis, [(i, (i + step) % size) for i in range(size)])]
    ppermute x13 -> x22, waiting for transfers between devices: 22.7 us -> 32.2 us  [shift(): lax.ppermute(block, axis, [(i, (i + step) % size) for i in range(size)])]
    all_to_all x4 -> x3, waiting for transfers between devices: 41.2 us -> 34.5 us  [gather(): return lax.all_to_all(copies, axes, 0, 0)]
    all_to_all x4 -> x3, starting transfers between devices: 19.9 us -> 16.7 us  [gather(): return lax.all_to_all(copies, axes, 0, 0)]
    unnamed x15 -> x21, local copies, waits for them, and re-layouts: 3.76 us -> 6.75 us
    pallas_call x2 -> x3, Pallas kernels: 7.95 us -> 6.35 us  [the longest x1 3.36 us: raw_feedback(): pl.pallas_call(feedback_kernel, grid=(NZ // steps,), in_specs=[smem()] +...]
  transfers between devices with their start and end apart: 25 -> 33, of which waited for: 11 -> 16; matrix products, arithmetic and copies ran while one was open for 2% -> 4% of each run, Pallas kernels for 17% -> 7%
where the time goes in v1:
time: 200 us; the launch traced here: 199 us
  waiting for transfers between devices  69.6 us (35%)
  starting transfers between devices  59.2 us (30%)
  blocking collectives  27.4 us (14%)
  Pallas kernels  26.9 us (13%)
  local copies, waits for them, and re-layouts  11.5 us (6%)
  matrix products  3.35 us (2%)
    all_to_all x3, waiting for transfers between devices, gather(): return lax.all_to_all(copies, axes, 0, 0)  34.5 us
    ppermute x22, waiting for transfers between devices, shift(): lax.ppermute(block, axis, [(i, (i + step) % size) for i in range(size)])  32.2 us
    ppermute x22, starting transfers between devices, shift(): lax.ppermute(block, axis, [(i, (i + step) % size) for i in range(size)])  27.5 us
    all_to_all x1, blocking collectives, scatter_sum(): return jnp.sum(lax.all_to_all(blocks, axes, 0, 0), axis=0)  27.4 us
    all_to_all x3, starting transfers between devices, gather(): return lax.all_to_all(copies, axes, 0, 0)  16.7 us
    ppermute x8, starting transfers between devices, swap(): return lax.ppermute(block, 'c', [(0, 1), (1, 0)])  15 us
    pallas_call x1, Pallas kernels, factor_inverse(): pl.pallas_call(inverse_kernel, in_specs=[pl.BlockSpec(memory_space=pltpu....  10.4 us
    pallas_call x1, Pallas kernels, update(): pl.pallas_call(update_kernel, grid=(NZ // 2,), in_specs=[smem(), whole, b...  7.12 us
  transfers between devices with their start and end apart: 33, of which 16 were waited for; matrix products, arithmetic and copies ran while one was open for 4% of the time, Pallas kernels for 7%

profile of v1, /device:TPU:1, one launch (start us, length us, event | category | flops | bytes accessed | tf_op | source)
XLA Modules:
  0.0 199.4 jit_solution(8296673708791711332)
XLA Ops:
  0.7 1.8 copy-done
  2.5 1.4 copy-done.2
  3.9 3.1 %shard_map.67 = (f32[8,176,128]{2,1,0:T(8,128)S(1)}, f32[8,176,128]{2,1,0:T(8,128)}, f32[8,176,128]{2,1,0:T(8,128)S(1)}, f32[8,176,128]{2,1,0:T(8,128)S(1)}) custom-call(s32[3]{0:T(128)S(1)} %pad_add_fusion.pos, bf16[128,5632]{1,0:T(8,128)(2,1)S(1)} %copy-done.2, f32[128,5632]{1,0:T(8,128)S(1)} %copy-done), custom_call_target="tpu_custom_call" | custom-call | bytes 7208960 | tf_op jit(solution)/shard_map/pallas_call | solution.py:101
  7.0 0.9 copy-done.5
  7.9 0.9 copy-done.6
  8.7 0.9 broadcast_in_dim.10
  9.7 9.0 %all-to-all-start = ((f32[8,88,256]{2,1,0:T(8,128)}), f32[8,88,256]{2,1,0:T(8,128)S(1)}, u32[]{:S(2)}, u32[]{:S(2)}) async-start(f32[8,88,256]{2,1,0:T(8,128)} %broadcast_in_dim.10), calls=%async_computation | async-start | bytes 1441792 | tf_op jit(solution)/shard_map/all_to_all | solution.py:38
  18.7 1.3 collective-permute-start
  20.0 1.5 collective-permute-start.1
  21.5 19.3 %all-to-all-done.refs_3_.refs_1_ = f32[8,88,256]{2,1,0:T(8,128)S(1)} async-done(((f32[8,88,256]{2,1,0:T(8,128)}), f32[8,88,256]{2,1,0:T(8,128)S(1)}, u32[]{:S(2)}, u32[]{:S(2)}) %all-to-all-start) | async-done | bytes 720928 | tf_op jit(solution)/shard_map/all_to_all | solution.py:38
  40.9 0.5 collective-permute-start.2
  41.4 2.9 %collective-permute-start.5 = (f32[8,176,128]{2,1,0:T(8,128)}, f32[8,176,128]{2,1,0:T(8,128)S(1)}, u32[]{:S(2)}, u32[]{:S(2)}) collective-permute-start(f32[8,176,128]{2,1,0:T(8,128)} %copy-done.5), channel_id=1, source_target_pairs={{0,16},{8,24},{16,0},{24,8},{1,17},{9,25},{17,1},{25,9},{2,18},{10... | collective-permute-start | bytes 2162696 | tf_op jit(solution)/shard_map/ppermute | solution.py:50
  44.3 1.8 shard_map.68
  46.1 1.7 collective-permute-start.3
  47.9 13.0 %collective-permute-done.5.s2 = f32[8,176,128]{2,1,0:T(8,128)S(1)} collective-permute-done((f32[8,176,128]{2,1,0:T(8,128)}, f32[8,176,128]{2,1,0:T(8,128)S(1)}, u32[]{:S(2)}, u32[]{:S(2)}) %collective-permute-start.5) | collective-permute-done | bytes 720928 | tf_op jit(solution)/shard_map/ppermute | solution.py:50
  60.9 1.2 shard_map.69
  62.0 3.0 %collective-permute-start.6 = (f32[128,256]{1,0:T(8,128)S(1)}, f32[128,256]{1,0:T(8,128)S(1)}, u32[]{:S(2)}, u32[]{:S(2)}) collective-permute-start(f32[128,256]{1,0:T(8,128)S(1)} %shard_map.69), channel_id=1, source_target_pairs={{0,16},{8,24},{16,0},{24,8},{1,17},{9,25},{17,1},{25,9},{2,18},{10... | collective-permute-start | bytes 393224 | tf_op jit(solution)/shard_map/ppermute | solution.py:50
  65.1 2.4 %collective-permute-done.6 = f32[128,256]{1,0:T(8,128)S(1)} collective-permute-done((f32[128,256]{1,0:T(8,128)S(1)}, f32[128,256]{1,0:T(8,128)S(1)}, u32[]{:S(2)}, u32[]{:S(2)}) %collective-permute-start.6) | collective-permute-done | bytes 131104 | tf_op jit(solution)/shard_map/ppermute | solution.py:50
  67.5 2.6 %collective-permute-start.9 = (f32[128,256]{1,0:T(8,128)S(1)}, f32[128,256]{1,0:T(8,128)S(1)}, u32[]{:S(2)}, u32[]{:S(2)}) collective-permute-start(f32[128,256]{1,0:T(8,128)S(1)} %add_add_fusion.1), channel_id=1, source_target_pairs={{0,3},{1,0},{2,1},{3,2},{4,7},{5,4},{6,5},{7,6},{8,11},{9,8},{10,9... | collective-permute-start | bytes 393224 | tf_op jit(solution)/shard_map/ppermute | solution.py:50
  70.0 0.5 collective-permute-start.8
  70.6 0.6 collective-permute-start.7
  71.2 1.8 collective-permute-done.9
  73.0 2.5 %collective-permute-done.8 = f32[128,256]{1,0:T(8,128)S(1)} collective-permute-done((f32[128,256]{1,0:T(8,128)S(1)}, f32[128,256]{1,0:T(8,128)S(1)}, u32[]{:S(2)}, u32[]{:S(2)}) %collective-permute-start.8) | collective-permute-done | bytes 131104 | tf_op jit(solution)/shard_map/ppermute | solution.py:50
  75.5 1.3 collective-permute-done.7
  76.8 2.8 %collective-permute-start.12 = (f32[128,256]{1,0:T(8,128)S(1)}, f32[128,256]{1,0:T(8,128)S(1)}, u32[]{:S(2)}, u32[]{:S(2)}) collective-permute-start(f32[128,256]{1,0:T(8,128)S(1)} %add_add_fusion.p0), channel_id=1, source_target_pairs={{0,24},{8,0},{16,8},{24,16},{1,25},{9,1},{17,9},{25,17},{2,26},{10... | collective-permute-start | bytes 393224 | tf_op jit(solution)/shard_map/ppermute | solution.py:50
  80.0 0.7 collective-permute-start.10
  80.7 2.3 %collective-permute-done.12.p3 = f32[128,256]{1,0:T(8,128)S(1)} collective-permute-done((f32[128,256]{1,0:T(8,128)S(1)}, f32[128,256]{1,0:T(8,128)S(1)}, u32[]{:S(2)}, u32[]{:S(2)}) %collective-permute-start.12) | collective-permute-done | bytes 131104 | tf_op jit(solution)/shard_map/ppermute | solution.py:50
  83.0 2.1 %collective-permute-done.11.p2 = f32[128,256]{1,0:T(8,128)S(1)} collective-permute-done((f32[128,256]{1,0:T(8,128)S(1)}, f32[128,256]{1,0:T(8,128)S(1)}, u32[]{:S(2)}, u32[]{:S(2)}) %collective-permute-start.11) | collective-permute-done | bytes 131104 | tf_op jit(solution)/shard_map/ppermute | solution.py:50
  85.1 1.3 collective-permute-done.10.p1
  86.4 3.4 %shard_map.70 = (f32[8,104,256]{2,1,0:T(8,128)S(1)}, f32[8,104,256]{2,1,0:T(8,128)S(1)}) custom-call(s32[3]{0:T(128)S(1)} %pad_add_fusion.pos, f32[8,176,128]{2,1,0:T(8,128)S(1)} %get-tuple-element.25.s0, f32[8,176,128]{2,1,0:T(8,128)S(1)} %collective-permute-done.s1, f32[8,176,128]{2,1,0:T(8,128)S(1)} %collective-permute-done.5.s2, ...), custom_call_target="tpu_custom_call" | custom-call | flops 1107296256 | bytes 4325376 | tf_op jit(solution)/shard_map/pallas_call | solution.py:174
  89.8 5.3 %collective-permute-start.13 = (f32[8,104,256]{2,1,0:T(8,128)S(1)}, f32[8,104,256]{2,1,0:T(8,128)S(1)}, u32[]{:S(2)}, u32[]{:S(2)}) collective-permute-start(f32[8,104,256]{2,1,0:T(8,128)S(1)} %get-tuple-element.34), channel_id=1, source_target_pairs={{0,4},{4,0},{1,5},{5,1},{2,6},{6,2},{3,7},{7,3},{8,12},{12,8},{9,1... | collective-permute-start | bytes 2555912 | tf_op jit(solution)/shard_map/ppermute | solution.py:46
  95.0 2.0 %collective-permute-done.13 = f32[8,104,256]{2,1,0:T(8,128)S(1)} collective-permute-done((f32[8,104,256]{2,1,0:T(8,128)S(1)}, f32[8,104,256]{2,1,0:T(8,128)S(1)}, u32[]{:S(2)}, u32[]{:S(2)}) %collective-permute-start.13) | collective-permute-done | bytes 852000 | tf_op jit(solution)/shard_map/ppermute | solution.py:46
  97.2 27.4 %all_to_all.20 = f32[8,104,256]{2,1,0:T(8,128)S(1)} all-to-all(f32[8,104,256]{2,1,0:T(8,128)S(1)} %add.53), channel_id=1, replica_groups=mesh['z'=8,'y'=4,'c'=2,'x'=4] {'z'}, dimensions={0} | all-to-all | bytes 1703936 | tf_op jit(solution)/shard_map/all_to_all | solution.py:42
  124.6 0.4 collective-permute-start.15
  125.0 0.5 collective-permute-start.14
  125.6 2.2 %collective-permute-start.16 = (f32[16,256]{1,0:T(8,128)S(1)}, f32[16,256]{1,0:T(8,128)S(1)}, u32[]{:S(2)}, u32[]{:S(2)}) collective-permute-start(f32[16,256]{1,0:T(8,128)S(1)} %get-tuple-element.40), channel_id=1, source_target_pairs={{0,24},{8,0},{16,8},{24,16},{1,25},{9,1},{17,9},{25,17},{2,26},{10... | collective-permute-start | bytes 49160 | tf_op jit(solution)/shard_map/ppermute | solution.py:50
  127.7 0.9 broadcast_in_dim.11
  128.6 4.2 %all-to-all-start.2 = ((f32[8,88,256]{2,1,0:T(8,128)}), f32[8,88,256]{2,1,0:T(8,128)}, u32[]{:S(2)}, u32[]{:S(2)}) async-start(f32[8,88,256]{2,1,0:T(8,128)} %broadcast_in_dim.11), calls=%async_computation.2 | async-start | bytes 1441792 | tf_op jit(solution)/shard_map/all_to_all | solution.py:38
  132.9 0.6 collective-permute-start.18
  133.8 2.3 %collective-permute-start.19 = (f32[4,16,256]{2,1,0:T(8,128)S(1)}, f32[4,16,256]{2,1,0:T(8,128)S(1)}, u32[]{:S(2)}, u32[]{:S(2)}) collective-permute-start(f32[4,16,256]{2,1,0:T(8,128)S(1)} %pad_maximum_fusion.1), channel_id=1, source_target_pairs={{0,3},{1,0},{2,1},{3,2},{4,7},{5,4},{6,5},{7,6},{8,11},{9,8},{10,9... | collective-permute-start | bytes 196616 | tf_op jit(solution)/shard_map/ppermute | solution.py:50
  136.2 2.1 %collective-permute-done.17 = f32[4,16,256]{2,1,0:T(8,128)S(1)} collective-permute-done((f32[4,16,256]{2,1,0:T(8,128)S(1)}, f32[4,16,256]{2,1,0:T(8,128)S(1)}, u32[]{:S(2)}, u32[]{:S(2)}) %collective-permute-start.17) | collective-permute-done | bytes 65568 | tf_op jit(solution)/shard_map/ppermute | solution.py:50
  138.7 10.4 %shard_map.71 = f32[256,256]{1,0:T(8,128)S(1)} custom-call(f32[256,256]{1,0:T(8,128)S(1)} %bitcast.40), custom_call_target="tpu_custom_call" | custom-call | flops 10000000000 | bytes 1000000 | tf_op jit(solution)/shard_map/pallas_call | solution.py:268
  149.0 6.0 %all-to-all-done.2.refs_0_ = f32[8,88,256]{2,1,0:T(8,128)} async-done(((f32[8,88,256]{2,1,0:T(8,128)}), f32[8,88,256]{2,1,0:T(8,128)}, u32[]{:S(2)}, u32[]{:S(2)}) %all-to-all-start.2) | async-done | bytes 720928 | tf_op jit(solution)/shard_map/all_to_all | solution.py:38
  155.2 1.2 collective-permute-start.21
  156.5 1.6 fusion
  158.1 1.1 collective-permute-start.20
  159.3 0.8 collective-permute-done.20
  160.1 0.6 broadcast_in_dim.27
  160.7 3.5 %all-to-all-start.3 = ((f32[16,1,256]{2,1,0:T(1,128)}), f32[16,1,256]{2,1,0:T(1,128)S(1)}, u32[]{:S(2)}, u32[]{:S(2)}) async-start(f32[16,1,256]{2,1,0:T(1,128)} %broadcast_in_dim.27), calls=%async_computation.3 | async-start | bytes 32768 | tf_op jit(solution)/shard_map/all_to_all | solution.py:38
  164.2 0.4 collective-permute-start.25
  164.6 9.2 %all-to-all-done.3 = f32[16,1,256]{2,1,0:T(1,128)S(1)} async-done(((f32[16,1,256]{2,1,0:T(1,128)}), f32[16,1,256]{2,1,0:T(1,128)S(1)}, u32[]{:S(2)}, u32[]{:S(2)}) %all-to-all-start.3) | async-done | bytes 16416 | tf_op jit(solution)/shard_map/all_to_all | solution.py:38
  173.9 1.1 slice.19
  175.0 0.9 collective-permute-start.24
  175.9 1.0 slice.18
  176.9 0.7 collective-permute-start.23
  177.6 2.2 %collective-permute-start.27 = (f32[8,88,256]{2,1,0:T(8,128)}, f32[8,88,256]{2,1,0:T(8,128)S(1)}, u32[]{:S(2)}, u32[]{:S(2)}) collective-permute-start(f32[8,88,256]{2,1,0:T(8,128)} %collective-permute-done.22.refs_2_), channel_id=1, source_target_pairs={{0,4},{4,0},{1,5},{5,1},{2,6},{6,2},{3,7},{7,3},{8,12},{12,8},{9,1... | collective-permute-start | bytes 2162696 | tf_op jit(solution)/shard_map/ppermute | solution.py:46
  179.9 0.4 broadcast_multiply_fusion
  180.3 3.0 %collective-permute-done.24.refs_4_ = f32[4,88,256]{2,1,0:T(8,128)S(1)} collective-permute-done((f32[4,88,256]{2,1,0:T(8,128)S(1)}, f32[4,88,256]{2,1,0:T(8,128)S(1)}, u32[]{:S(2)}, u32[]{:S(2)}) %collective-permute-start.24) | collective-permute-done | bytes 360480 | tf_op jit(solution)/shard_map/ppermute | solution.py:50
  183.3 2.6 %collective-permute-start.29 = (f32[4,88,256]{2,1,0:T(8,128)S(1)}, f32[4,88,256]{2,1,0:T(8,128)S(1)}, u32[]{:S(2)}, u32[]{:S(2)}) collective-permute-start(f32[4,88,256]{2,1,0:T(8,128)S(1)} %collective-permute-done.24.refs_4_), channel_id=1, source_target_pairs={{0,4},{4,0},{1,5},{5,1},{2,6},{6,2},{3,7},{7,3},{8,12},{12,8},{9,1... | collective-permute-start | bytes 1081352 | tf_op jit(solution)/shard_map/ppermute | solution.py:46
  186.2 2.8 %collective-permute-start.28 = (f32[4,88,256]{2,1,0:T(8,128)S(1)}, f32[4,88,256]{2,1,0:T(8,128)S(1)}, u32[]{:S(2)}, u32[]{:S(2)}) collective-permute-start(f32[4,88,256]{2,1,0:T(8,128)S(1)} %collective-permute-done.23.refs_3_), channel_id=1, source_target_pairs={{0,4},{4,0},{1,5},{5,1},{2,6},{6,2},{3,7},{7,3},{8,12},{12,8},{9,1... | collective-permute-start | bytes 1081352 | tf_op jit(solution)/shard_map/ppermute | solution.py:46
  189.1 0.9 convolution_multiply_fusion.1
  190.0 0.4 fusion.1.left
  190.4 1.8 copy-done.4
  192.3 7.1 %shard_map.72 = (f32[128,5632]{1,0:T(8,128)}, f32[128,5632]{1,0:T(8,128)}) custom-call(s32[3]{0:T(128)S(1)} %pad_add_fusion.pos, f32[256,256]{1,0:T(8,128)S(1)} %fusion.1.left, bf16[128,5632]{1,0:T(8,128)(2,1)S(1)} %copy-done.3, f32[128,5632]{1,0:T(8,128)S(1)} %copy-done.1, f32[128,5632]{1,0:T(8,128)S(1)} %copy-done.4, ...), custom_call_target="tpu_custom_call" | custom-call | flops 2214592512 | bytes 12976128 | tf_op jit(solution)/shard_map/pallas_call | solution.py:323
  (59 shorter events, 2.0 us)
Async XLA Ops:
  0.7 1.8 copy-start
  2.5 1.4 copy-start.2
  3.9 4.8 %copy-start.7 = (f32[88,256]{1,0:T(8,128)S(1)}, f32[88,256]{1,0:T(8,128)}, u32[]{:S(2)}) copy-start(f32[88,256]{1,0:T(8,128)} %param.7) | copy-start | bytes 270340
  7.0 0.9 copy-start.5
  7.9 0.9 copy-start.6
  9.7 31.2 %all-to-all-start = ((f32[8,88,256]{2,1,0:T(8,128)}), f32[8,88,256]{2,1,0:T(8,128)S(1)}, u32[]{:S(2)}, u32[]{:S(2)}) async-start(f32[8,88,256]{2,1,0:T(8,128)} %broadcast_in_dim.10), calls=%async_computation | async-start | bytes 1441792 | tf_op jit(solution)/shard_map/all_to_all | solution.py:38
  18.7 25.6 %collective-permute-start = (f32[8,176,128]{2,1,0:T(8,128)}, f32[8,176,128]{2,1,0:T(8,128)S(1)}, u32[]{:S(2)}, u32[]{:S(2)}) collective-permute-start(f32[8,176,128]{2,1,0:T(8,128)} %get-tuple-element.26), channel_id=1, source_target_pairs={{0,8},{8,16},{16,24},{24,0},{1,9},{9,17},{17,25},{25,1},{2,10},{10... | collective-permute-start | bytes 2162696 | tf_op jit(solution)/shard_map/ppermute | solution.py:50
  20.0 24.3 %collective-permute-start.1 = (f32[8,176,128]{2,1,0:T(8,128)}, f32[8,176,128]{2,1,0:T(8,128)S(1)}, u32[]{:S(2)}, u32[]{:S(2)}) collective-permute-start(f32[8,176,128]{2,1,0:T(8,128)} %copy-done.6), channel_id=1, source_target_pairs={{0,24},{8,0},{16,8},{24,16},{1,25},{9,1},{17,9},{25,17},{2,26},{10... | collective-permute-start | bytes 2162696 | tf_op jit(solution)/shard_map/ppermute | solution.py:50
  40.9 3.4 %collective-permute-start.2 = (f32[8,88,256]{2,1,0:T(8,128)S(1)}, f32[8,88,256]{2,1,0:T(8,128)S(1)}, u32[]{:S(2)}, u32[]{:S(2)}) collective-permute-start(f32[8,88,256]{2,1,0:T(8,128)S(1)} %all-to-all-done.refs_3_.refs_1_), channel_id=1, source_target_pairs={{0,4},{4,0},{1,5},{5,1},{2,6},{6,2},{3,7},{7,3},{8,12},{12,8},{9,1... | collective-permute-start | bytes 2162696 | tf_op jit(solution)/shard_map/ppermute | solution.py:46
  41.4 19.5 %collective-permute-start.5 = (f32[8,176,128]{2,1,0:T(8,128)}, f32[8,176,128]{2,1,0:T(8,128)S(1)}, u32[]{:S(2)}, u32[]{:S(2)}) collective-permute-start(f32[8,176,128]{2,1,0:T(8,128)} %copy-done.5), channel_id=1, source_target_pairs={{0,16},{8,24},{16,0},{24,8},{1,17},{9,25},{17,1},{25,9},{2,18},{10... | collective-permute-start | bytes 2162696 | tf_op jit(solution)/shard_map/ppermute | solution.py:50
  46.1 18.9 %collective-permute-start.3 = (f32[128,256]{1,0:T(8,128)S(1)}, f32[128,256]{1,0:T(8,128)S(1)}, u32[]{:S(2)}, u32[]{:S(2)}) collective-permute-start(f32[128,256]{1,0:T(8,128)S(1)} %get-tuple-element.30), channel_id=1, source_target_pairs={{0,24},{8,0},{16,8},{24,16},{1,25},{9,1},{17,9},{25,17},{2,26},{10... | collective-permute-start | bytes 393224 | tf_op jit(solution)/shard_map/ppermute | solution.py:50
  47.9 17.2 %collective-permute-start.4 = (f32[128,256]{1,0:T(8,128)S(1)}, f32[128,256]{1,0:T(8,128)S(1)}, u32[]{:S(2)}, u32[]{:S(2)}) collective-permute-start(f32[128,256]{1,0:T(8,128)S(1)} %get-tuple-element.31), channel_id=1, source_target_pairs={{0,8},{8,16},{16,24},{24,0},{1,9},{9,17},{17,25},{25,1},{2,10},{10... | collective-permute-start | bytes 393224 | tf_op jit(solution)/shard_map/ppermute | solution.py:50
  62.0 5.4 %collective-permute-start.6 = (f32[128,256]{1,0:T(8,128)S(1)}, f32[128,256]{1,0:T(8,128)S(1)}, u32[]{:S(2)}, u32[]{:S(2)}) collective-permute-start(f32[128,256]{1,0:T(8,128)S(1)} %shard_map.69), channel_id=1, source_target_pairs={{0,16},{8,24},{16,0},{24,8},{1,17},{9,25},{17,1},{25,9},{2,18},{10... | collective-permute-start | bytes 393224 | tf_op jit(solution)/shard_map/ppermute | solution.py:50
  67.5 5.5 %collective-permute-start.9 = (f32[128,256]{1,0:T(8,128)S(1)}, f32[128,256]{1,0:T(8,128)S(1)}, u32[]{:S(2)}, u32[]{:S(2)}) collective-permute-start(f32[128,256]{1,0:T(8,128)S(1)} %add_add_fusion.1), channel_id=1, source_target_pairs={{0,3},{1,0},{2,1},{3,2},{4,7},{5,4},{6,5},{7,6},{8,11},{9,8},{10,9... | collective-permute-start | bytes 393224 | tf_op jit(solution)/shard_map/ppermute | solution.py:50
  70.0 5.4 %collective-permute-start.8 = (f32[128,256]{1,0:T(8,128)S(1)}, f32[128,256]{1,0:T(8,128)S(1)}, u32[]{:S(2)}, u32[]{:S(2)}) collective-permute-start(f32[128,256]{1,0:T(8,128)S(1)} %add_add_fusion.1), channel_id=1, source_target_pairs={{0,2},{1,3},{2,0},{3,1},{4,6},{5,7},{6,4},{7,5},{8,10},{9,11},{10,... | collective-permute-start | bytes 393224 | tf_op jit(solution)/shard_map/ppermute | solution.py:50
  70.6 6.2 %collective-permute-start.7 = (f32[128,256]{1,0:T(8,128)S(1)}, f32[128,256]{1,0:T(8,128)S(1)}, u32[]{:S(2)}, u32[]{:S(2)}) collective-permute-start(f32[128,256]{1,0:T(8,128)S(1)} %add_add_fusion.1), channel_id=1, source_target_pairs={{0,1},{1,2},{2,3},{3,0},{4,5},{5,6},{6,7},{7,4},{8,9},{9,10},{10,1... | collective-permute-start | bytes 393224 | tf_op jit(solution)/shard_map/ppermute | solution.py:50
  76.8 6.2 %collective-permute-start.12 = (f32[128,256]{1,0:T(8,128)S(1)}, f32[128,256]{1,0:T(8,128)S(1)}, u32[]{:S(2)}, u32[]{:S(2)}) collective-permute-start(f32[128,256]{1,0:T(8,128)S(1)} %add_add_fusion.p0), channel_id=1, source_target_pairs={{0,24},{8,0},{16,8},{24,16},{1,25},{9,1},{17,9},{25,17},{2,26},{10... | collective-permute-start | bytes 393224 | tf_op jit(solution)/shard_map/ppermute | solution.py:50
  79.7 5.4 %collective-permute-start.11 = (f32[128,256]{1,0:T(8,128)S(1)}, f32[128,256]{1,0:T(8,128)S(1)}, u32[]{:S(2)}, u32[]{:S(2)}) collective-permute-start(f32[128,256]{1,0:T(8,128)S(1)} %add_add_fusion.p0), channel_id=1, source_target_pairs={{0,16},{8,24},{16,0},{24,8},{1,17},{9,25},{17,1},{25,9},{2,18},{10... | collective-permute-start | bytes 393224 | tf_op jit(solution)/shard_map/ppermute | solution.py:50
  80.0 6.4 %collective-permute-start.10 = (f32[128,256]{1,0:T(8,128)S(1)}, f32[128,256]{1,0:T(8,128)S(1)}, u32[]{:S(2)}, u32[]{:S(2)}) collective-permute-start(f32[128,256]{1,0:T(8,128)S(1)} %add_add_fusion.p0), channel_id=1, source_target_pairs={{0,8},{8,16},{16,24},{24,0},{1,9},{9,17},{17,25},{25,1},{2,10},{10... | collective-permute-start | bytes 393224 | tf_op jit(solution)/shard_map/ppermute | solution.py:50
  89.8 7.3 %collective-permute-start.13 = (f32[8,104,256]{2,1,0:T(8,128)S(1)}, f32[8,104,256]{2,1,0:T(8,128)S(1)}, u32[]{:S(2)}, u32[]{:S(2)}) collective-permute-start(f32[8,104,256]{2,1,0:T(8,128)S(1)} %get-tuple-element.34), channel_id=1, source_target_pairs={{0,4},{4,0},{1,5},{5,1},{2,6},{6,2},{3,7},{7,3},{8,12},{12,8},{9,1... | collective-permute-start | bytes 2555912 | tf_op jit(solution)/shard_map/ppermute | solution.py:46
  124.6 8.2 %collective-permute-start.15 = (f32[16,256]{1,0:T(8,128)S(1)}, f32[16,256]{1,0:T(8,128)S(1)}, u32[]{:S(2)}, u32[]{:S(2)}) collective-permute-start(f32[16,256]{1,0:T(8,128)S(1)} %get-tuple-element.40), channel_id=1, source_target_pairs={{0,16},{8,24},{16,0},{24,8},{1,17},{9,25},{17,1},{25,9},{2,18},{10... | collective-permute-start | bytes 49160 | tf_op jit(solution)/shard_map/ppermute | solution.py:50
  125.0 7.8 %collective-permute-start.14 = (f32[16,256]{1,0:T(8,128)S(1)}, f32[16,256]{1,0:T(8,128)S(1)}, u32[]{:S(2)}, u32[]{:S(2)}) collective-permute-start(f32[16,256]{1,0:T(8,128)S(1)} %get-tuple-element.40), channel_id=1, source_target_pairs={{0,8},{8,16},{16,24},{24,0},{1,9},{9,17},{17,25},{25,1},{2,10},{10... | collective-permute-start | bytes 49160 | tf_op jit(solution)/shard_map/ppermute | solution.py:50
  125.6 7.3 %collective-permute-start.16 = (f32[16,256]{1,0:T(8,128)S(1)}, f32[16,256]{1,0:T(8,128)S(1)}, u32[]{:S(2)}, u32[]{:S(2)}) collective-permute-start(f32[16,256]{1,0:T(8,128)S(1)} %get-tuple-element.40), channel_id=1, source_target_pairs={{0,24},{8,0},{16,8},{24,16},{1,25},{9,1},{17,9},{25,17},{2,26},{10... | collective-permute-start | bytes 49160 | tf_op jit(solution)/shard_map/ppermute | solution.py:50
  128.6 26.4 %all-to-all-start.2 = ((f32[8,88,256]{2,1,0:T(8,128)}), f32[8,88,256]{2,1,0:T(8,128)}, u32[]{:S(2)}, u32[]{:S(2)}) async-start(f32[8,88,256]{2,1,0:T(8,128)} %broadcast_in_dim.11), calls=%async_computation.2 | async-start | bytes 1441792 | tf_op jit(solution)/shard_map/all_to_all | solution.py:38
  132.9 5.4 %collective-permute-start.18 = (f32[4,16,256]{2,1,0:T(8,128)S(1)}, f32[4,16,256]{2,1,0:T(8,128)S(1)}, u32[]{:S(2)}, u32[]{:S(2)}) collective-permute-start(f32[4,16,256]{2,1,0:T(8,128)S(1)} %pad_maximum_fusion.1), channel_id=1, source_target_pairs={{0,2},{1,3},{2,0},{3,1},{4,6},{5,7},{6,4},{7,5},{8,10},{9,11},{10,... | collective-permute-start | bytes 196616 | tf_op jit(solution)/shard_map/ppermute | solution.py:50
  133.5 4.8 %collective-permute-start.17 = (f32[4,16,256]{2,1,0:T(8,128)S(1)}, f32[4,16,256]{2,1,0:T(8,128)S(1)}, u32[]{:S(2)}, u32[]{:S(2)}) collective-permute-start(f32[4,16,256]{2,1,0:T(8,128)S(1)} %pad_maximum_fusion.1), channel_id=1, source_target_pairs={{0,1},{1,2},{2,3},{3,0},{4,5},{5,6},{6,7},{7,4},{8,9},{9,10},{10,1... | collective-permute-start | bytes 196616 | tf_op jit(solution)/shard_map/ppermute | solution.py:50
  133.8 4.5 %collective-permute-start.19 = (f32[4,16,256]{2,1,0:T(8,128)S(1)}, f32[4,16,256]{2,1,0:T(8,128)S(1)}, u32[]{:S(2)}, u32[]{:S(2)}) collective-permute-start(f32[4,16,256]{2,1,0:T(8,128)S(1)} %pad_maximum_fusion.1), channel_id=1, source_target_pairs={{0,3},{1,0},{2,1},{3,2},{4,7},{5,4},{6,5},{7,6},{8,11},{9,8},{10,9... | collective-permute-start | bytes 196616 | tf_op jit(solution)/shard_map/ppermute | solution.py:50
  149.0 41.4 %copy-start.1 = (f32[128,5632]{1,0:T(8,128)S(1)}, f32[128,5632]{1,0:T(8,128)}, u32[]{:S(2)}) copy-start(f32[128,5632]{1,0:T(8,128)} %mom.3) | copy-start | bytes 8650756
  155.0 18.9 %collective-permute-start.22 = (f32[8,88,256]{2,1,0:T(8,128)}, f32[8,88,256]{2,1,0:T(8,128)}, u32[]{:S(2)}, u32[]{:S(2)}) collective-permute-start(f32[8,88,256]{2,1,0:T(8,128)} %all-to-all-done.2.refs_0_), channel_id=1, source_target_pairs={{0,24},{8,0},{16,8},{24,16},{1,25},{9,1},{17,9},{25,17},{2,26},{10... | collective-permute-start | bytes 2162696 | tf_op jit(solution)/shard_map/ppermute | solution.py:50
  155.2 20.7 %collective-permute-start.21 = (f32[8,88,256]{2,1,0:T(8,128)}, f32[8,88,256]{2,1,0:T(8,128)}, u32[]{:S(2)}, u32[]{:S(2)}) collective-permute-start(f32[8,88,256]{2,1,0:T(8,128)} %all-to-all-done.2.refs_0_), channel_id=1, source_target_pairs={{0,8},{8,16},{16,24},{24,0},{1,9},{9,17},{17,25},{25,1},{2,10},{10... | collective-permute-start | bytes 2162696 | tf_op jit(solution)/shard_map/ppermute | solution.py:50
  158.1 2.0 collective-permute-start.20
  160.7 13.1 %all-to-all-start.3 = ((f32[16,1,256]{2,1,0:T(1,128)}), f32[16,1,256]{2,1,0:T(1,128)S(1)}, u32[]{:S(2)}, u32[]{:S(2)}) async-start(f32[16,1,256]{2,1,0:T(1,128)} %broadcast_in_dim.27), calls=%async_computation.3 | async-start | bytes 32768 | tf_op jit(solution)/shard_map/all_to_all | solution.py:38
  164.2 26.2 %collective-permute-start.25 = (f32[8,88,256]{2,1,0:T(8,128)}, f32[8,88,256]{2,1,0:T(8,128)}, u32[]{:S(2)}, u32[]{:S(2)}) collective-permute-start(f32[8,88,256]{2,1,0:T(8,128)} %all-to-all-done.2.refs_0_), channel_id=1, source_target_pairs={{0,4},{4,0},{1,5},{5,1},{2,6},{6,2},{3,7},{7,3},{8,12},{12,8},{9,1... | collective-permute-start | bytes 2162696 | tf_op jit(solution)/shard_map/ppermute | solution.py:46
  173.8 16.6 %copy-start.3 = (bf16[128,5632]{1,0:T(8,128)(2,1)S(1)}, bf16[128,5632]{1,0:T(8,128)(2,1)}, u32[]{:S(2)}) copy-start(bf16[128,5632]{1,0:T(8,128)(2,1)} %grad.3) | copy-start | bytes 4325380
  175.0 8.3 %collective-permute-start.24 = (f32[4,88,256]{2,1,0:T(8,128)S(1)}, f32[4,88,256]{2,1,0:T(8,128)S(1)}, u32[]{:S(2)}, u32[]{:S(2)}) collective-permute-start(f32[4,88,256]{2,1,0:T(8,128)S(1)} %slice.19), channel_id=1, source_target_pairs={{0,24},{8,0},{16,8},{24,16},{1,25},{9,1},{17,9},{25,17},{2,26},{10... | collective-permute-start | bytes 1081352 | tf_op jit(solution)/shard_map/ppermute | solution.py:50
  176.9 9.3 %collective-permute-start.23 = (f32[4,88,256]{2,1,0:T(8,128)S(1)}, f32[4,88,256]{2,1,0:T(8,128)S(1)}, u32[]{:S(2)}, u32[]{:S(2)}) collective-permute-start(f32[4,88,256]{2,1,0:T(8,128)S(1)} %slice.18), channel_id=1, source_target_pairs={{0,8},{8,16},{16,24},{24,0},{1,9},{9,17},{17,25},{25,1},{2,10},{10... | collective-permute-start | bytes 1081352 | tf_op jit(solution)/shard_map/ppermute | solution.py:50
  177.6 12.8 %collective-permute-start.27 = (f32[8,88,256]{2,1,0:T(8,128)}, f32[8,88,256]{2,1,0:T(8,128)S(1)}, u32[]{:S(2)}, u32[]{:S(2)}) collective-permute-start(f32[8,88,256]{2,1,0:T(8,128)} %collective-permute-done.22.refs_2_), channel_id=1, source_target_pairs={{0,4},{4,0},{1,5},{5,1},{2,6},{6,2},{3,7},{7,3},{8,12},{12,8},{9,1... | collective-permute-start | bytes 2162696 | tf_op jit(solution)/shard_map/ppermute | solution.py:46
  179.8 10.6 %collective-permute-start.26 = (f32[8,88,256]{2,1,0:T(8,128)}, f32[8,88,256]{2,1,0:T(8,128)S(1)}, u32[]{:S(2)}, u32[]{:S(2)}) collective-permute-start(f32[8,88,256]{2,1,0:T(8,128)} %collective-permute-done.21.refs_1_), channel_id=1, source_target_pairs={{0,4},{4,0},{1,5},{5,1},{2,6},{6,2},{3,7},{7,3},{8,12},{12,8},{9,1... | collective-permute-start | bytes 2162696 | tf_op jit(solution)/shard_map/ppermute | solution.py:46
  183.3 7.1 %collective-permute-start.29 = (f32[4,88,256]{2,1,0:T(8,128)S(1)}, f32[4,88,256]{2,1,0:T(8,128)S(1)}, u32[]{:S(2)}, u32[]{:S(2)}) collective-permute-start(f32[4,88,256]{2,1,0:T(8,128)S(1)} %collective-permute-done.24.refs_4_), channel_id=1, source_target_pairs={{0,4},{4,0},{1,5},{5,1},{2,6},{6,2},{3,7},{7,3},{8,12},{12,8},{9,1... | collective-permute-start | bytes 1081352 | tf_op jit(solution)/shard_map/ppermute | solution.py:46
  186.2 4.2 %collective-permute-start.28 = (f32[4,88,256]{2,1,0:T(8,128)S(1)}, f32[4,88,256]{2,1,0:T(8,128)S(1)}, u32[]{:S(2)}, u32[]{:S(2)}) collective-permute-start(f32[4,88,256]{2,1,0:T(8,128)S(1)} %collective-permute-done.23.refs_3_), channel_id=1, source_target_pairs={{0,4},{4,0},{1,5},{5,1},{2,6},{6,2},{3,7},{7,3},{8,12},{12,8},{9,1... | collective-permute-start | bytes 1081352 | tf_op jit(solution)/shard_map/ppermute | solution.py:46
  190.4 1.8 copy-start.4

commit v2 on v1

--- a/solution.py
+++ b/solution.py
@@ -81,39 +81,34 @@
     return pl.BlockSpec(memory_space=pltpu.SMEM)
 
 
-def split_kernel(pos, grad, mom, out0, out1, out2, out3, turned):
-    y = pos[0]
+def split_kernel(grad, mom, out, turned):
     turned[...] = (mom[...] + grad[...].astype(jnp.float32)).T
-    size = out0.shape[1]
-    for d, out in enumerate((out0, out1, out2, out3)):
-        owner = lax.rem(y + d, NY)
-        for part in range(out.shape[0]):
-            start = pl.multiple_of((part * NY + owner) * size, 8)
-            out[part] = turned[pl.ds(start, size), :]
-
-
-def split_columns(pos, gradient, momentum):
+    size = out.shape[2]
+    for part in range(out.shape[1]):
+        for owner in range(NY):
+            start = (part * NY + owner) * size
+            out[owner, part] = turned[start : start + size]
+
+
+def split_columns(gradient, momentum):
     rows, cols = momentum.shape
     wide = 2 * cols // NZ
     size = wide // (2 * NY)
     block = pl.BlockSpec((rows, wide), lambda i: (0, i))
-    piece = pl.BlockSpec((2, size, rows), lambda i: (i, 0, 0))
     return pl.pallas_call(
         split_kernel,
         grid=(NZ // 2,),
-        in_specs=[smem(), block, block],
-        out_specs=[piece] * NY,
-        out_shape=[jax.ShapeDtypeStruct((NZ, size, rows), jnp.float32)] * NY,
+        in_specs=[block, block],
+        out_specs=pl.BlockSpec((NY, 2, size, rows), lambda i: (0, i, 0, 0)),
+        out_shape=jax.ShapeDtypeStruct((NY, NZ, size, rows), jnp.float32),
         scratch_shapes=[pltpu.VMEM((wide, rows), jnp.float32)],
-        compiler_params=params(16),
+        compiler_params=params(60),
         cost_estimate=cost(0, rows * cols * 10),
-    )(pos, gradient, momentum)
-
-
-def project_kernel(count, pos, *refs):
-    core = pos[1]
-    mine, other = refs[count : count + 2]
-    full = refs[-1]
+    )(gradient, momentum)
+
+
+def project_kernel(pos, strips, mine, other, o0, o1, o2, o3, full):
+    y, core = pos[0], pos[1]
     half = mine.shape[1]
     for z in range(NZ):
         start = pl.multiple_of(z * 2 * half + core * half, 8)
@@ -121,28 +116,26 @@
         start = pl.multiple_of(z * 2 * half + (1 - core) * half, 8)
         full[pl.ds(start, half), :] = other[z]
     right = halves(full[...])
-    for strip, out in zip(refs[:count], refs[count + 2 : -1]):
-        out[...] = dot_halves(halves(strip[...]), right, 0, 0)
+    for d, out in enumerate((o0, o1, o2, o3)):
+        out[...] = dot_halves(halves(strips[lax.rem(y + NY - d, NY)]), right, 0, 0)
 
 
 def project(pos, strips, mine, other):
-    cols, rows = strips[0].shape
-    count = len(strips)
+    _, cols, rows = strips.shape
     return pl.pallas_call(
-        functools.partial(project_kernel, count),
-        in_specs=[smem()] + [pl.BlockSpec(memory_space=pltpu.VMEM)] * (count + 2),
-        out_specs=[pl.BlockSpec(memory_space=pltpu.VMEM)] * count,
-        out_shape=[jax.ShapeDtypeStruct((rows, RANK), jnp.float32)] * count,
+        project_kernel,
+        in_specs=[smem()] + [pl.BlockSpec(memory_space=pltpu.VMEM)] * 3,
+        out_specs=[pl.BlockSpec(memory_space=pltpu.VMEM)] * NY,
+        out_shape=[jax.ShapeDtypeStruct((rows, RANK), jnp.float32)] * NY,
         scratch_shapes=[pltpu.VMEM((cols, RANK), jnp.float32)],
         compiler_params=params(24),
-        cost_estimate=cost(6 * count * rows * cols * RANK, count * rows * cols * 8),
-    )(pos, *strips, mine, other)
-
-
-def feedback_kernel(pos, s0, s1, s2, s3, p0, p1, p2, p3, mine, other, low, high, full, gram):
-    core = pos[1]
-    rows = s0.shape[2]
-    steps, size = s0.shape[:2]
+        cost_estimate=cost(6 * NY * rows * cols * RANK, NY * rows * cols * 8),
+    )(pos, strips, mine, other)
+
+
+def feedback_kernel(pos, strips, p0, p1, p2, p3, mine, other, low, high, full, gram):
+    y, core = pos[0], pos[1]
+    steps, size = strips.shape[1:3]
     half = size // 2
     part = mine.shape[1] - half
 
@@ -156,7 +149,9 @@
     other_at = pl.multiple_of((1 - core) * half, 8)
     gram_rows = gram[pl.ds(pl.multiple_of(pos[2] * part, 8), part), :]
     for z in range(steps):
-        strip = jnp.concatenate([s0[z], s1[z], s2[z], s3[z]], axis=1)
+        strip = jnp.concatenate(
+            [strips[lax.rem(y + NY - d, NY), z] for d in range(NY)], axis=1
+        )
         full[...] = dot_halves(halves(strip), (high[...], low[...]), 1, 0)
         mine[z, :half] = full[pl.ds(mine_at, half), :]
         other[z, :half] = full[pl.ds(other_at, half), :]
@@ -165,16 +160,16 @@
 
 
 def raw_feedback(pos, strips, projs):
-    _, size, rows = strips[0].shape
+    _, _, size, rows = strips.shape
     part = RANK // (NY * NX)
     steps = 2
-    strip = pl.BlockSpec((steps, size, rows), lambda z: (z, 0, 0))
+    strip = pl.BlockSpec((NY, steps, size, rows), lambda z: (0, z, 0, 0))
     proj = pl.BlockSpec((rows, RANK), lambda z: (0, 0))
     out = pl.BlockSpec((steps, size // 2 + part, RANK), lambda z: (z, 0, 0))
     return pl.pallas_call(
         feedback_kernel,
         grid=(NZ // steps,),
-        in_specs=[smem()] + [strip] * NY + [proj] * NY,
+        in_specs=[smem(), strip] + [proj] * NY,
         out_specs=[out] * 2,
         out_shape=[jax.ShapeDtypeStruct((NZ, size // 2 + part, RANK), jnp.float32)] * 2,
         scratch_shapes=[
@@ -185,7 +180,7 @@
         ],
         compiler_params=params(24),
         cost_estimate=cost(6 * NY * rows * NZ * size * RANK, NZ * size * rows * 24),
-    )(pos, *strips, *projs)
+    )(pos, strips, *projs)
 
 
 BLOCK = 64
@@ -327,7 +322,7 @@
         out_specs=[block, block],
         out_shape=[jax.ShapeDtypeStruct(momentum.shape, jnp.float32)] * 2,
         scratch_shapes=[pltpu.VMEM((wide, RANK), jnp.float32)],
-        compiler_params=params(28),
+        compiler_params=params(48),
         cost_estimate=cost(12 * rows * cols * RANK, rows * cols * 18),
     )(pos, left, gradient, momentum, weight, *mine, *other)
 
@@ -338,17 +333,11 @@
     rows, cols = momentum.shape
     shard = basis.shape[0]
 
-    sent = split_columns(pos, gradient, momentum)
-    sent, basis = lax.optimization_barrier((sent, basis))
-    strips = [sent[0], None, None, None]
-    for d in (2, 1, 3):
-        strips[d] = shift(sent[d], "y", NY, d)
-    flat = [strip.reshape(NZ * NC * shard, rows) for strip in strips]
-
-    basis_z = gather(basis, "z", NZ)
-    basis_other = swap(basis_z)
-    near, first, third = project(pos, [flat[0], flat[1], flat[3]], basis_z, basis_other)
-    (second,) = project(pos, [flat[2]], basis_z, basis_other)
+    sent = split_columns(gradient, momentum)
+    strips = lax.all_to_all(sent, "y", 0, 0)
+    basis_z = lax.all_gather(basis, "z", axis=0)
+    flat = strips.reshape(NY, NZ * NC * shard, rows)
+    near, first, second, third = project(pos, flat, basis_z, swap(basis_z))
     projected = (
         near
         + shift(first, "y", NY, NY - 1)
@@ -361,8 +350,8 @@
     mine, other = raw_feedback(pos, strips, projs)
     reduced = scatter_sum(mine + swap(other), "z")
     raw_shard, gram_part = reduced[:shard], reduced[shard:]
-
     raw = gather(raw_shard, "z", NZ)
+
     by_y = jnp.stack([gram_part] + [shift(gram_part, "y", NY, d) for d in range(1, NY)])
     by_x = jnp.stack([by_y] + [shift(by_y, "x", NX, d) for d in range(1, NX)])
     by_x = jnp.flip(jnp.concatenate([by_x, by_x], 0), 0)
@@ -373,26 +362,28 @@
     inverse = factor_inverse(gram_matrix)
 
     raw, inverse = lax.optimization_barrier((raw, inverse))
-    ahead = shift(raw, "y", NY, 1)
-    behind = shift(raw, "y", NY, NY - 1)
-    ahead2 = shift(ahead[: NZ // 2], "y", NY, 1)
-    behind2 = shift(behind[NZ // 2 :], "y", NY, NY - 1)
-    own = [raw, ahead, behind, ahead2, behind2]
-    paired = [swap(block) for block in own]
-
-    orthonormal = dot(projected, inverse, 1, 1, HIGHEST)
-    strip_feedback = dot(raw.reshape(NZ * shard, RANK), inverse, 1, 1)
-    squares = jnp.sum(strip_feedback * strip_feedback, axis=0, keepdims=True)
+    feedback = dot(raw.reshape(NZ * shard, RANK), inverse, 1, 1)
+    squares = jnp.sum(feedback * feedback, axis=0, keepdims=True)
+    feedback = feedback.reshape(NZ, shard, RANK)
+    ahead = shift(feedback, "y", NY, 1)
+    behind = shift(feedback, "y", NY, NY - 1)
     squares = squares + swap(squares)
     squares = jnp.sum(gather(squares, ("y", "x"), NY * NX), axis=0)
+    squares, ahead, behind = lax.optimization_barrier((squares, ahead, behind))
+    far_low = shift(ahead[: NZ // 2], "y", NY, 1)
+    far_high = shift(behind[NZ // 2 :], "y", NY, NY - 1)
+    own = [feedback, ahead, behind, far_low, far_high]
+    paired = [swap(block) for block in own]
     scales = math.sqrt(FF) / (jnp.sqrt(squares) + epsilon)
 
+    orthonormal = dot(projected, inverse, 1, 1, HIGHEST)
     left = jnp.concatenate([orthonormal, orthonormal * scales], axis=0)
-    left = dot(left, inverse, 1, 0, HIGHEST)
     new_momentum, new_weight = update(
         pos, left, gradient, momentum, weight, own, paired
     )
-    new_basis = dot(raw_shard, inverse, 1, 1) * scales
+    new_basis = scales * lax.dynamic_index_in_dim(
+        feedback, lax.axis_index("z"), 0, keepdims=False
+    )
     return (new_momentum, new_weight, new_basis)
 
 

time: 200 us -> 183 us (0.915)
  waiting for transfers between devices: 69.6 us -> 24.5 us
  blocking collectives: 27.4 us -> 67.2 us
  local copies, waits for them, and re-layouts: 11.5 us -> 2.62 us
  starting transfers between devices: 59.2 us -> 56.6 us
  matrix products: 3.35 us -> 0.9 us
  Pallas kernels: 26.9 us -> 29.1 us
    all_to_all x3 -> x1, waiting for transfers between devices: 34.5 us -> 3.56 us  [gather(): return lax.all_to_all(copies, axes, 0, 0)]
    all_gather x0 -> x1, blocking collectives: none -> 27.1 us  [body(): basis_z = lax.all_gather(basis, 'z', axis=0)]
    ppermute x22 -> x19, waiting for transfers between devices: 32.2 us -> 15.8 us  [shift(): lax.ppermute(block, axis, [(i, (i + step) % size) for i in range(size)])]
    all_to_all x3 -> x1, starting transfers between devices: 16.7 us -> 3.54 us  [gather(): return lax.all_to_all(copies, axes, 0, 0)]
    all_to_all x0 -> x1, blocking collectives: none -> 10.5 us  [gather(): return lax.all_to_all(copies, axes, 0, 0)]
    unnamed x21 -> x7, local copies, waits for them, and re-layouts: 6.75 us -> 0.04 us
    ppermute x8, starting transfers between devices: 15 us -> 21.7 us  [swap(): return lax.ppermute(block, 'c', [(0, 1), (1, 0)])]
    all_to_all x0 -> x1, starting transfers between devices: none -> 5.14 us  [body(): strips = lax.all_to_all(sent, 'y', 0, 0)]
  transfers between devices with their start and end apart: 33 -> 29, of which waited for: 16 -> 16; matrix products, arithmetic and copies ran while one was open for 4% -> 2% of each run, Pallas kernels for 7% -> 6%
where the time goes in v2:
time: 183 us
  blocking collectives  67.2 us (37%)
  starting transfers between devices  56.6 us (31%)
  Pallas kernels  29.1 us (16%)
  waiting for transfers between devices  24.5 us (13%)
  local copies, waits for them, and re-layouts  2.62 us (1%)
    all_to_all x1, blocking collectives, scatter_sum(): return jnp.sum(lax.all_to_all(blocks, axes, 0, 0), axis=0)  29.6 us
    all_gather x1, blocking collectives, body(): basis_z = lax.all_gather(basis, 'z', axis=0)  27.1 us
    ppermute x19, starting transfers between devices, shift(): lax.ppermute(block, axis, [(i, (i + step) % size) for i in range(size)])  26.3 us
    ppermute x8, starting transfers between devices, swap(): return lax.ppermute(block, 'c', [(0, 1), (1, 0)])  21.7 us
    ppermute x19, waiting for transfers between devices, shift(): lax.ppermute(block, axis, [(i, (i + step) % size) for i in range(size)])  15.8 us
    all_to_all x1, blocking collectives, gather(): return lax.all_to_all(copies, axes, 0, 0)  10.5 us
    pallas_call x1, Pallas kernels, factor_inverse(): pl.pallas_call(inverse_kernel, in_specs=[pl.BlockSpec(memory_space=pltpu....  10.4 us
    pallas_call x1, Pallas kernels, update(): pl.pallas_call(update_kernel, grid=(NZ // 2,), in_specs=[smem(), whole, b...  7.55 us
  transfers between devices with their start and end apart: 29, of which 16 were waited for; matrix products, arithmetic and copies ran while one was open for 2% of the time, Pallas kernels for 6%

profile of v2, /device:TPU:1, one launch (start us, length us, event | category | flops | bytes accessed | tf_op | source)
XLA Modules:
  0.0 182.9 jit_solution(719322545856741357)
XLA Ops:
  0.6 4.8 %shard_map.67 = f32[4,8,176,128]{3,2,1,0:T(8,128)} custom-call(bf16[128,5632]{1,0:T(8,128)(2,1)} %grad.3, f32[128,5632]{1,0:T(8,128)} %mom.3), custom_call_target="tpu_custom_call" | custom-call | bytes 7208960 | tf_op jit(solution)/shard_map/pallas_call | solution.py:98
  5.4 5.1 %all-to-all-start = ((f32[4,8,176,128]{3,2,1,0:T(8,128)}), f32[4,8,176,128]{3,2,1,0:T(8,128)S(1)}, u32[]{:S(2)}, u32[]{:S(2)}) async-start(f32[4,8,176,128]{3,2,1,0:T(8,128)} %shard_map.67), calls=%async_computation | async-start | bytes 5767168 | tf_op jit(solution)/shard_map/all_to_all | solution.py:337
  10.6 27.1 %all-gather = f32[704,256]{1,0:T(8,128)} all-gather(f32[88,256]{1,0:T(8,128)S(1)} %copy-done), channel_id=2, replica_groups=mesh['z'=8,'y'=4,'c'=2,'x'=4] {'z'}, dimensions={0}, use_global_device_ids=true | all-gather | bytes 811008 | tf_op jit(solution)/shard_map/all_gather | solution.py:338
  37.6 5.4 %collective-permute-start = (f32[8,88,256]{2,1,0:T(8,128)}, f32[8,88,256]{2,1,0:T(8,128)}, u32[]{:S(2)}, u32[]{:S(2)}) collective-permute-start(f32[8,88,256]{2,1,0:T(8,128)} %bitcast.4.mine), channel_id=1, source_target_pairs={{0,4},{4,0},{1,5},{5,1},{2,6},{6,2},{3,7},{7,3},{8,12},{12,8},{9,1... | collective-permute-start | bytes 2162696 | tf_op jit(solution)/shard_map/ppermute | solution.py:46
  43.1 0.1 pad_add_fusion.pos
  43.1 2.1 %collective-permute-done.other = f32[8,88,256]{2,1,0:T(8,128)} collective-permute-done((f32[8,88,256]{2,1,0:T(8,128)}, f32[8,88,256]{2,1,0:T(8,128)}, u32[]{:S(2)}, u32[]{:S(2)}) %collective-permute-start) | collective-permute-done | bytes 720928 | tf_op jit(solution)/shard_map/ppermute | solution.py:46
  45.2 0.0 all-to-all-done.strips
  45.2 2.9 %shard_map.68 = (f32[128,256]{1,0:T(8,128)S(1)}, f32[128,256]{1,0:T(8,128)S(1)}, f32[128,256]{1,0:T(8,128)S(1)}, f32[128,256]{1,0:T(8,128)S(1)}) custom-call(s32[3]{0:T(128)S(1)} %pad_add_fusion.pos, f32[4,1408,128]{2,1,0:T(8,128)S(1)} %bitcast.46, f32[8,88,256]{2,1,0:T(8,128)} %bitcast.4.mine, f32[8,88,256]{2,1,0:T(8,128)} %collective-permute-done.other), custom_call_target="tpu_custom_call" | custom-call | flops 1107296256 | bytes 5767168 | tf_op jit(solution)/shard_map/pallas_call | solution.py:125
  48.1 3.5 %collective-permute-start.3 = (f32[128,256]{1,0:T(8,128)S(1)}, f32[128,256]{1,0:T(8,128)S(1)}, u32[]{:S(2)}, u32[]{:S(2)}) collective-permute-start(f32[128,256]{1,0:T(8,128)S(1)} %get-tuple-element.19), channel_id=1, source_target_pairs={{0,16},{8,24},{16,0},{24,8},{1,17},{9,25},{17,1},{25,9},{2,18},{10... | collective-permute-start | bytes 393224 | tf_op jit(solution)/shard_map/ppermute | solution.py:50
  51.6 0.1 collective-permute-start.2
  51.7 2.6 %collective-permute-start.1 = (f32[128,256]{1,0:T(8,128)S(1)}, f32[128,256]{1,0:T(8,128)S(1)}, u32[]{:S(2)}, u32[]{:S(2)}) collective-permute-start(f32[128,256]{1,0:T(8,128)S(1)} %get-tuple-element.17), channel_id=1, source_target_pairs={{0,24},{8,0},{16,8},{24,16},{1,25},{9,1},{17,9},{25,17},{2,26},{10... | collective-permute-start | bytes 393224 | tf_op jit(solution)/shard_map/ppermute | solution.py:50
  54.3 0.3 collective-permute-done.3
  54.5 3.5 %collective-permute-done.2 = f32[128,256]{1,0:T(8,128)S(1)} collective-permute-done((f32[128,256]{1,0:T(8,128)S(1)}, f32[128,256]{1,0:T(8,128)S(1)}, u32[]{:S(2)}, u32[]{:S(2)}) %collective-permute-start.2) | collective-permute-done | bytes 131104 | tf_op jit(solution)/shard_map/ppermute | solution.py:50
  58.1 0.0 collective-permute-done.1
  58.1 2.6 %collective-permute-start.6 = (f32[128,256]{1,0:T(8,128)S(1)}, f32[128,256]{1,0:T(8,128)S(1)}, u32[]{:S(2)}, u32[]{:S(2)}) collective-permute-start(f32[128,256]{1,0:T(8,128)S(1)} %add_add_fusion.1), channel_id=1, source_target_pairs={{0,3},{1,0},{2,1},{3,2},{4,7},{5,4},{6,5},{7,6},{8,11},{9,8},{10,9... | collective-permute-start | bytes 393224 | tf_op jit(solution)/shard_map/ppermute | solution.py:50
  60.7 0.0 collective-permute-start.4
  60.7 1.7 collective-permute-start.5
  62.4 0.2 collective-permute-done.6
  62.6 5.2 %collective-permute-done.4 = f32[128,256]{1,0:T(8,128)S(1)} collective-permute-done((f32[128,256]{1,0:T(8,128)S(1)}, f32[128,256]{1,0:T(8,128)S(1)}, u32[]{:S(2)}, u32[]{:S(2)}) %collective-permute-start.4) | collective-permute-done | bytes 131104 | tf_op jit(solution)/shard_map/ppermute | solution.py:50
  67.9 1.9 %collective-permute-start.7 = (f32[128,256]{1,0:T(8,128)S(1)}, f32[128,256]{1,0:T(8,128)S(1)}, u32[]{:S(2)}, u32[]{:S(2)}) collective-permute-start(f32[128,256]{1,0:T(8,128)S(1)} %add_add_fusion.p0), channel_id=1, source_target_pairs={{0,8},{8,16},{16,24},{24,0},{1,9},{9,17},{17,25},{25,1},{2,10},{10... | collective-permute-start | bytes 393224 | tf_op jit(solution)/shard_map/ppermute | solution.py:50
  69.8 1.6 collective-permute-start.8
  71.3 0.9 collective-permute-start.9
  72.3 0.7 collective-permute-done.7.p1
  73.0 2.1 %collective-permute-done.8.p2 = f32[128,256]{1,0:T(8,128)S(1)} collective-permute-done((f32[128,256]{1,0:T(8,128)S(1)}, f32[128,256]{1,0:T(8,128)S(1)}, u32[]{:S(2)}, u32[]{:S(2)}) %collective-permute-start.8) | collective-permute-done | bytes 131104 | tf_op jit(solution)/shard_map/ppermute | solution.py:50
  75.1 0.3 collective-permute-done.9.p3
  75.5 3.5 %shard_map.69 = (f32[8,104,256]{2,1,0:T(8,128)S(1)}, f32[8,104,256]{2,1,0:T(8,128)S(1)}) custom-call(s32[3]{0:T(128)S(1)} %pad_add_fusion.pos, f32[4,8,176,128]{3,2,1,0:T(8,128)S(1)} %all-to-all-done.strips, f32[128,256]{1,0:T(8,128)S(1)} %add_add_fusion.p0, f32[128,256]{1,0:T(8,128)S(1)} %collective-permute-done.7.p1, ...), custom_call_target="tpu_custom_call" | custom-call | flops 1107296256 | bytes 4325376 | tf_op jit(solution)/shard_map/pallas_call | solution.py:169
  79.0 4.3 %collective-permute-start.10 = (f32[8,104,256]{2,1,0:T(8,128)S(1)}, f32[8,104,256]{2,1,0:T(8,128)S(1)}, u32[]{:S(2)}, u32[]{:S(2)}) collective-permute-start(f32[8,104,256]{2,1,0:T(8,128)S(1)} %get-tuple-element.21), channel_id=1, source_target_pairs={{0,4},{4,0},{1,5},{5,1},{2,6},{6,2},{3,7},{7,3},{8,12},{12,8},{9,1... | collective-permute-start | bytes 2555912 | tf_op jit(solution)/shard_map/ppermute | solution.py:46
  83.3 2.0 %collective-permute-done.10 = f32[8,104,256]{2,1,0:T(8,128)S(1)} collective-permute-done((f32[8,104,256]{2,1,0:T(8,128)S(1)}, f32[8,104,256]{2,1,0:T(8,128)S(1)}, u32[]{:S(2)}, u32[]{:S(2)}) %collective-permute-start.10) | collective-permute-done | bytes 852000 | tf_op jit(solution)/shard_map/ppermute | solution.py:46
  85.3 0.1 add.52
  85.4 29.6 %all_to_all.20 = f32[8,104,256]{2,1,0:T(8,128)S(1)} all-to-all(f32[8,104,256]{2,1,0:T(8,128)S(1)} %add.52), channel_id=1, replica_groups=mesh['z'=8,'y'=4,'c'=2,'x'=4] {'z'}, dimensions={0} | all-to-all | bytes 1703936 | tf_op jit(solution)/shard_map/all_to_all | solution.py:42
  115.0 0.1 reduce_sum.29
  115.0 2.3 %collective-permute-start.13 = (f32[16,256]{1,0:T(8,128)S(1)}, f32[16,256]{1,0:T(8,128)S(1)}, u32[]{:S(2)}, u32[]{:S(2)}) collective-permute-start(f32[16,256]{1,0:T(8,128)S(1)} %get-tuple-element.30), channel_id=1, source_target_pairs={{0,24},{8,0},{16,8},{24,16},{1,25},{9,1},{17,9},{25,17},{2,26},{10... | collective-permute-start | bytes 49160 | tf_op jit(solution)/shard_map/ppermute | solution.py:50
  117.3 0.0 collective-permute-start.12
  117.3 0.9 collective-permute-start.11
  118.2 0.9 broadcast_in_dim.8
  119.1 3.5 %all-to-all-start.2 = ((f32[8,88,256]{2,1,0:T(8,128)}), f32[8,88,256]{2,1,0:T(8,128)S(1)}, u32[]{:S(2)}, u32[]{:S(2)}) async-start(f32[8,88,256]{2,1,0:T(8,128)} %broadcast_in_dim.8), calls=%async_computation.2 | async-start | bytes 1441792 | tf_op jit(solution)/shard_map/all_to_all | solution.py:38
  122.7 0.1 collective-permute-start.14
  122.8 2.6 %collective-permute-start.15 = (f32[4,16,256]{2,1,0:T(8,128)S(1)}, f32[4,16,256]{2,1,0:T(8,128)S(1)}, u32[]{:S(2)}, u32[]{:S(2)}) collective-permute-start(f32[4,16,256]{2,1,0:T(8,128)S(1)} %pad_maximum_fusion.2), channel_id=1, source_target_pairs={{0,2},{1,3},{2,0},{3,1},{4,6},{5,7},{6,4},{7,5},{8,10},{9,11},{10,... | collective-permute-start | bytes 196616 | tf_op jit(solution)/shard_map/ppermute | solution.py:50
  125.4 0.2 collective-permute-start.16
  125.6 1.5 collective-permute-done.14
  127.1 0.7 collective-permute-done.15
  127.8 1.0 collective-permute-done.16
  129.0 0.1 pad_maximum_fusion
  129.1 10.4 %shard_map.70 = f32[256,256]{1,0:T(8,128)S(1)} custom-call(f32[256,256]{1,0:T(8,128)S(1)} %bitcast.52), custom_call_target="tpu_custom_call" | custom-call | flops 10000000000 | bytes 1000000 | tf_op jit(solution)/shard_map/pallas_call | solution.py:263
  139.5 3.6 %all-to-all-done.2 = f32[8,88,256]{2,1,0:T(8,128)S(1)} async-done(((f32[8,88,256]{2,1,0:T(8,128)}), f32[8,88,256]{2,1,0:T(8,128)S(1)}, u32[]{:S(2)}, u32[]{:S(2)}) %all-to-all-start.2) | async-done | bytes 720928 | tf_op jit(solution)/shard_map/all_to_all | solution.py:38
  143.0 0.5 multiply_reduce_fusion
  143.5 1.3 collective-permute-start.18
  144.9 1.4 collective-permute-start.19
  146.3 2.8 %collective-permute-start.17 = (f32[1,256]{1,0:T(1,128)S(1)}, f32[1,256]{1,0:T(1,128)S(1)}, u32[]{:S(2)}, u32[]{:S(2)}) collective-permute-start(f32[1,256]{1,0:T(1,128)S(1)} %bitcast.65), channel_id=1, source_target_pairs={{0,4},{4,0},{1,5},{5,1},{2,6},{6,2},{3,7},{7,3},{8,12},{12,8},{9,1... | collective-permute-start | bytes 3080 | tf_op jit(solution)/shard_map/ppermute | solution.py:46
  149.1 0.8 collective-permute-done.17
  149.9 10.5 %all_to_all.21 = f32[16,1,256]{2,1,0:T(1,128)S(1)} all-to-all(f32[16,1,256]{2,1,0:T(1,128)S(1)} %broadcast_in_dim.20), channel_id=1, replica_groups=mesh['z'=8,'y'=4,'c'=2,'x'=4] {'y','x'}, dimensions={0} | all-to-all | bytes 32768 | tf_op jit(solution)/shard_map/all_to_all | solution.py:38
  160.5 0.8 slice.14
  161.2 0.6 collective-permute-start.20
  161.8 0.8 slice.15
  162.6 2.1 %collective-permute-start.21 = (f32[4,88,256]{2,1,0:T(8,128)}, f32[4,88,256]{2,1,0:T(8,128)S(1)}, u32[]{:S(2)}, u32[]{:S(2)}) collective-permute-start(f32[4,88,256]{2,1,0:T(8,128)} %slice.15), channel_id=1, source_target_pairs={{0,24},{8,0},{16,8},{24,16},{1,25},{9,1},{17,9},{25,17},{2,26},{10... | collective-permute-start | bytes 1081352 | tf_op jit(solution)/shard_map/ppermute | solution.py:50
  164.7 3.9 %collective-permute-start.22 = (f32[8,88,256]{2,1,0:T(8,128)S(1)}, f32[8,88,256]{2,1,0:T(8,128)S(1)}, u32[]{:S(2)}, u32[]{:S(2)}) collective-permute-start(f32[8,88,256]{2,1,0:T(8,128)S(1)} %bitcast.49), channel_id=1, source_target_pairs={{0,4},{4,0},{1,5},{5,1},{2,6},{6,2},{3,7},{7,3},{8,12},{12,8},{9,1... | collective-permute-start | bytes 2162696 | tf_op jit(solution)/shard_map/ppermute | solution.py:46
  168.5 0.5 collective-permute-start.24
  169.1 0.2 collective-permute-done.20.refs_3_
  169.2 4.2 %collective-permute-start.25 = (f32[4,88,256]{2,1,0:T(8,128)S(1)}, f32[4,88,256]{2,1,0:T(8,128)S(1)}, u32[]{:S(2)}, u32[]{:S(2)}) collective-permute-start(f32[4,88,256]{2,1,0:T(8,128)S(1)} %collective-permute-done.20.refs_3_), channel_id=1, source_target_pairs={{0,4},{4,0},{1,5},{5,1},{2,6},{6,2},{3,7},{7,3},{8,12},{12,8},{9,1... | collective-permute-start | bytes 1081352 | tf_op jit(solution)/shard_map/ppermute | solution.py:46
  173.5 0.6 collective-permute-start.26
  174.1 0.4 broadcast_multiply_fusion
  174.5 0.7 bitcast_multiply_fusion
  175.2 0.2 collective-permute-done.26.refs_9_
  175.4 7.6 %shard_map.71 = (f32[128,5632]{1,0:T(8,128)}, f32[128,5632]{1,0:T(8,128)}) custom-call(s32[3]{0:T(128)S(1)} %pad_add_fusion.pos, f32[256,256]{1,0:T(8,128)S(1)} %pad_maximum_fusion.1.left, bf16[128,5632]{1,0:T(8,128)(2,1)} %grad.3, f32[128,5632]{1,0:T(8,128)} %mom.3, f32[128,5632]{1,0:T(8,128)} %wgt.1, f32[8,88,256]{2,1,0:T(8,128)S(1)} %bitcast.51, ...), custom_call_target="tpu_custom_call" | custom-call | flops 2214592512 | bytes 12976128 | tf_op jit(solution)/shard_map/pallas_call | solution.py:318
  (36 shorter events, 0.4 us)
Async XLA Ops:
  5.4 5.1 %copy-start = (f32[88,256]{1,0:T(8,128)S(1)}, f32[88,256]{1,0:T(8,128)}, u32[]{:S(2)}) copy-start(f32[88,256]{1,0:T(8,128)} %param.7) | copy-start | bytes 270340
  5.4 39.8 %all-to-all-start = ((f32[4,8,176,128]{3,2,1,0:T(8,128)}), f32[4,8,176,128]{3,2,1,0:T(8,128)S(1)}, u32[]{:S(2)}, u32[]{:S(2)}) async-start(f32[4,8,176,128]{3,2,1,0:T(8,128)} %shard_map.67), calls=%async_computation | async-start | bytes 5767168 | tf_op jit(solution)/shard_map/all_to_all | solution.py:337
  37.6 7.6 %collective-permute-start = (f32[8,88,256]{2,1,0:T(8,128)}, f32[8,88,256]{2,1,0:T(8,128)}, u32[]{:S(2)}, u32[]{:S(2)}) collective-permute-start(f32[8,88,256]{2,1,0:T(8,128)} %bitcast.4.mine), channel_id=1, source_target_pairs={{0,4},{4,0},{1,5},{5,1},{2,6},{6,2},{3,7},{7,3},{8,12},{12,8},{9,1... | collective-permute-start | bytes 2162696 | tf_op jit(solution)/shard_map/ppermute | solution.py:46
  48.1 6.4 %collective-permute-start.3 = (f32[128,256]{1,0:T(8,128)S(1)}, f32[128,256]{1,0:T(8,128)S(1)}, u32[]{:S(2)}, u32[]{:S(2)}) collective-permute-start(f32[128,256]{1,0:T(8,128)S(1)} %get-tuple-element.19), channel_id=1, source_target_pairs={{0,16},{8,24},{16,0},{24,8},{1,17},{9,25},{17,1},{25,9},{2,18},{10... | collective-permute-start | bytes 393224 | tf_op jit(solution)/shard_map/ppermute | solution.py:50
  51.6 6.5 %collective-permute-start.2 = (f32[128,256]{1,0:T(8,128)S(1)}, f32[128,256]{1,0:T(8,128)S(1)}, u32[]{:S(2)}, u32[]{:S(2)}) collective-permute-start(f32[128,256]{1,0:T(8,128)S(1)} %get-tuple-element.18), channel_id=1, source_target_pairs={{0,8},{8,16},{16,24},{24,0},{1,9},{9,17},{17,25},{25,1},{2,10},{10... | collective-permute-start | bytes 393224 | tf_op jit(solution)/shard_map/ppermute | solution.py:50
  51.7 6.4 %collective-permute-start.1 = (f32[128,256]{1,0:T(8,128)S(1)}, f32[128,256]{1,0:T(8,128)S(1)}, u32[]{:S(2)}, u32[]{:S(2)}) collective-permute-start(f32[128,256]{1,0:T(8,128)S(1)} %get-tuple-element.17), channel_id=1, source_target_pairs={{0,24},{8,0},{16,8},{24,16},{1,25},{9,1},{17,9},{25,17},{2,26},{10... | collective-permute-start | bytes 393224 | tf_op jit(solution)/shard_map/ppermute | solution.py:50
  58.1 4.5 %collective-permute-start.6 = (f32[128,256]{1,0:T(8,128)S(1)}, f32[128,256]{1,0:T(8,128)S(1)}, u32[]{:S(2)}, u32[]{:S(2)}) collective-permute-start(f32[128,256]{1,0:T(8,128)S(1)} %add_add_fusion.1), channel_id=1, source_target_pairs={{0,3},{1,0},{2,1},{3,2},{4,7},{5,4},{6,5},{7,6},{8,11},{9,8},{10,9... | collective-permute-start | bytes 393224 | tf_op jit(solution)/shard_map/ppermute | solution.py:50
  60.7 7.2 %collective-permute-start.4 = (f32[128,256]{1,0:T(8,128)S(1)}, f32[128,256]{1,0:T(8,128)S(1)}, u32[]{:S(2)}, u32[]{:S(2)}) collective-permute-start(f32[128,256]{1,0:T(8,128)S(1)} %add_add_fusion.1), channel_id=1, source_target_pairs={{0,1},{1,2},{2,3},{3,0},{4,5},{5,6},{6,7},{7,4},{8,9},{9,10},{10,1... | collective-permute-start | bytes 393224 | tf_op jit(solution)/shard_map/ppermute | solution.py:50
  60.7 7.2 %collective-permute-start.5 = (f32[128,256]{1,0:T(8,128)S(1)}, f32[128,256]{1,0:T(8,128)S(1)}, u32[]{:S(2)}, u32[]{:S(2)}) collective-permute-start(f32[128,256]{1,0:T(8,128)S(1)} %add_add_fusion.1), channel_id=1, source_target_pairs={{0,2},{1,3},{2,0},{3,1},{4,6},{5,7},{6,4},{7,5},{8,10},{9,11},{10,... | collective-permute-start | bytes 393224 | tf_op jit(solution)/shard_map/ppermute | solution.py:50
  67.9 5.1 %collective-permute-start.7 = (f32[128,256]{1,0:T(8,128)S(1)}, f32[128,256]{1,0:T(8,128)S(1)}, u32[]{:S(2)}, u32[]{:S(2)}) collective-permute-start(f32[128,256]{1,0:T(8,128)S(1)} %add_add_fusion.p0), channel_id=1, source_target_pairs={{0,8},{8,16},{16,24},{24,0},{1,9},{9,17},{17,25},{25,1},{2,10},{10... | collective-permute-start | bytes 393224 | tf_op jit(solution)/shard_map/ppermute | solution.py:50
  69.8 5.3 %collective-permute-start.8 = (f32[128,256]{1,0:T(8,128)S(1)}, f32[128,256]{1,0:T(8,128)S(1)}, u32[]{:S(2)}, u32[]{:S(2)}) collective-permute-start(f32[128,256]{1,0:T(8,128)S(1)} %add_add_fusion.p0), channel_id=1, source_target_pairs={{0,16},{8,24},{16,0},{24,8},{1,17},{9,25},{17,1},{25,9},{2,18},{10... | collective-permute-start | bytes 393224 | tf_op jit(solution)/shard_map/ppermute | solution.py:50
  71.3 4.1 %collective-permute-start.9 = (f32[128,256]{1,0:T(8,128)S(1)}, f32[128,256]{1,0:T(8,128)S(1)}, u32[]{:S(2)}, u32[]{:S(2)}) collective-permute-start(f32[128,256]{1,0:T(8,128)S(1)} %add_add_fusion.p0), channel_id=1, source_target_pairs={{0,24},{8,0},{16,8},{24,16},{1,25},{9,1},{17,9},{25,17},{2,26},{10... | collective-permute-start | bytes 393224 | tf_op jit(solution)/shard_map/ppermute | solution.py:50
  79.0 6.3 %collective-permute-start.10 = (f32[8,104,256]{2,1,0:T(8,128)S(1)}, f32[8,104,256]{2,1,0:T(8,128)S(1)}, u32[]{:S(2)}, u32[]{:S(2)}) collective-permute-start(f32[8,104,256]{2,1,0:T(8,128)S(1)} %get-tuple-element.21), channel_id=1, source_target_pairs={{0,4},{4,0},{1,5},{5,1},{2,6},{6,2},{3,7},{7,3},{8,12},{12,8},{9,1... | collective-permute-start | bytes 2555912 | tf_op jit(solution)/shard_map/ppermute | solution.py:46
  115.0 7.6 %collective-permute-start.13 = (f32[16,256]{1,0:T(8,128)S(1)}, f32[16,256]{1,0:T(8,128)S(1)}, u32[]{:S(2)}, u32[]{:S(2)}) collective-permute-start(f32[16,256]{1,0:T(8,128)S(1)} %get-tuple-element.30), channel_id=1, source_target_pairs={{0,24},{8,0},{16,8},{24,16},{1,25},{9,1},{17,9},{25,17},{2,26},{10... | collective-permute-start | bytes 49160 | tf_op jit(solution)/shard_map/ppermute | solution.py:50
  117.3 5.3 %collective-permute-start.12 = (f32[16,256]{1,0:T(8,128)S(1)}, f32[16,256]{1,0:T(8,128)S(1)}, u32[]{:S(2)}, u32[]{:S(2)}) collective-permute-start(f32[16,256]{1,0:T(8,128)S(1)} %get-tuple-element.30), channel_id=1, source_target_pairs={{0,16},{8,24},{16,0},{24,8},{1,17},{9,25},{17,1},{25,9},{2,18},{10... | collective-permute-start | bytes 49160 | tf_op jit(solution)/shard_map/ppermute | solution.py:50
  117.3 5.3 %collective-permute-start.11 = (f32[16,256]{1,0:T(8,128)S(1)}, f32[16,256]{1,0:T(8,128)S(1)}, u32[]{:S(2)}, u32[]{:S(2)}) collective-permute-start(f32[16,256]{1,0:T(8,128)S(1)} %get-tuple-element.30), channel_id=1, source_target_pairs={{0,8},{8,16},{16,24},{24,0},{1,9},{9,17},{17,25},{25,1},{2,10},{10... | collective-permute-start | bytes 49160 | tf_op jit(solution)/shard_map/ppermute | solution.py:50
  119.1 23.9 %all-to-all-start.2 = ((f32[8,88,256]{2,1,0:T(8,128)}), f32[8,88,256]{2,1,0:T(8,128)S(1)}, u32[]{:S(2)}, u32[]{:S(2)}) async-start(f32[8,88,256]{2,1,0:T(8,128)} %broadcast_in_dim.8), calls=%async_computation.2 | async-start | bytes 1441792 | tf_op jit(solution)/shard_map/all_to_all | solution.py:38
  122.7 4.4 %collective-permute-start.14 = (f32[4,16,256]{2,1,0:T(8,128)S(1)}, f32[4,16,256]{2,1,0:T(8,128)S(1)}, u32[]{:S(2)}, u32[]{:S(2)}) collective-permute-start(f32[4,16,256]{2,1,0:T(8,128)S(1)} %pad_maximum_fusion.2), channel_id=1, source_target_pairs={{0,1},{1,2},{2,3},{3,0},{4,5},{5,6},{6,7},{7,4},{8,9},{9,10},{10,1... | collective-permute-start | bytes 196616 | tf_op jit(solution)/shard_map/ppermute | solution.py:50
  122.8 5.0 %collective-permute-start.15 = (f32[4,16,256]{2,1,0:T(8,128)S(1)}, f32[4,16,256]{2,1,0:T(8,128)S(1)}, u32[]{:S(2)}, u32[]{:S(2)}) collective-permute-start(f32[4,16,256]{2,1,0:T(8,128)S(1)} %pad_maximum_fusion.2), channel_id=1, source_target_pairs={{0,2},{1,3},{2,0},{3,1},{4,6},{5,7},{6,4},{7,5},{8,10},{9,11},{10,... | collective-permute-start | bytes 196616 | tf_op jit(solution)/shard_map/ppermute | solution.py:50
  125.4 3.4 %collective-permute-start.16 = (f32[4,16,256]{2,1,0:T(8,128)S(1)}, f32[4,16,256]{2,1,0:T(8,128)S(1)}, u32[]{:S(2)}, u32[]{:S(2)}) collective-permute-start(f32[4,16,256]{2,1,0:T(8,128)S(1)} %pad_maximum_fusion.2), channel_id=1, source_target_pairs={{0,3},{1,0},{2,1},{3,2},{4,7},{5,4},{6,5},{7,6},{8,11},{9,8},{10,9... | collective-permute-start | bytes 196616 | tf_op jit(solution)/shard_map/ppermute | solution.py:50
  143.5 16.9 %collective-permute-start.18 = (f32[8,88,256]{2,1,0:T(8,128)S(1)}, f32[8,88,256]{2,1,0:T(8,128)S(1)}, u32[]{:S(2)}, u32[]{:S(2)}) collective-permute-start(f32[8,88,256]{2,1,0:T(8,128)S(1)} %bitcast.47), channel_id=1, source_target_pairs={{0,8},{8,16},{16,24},{24,0},{1,9},{9,17},{17,25},{25,1},{2,10},{10... | collective-permute-start | bytes 2162696 | tf_op jit(solution)/shard_map/ppermute | solution.py:50
  144.9 15.6 %collective-permute-start.19 = (f32[8,88,256]{2,1,0:T(8,128)S(1)}, f32[8,88,256]{2,1,0:T(8,128)S(1)}, u32[]{:S(2)}, u32[]{:S(2)}) collective-permute-start(f32[8,88,256]{2,1,0:T(8,128)S(1)} %bitcast.48), channel_id=1, source_target_pairs={{0,24},{8,0},{16,8},{24,16},{1,25},{9,1},{17,9},{25,17},{2,26},{10... | collective-permute-start | bytes 2162696 | tf_op jit(solution)/shard_map/ppermute | solution.py:50
  146.3 3.6 %collective-permute-start.17 = (f32[1,256]{1,0:T(1,128)S(1)}, f32[1,256]{1,0:T(1,128)S(1)}, u32[]{:S(2)}, u32[]{:S(2)}) collective-permute-start(f32[1,256]{1,0:T(1,128)S(1)} %bitcast.65), channel_id=1, source_target_pairs={{0,4},{4,0},{1,5},{5,1},{2,6},{6,2},{3,7},{7,3},{8,12},{12,8},{9,1... | collective-permute-start | bytes 3080 | tf_op jit(solution)/shard_map/ppermute | solution.py:46
  161.2 8.0 %collective-permute-start.20 = (f32[4,88,256]{2,1,0:T(8,128)}, f32[4,88,256]{2,1,0:T(8,128)S(1)}, u32[]{:S(2)}, u32[]{:S(2)}) collective-permute-start(f32[4,88,256]{2,1,0:T(8,128)} %slice.14), channel_id=1, source_target_pairs={{0,8},{8,16},{16,24},{24,0},{1,9},{9,17},{17,25},{25,1},{2,10},{10... | collective-permute-start | bytes 1081352 | tf_op jit(solution)/shard_map/ppermute | solution.py:50
  162.6 10.9 %collective-permute-start.21 = (f32[4,88,256]{2,1,0:T(8,128)}, f32[4,88,256]{2,1,0:T(8,128)S(1)}, u32[]{:S(2)}, u32[]{:S(2)}) collective-permute-start(f32[4,88,256]{2,1,0:T(8,128)} %slice.15), channel_id=1, source_target_pairs={{0,24},{8,0},{16,8},{24,16},{1,25},{9,1},{17,9},{25,17},{2,26},{10... | collective-permute-start | bytes 1081352 | tf_op jit(solution)/shard_map/ppermute | solution.py:50
  164.7 10.5 %collective-permute-start.22 = (f32[8,88,256]{2,1,0:T(8,128)S(1)}, f32[8,88,256]{2,1,0:T(8,128)S(1)}, u32[]{:S(2)}, u32[]{:S(2)}) collective-permute-start(f32[8,88,256]{2,1,0:T(8,128)S(1)} %bitcast.49), channel_id=1, source_target_pairs={{0,4},{4,0},{1,5},{5,1},{2,6},{6,2},{3,7},{7,3},{8,12},{12,8},{9,1... | collective-permute-start | bytes 2162696 | tf_op jit(solution)/shard_map/ppermute | solution.py:46
  168.5 6.8 %collective-permute-start.23 = (f32[8,88,256]{2,1,0:T(8,128)S(1)}, f32[8,88,256]{2,1,0:T(8,128)S(1)}, u32[]{:S(2)}, u32[]{:S(2)}) collective-permute-start(f32[8,88,256]{2,1,0:T(8,128)S(1)} %collective-permute-done.18.refs_1_), channel_id=1, source_target_pairs={{0,4},{4,0},{1,5},{5,1},{2,6},{6,2},{3,7},{7,3},{8,12},{12,8},{9,1... | collective-permute-start | bytes 2162696 | tf_op jit(solution)/shard_map/ppermute | solution.py:46
  168.5 6.8 %collective-permute-start.24 = (f32[8,88,256]{2,1,0:T(8,128)S(1)}, f32[8,88,256]{2,1,0:T(8,128)S(1)}, u32[]{:S(2)}, u32[]{:S(2)}) collective-permute-start(f32[8,88,256]{2,1,0:T(8,128)S(1)} %collective-permute-done.19.refs_2_), channel_id=1, source_target_pairs={{0,4},{4,0},{1,5},{5,1},{2,6},{6,2},{3,7},{7,3},{8,12},{12,8},{9,1... | collective-permute-start | bytes 2162696 | tf_op jit(solution)/shard_map/ppermute | solution.py:46
  169.2 5.9 %collective-permute-start.25 = (f32[4,88,256]{2,1,0:T(8,128)S(1)}, f32[4,88,256]{2,1,0:T(8,128)S(1)}, u32[]{:S(2)}, u32[]{:S(2)}) collective-permute-start(f32[4,88,256]{2,1,0:T(8,128)S(1)} %collective-permute-done.20.refs_3_), channel_id=1, source_target_pairs={{0,4},{4,0},{1,5},{5,1},{2,6},{6,2},{3,7},{7,3},{8,12},{12,8},{9,1... | collective-permute-start | bytes 1081352 | tf_op jit(solution)/shard_map/ppermute | solution.py:46
  173.5 1.9 %collective-permute-start.26 = (f32[4,88,256]{2,1,0:T(8,128)S(1)}, f32[4,88,256]{2,1,0:T(8,128)S(1)}, u32[]{:S(2)}, u32[]{:S(2)}) collective-permute-start(f32[4,88,256]{2,1,0:T(8,128)S(1)} %collective-permute-done.21.refs_4_), channel_id=1, source_target_pairs={{0,4},{4,0},{1,5},{5,1},{2,6},{6,2},{3,7},{7,3},{8,12},{12,8},{9,1... | collective-permute-start | bytes 1081352 | tf_op jit(solution)/shard_map/ppermute | solution.py:46

commit v3 on v2

--- a/solution.py
+++ b/solution.py
@@ -92,14 +92,15 @@
 
 def split_columns(gradient, momentum):
     rows, cols = momentum.shape
-    wide = 2 * cols // NZ
-    size = wide // (2 * NY)
+    steps = 2
+    wide = cols // steps
+    size = cols // (NZ * NY)
     block = pl.BlockSpec((rows, wide), lambda i: (0, i))
     return pl.pallas_call(
         split_kernel,
-        grid=(NZ // 2,),
+        grid=(steps,),
         in_specs=[block, block],
-        out_specs=pl.BlockSpec((NY, 2, size, rows), lambda i: (0, i, 0, 0)),
+        out_specs=pl.BlockSpec((NY, NZ // steps, size, rows), lambda i: (0, i, 0, 0)),
         out_shape=jax.ShapeDtypeStruct((NY, NZ, size, rows), jnp.float32),
         scratch_shapes=[pltpu.VMEM((wide, rows), jnp.float32)],
         compiler_params=params(60),
@@ -267,37 +268,42 @@
         out_shape=jax.ShapeDtypeStruct((RANK, RANK), jnp.float32),
         scratch_shapes=[pltpu.VMEM((RANK, RANK), jnp.float32)] * 2,
         compiler_params=params(16),
-        cost_estimate=cost(10_000_000_000, 1_000_000),
+        cost_estimate=cost(100_000_000, 1_000_000),
     )(gram)
 
 
 def update_kernel(pos, left, grad, mom, wgt, *refs):
-    mine, other = refs[0:5], refs[5:10]
-    new_mom, new_wgt, full = refs[10:]
+    new_mom, new_wgt, full, high, low = refs[10:]
     y, core, i = pos[0], pos[1], pl.program_id(0)
-    half = mine[0].shape[1]
-
-    def place(ref, d, first):
+    half = refs[0].shape[1]
+    near = NZ // 2
+
+    @pl.when(i == 0)
+    def _():
+        high[...], low[...] = halves(left[...])
+
+    def place(ref, z, part, d, first):
         owner = lax.rem(y + NY - d, NY)
+        start = ((part * NY + owner) * 2 + first) * half
+        full[pl.ds(pl.multiple_of(start, 8), half), :] = ref[z]
+
+    for group, first in ((refs[:5], core), (refs[5:10], 1 - core)):
         for part in range(2):
-            start = ((part * NY + owner) * 2 + first) * half
-            full[pl.ds(pl.multiple_of(start, 8), half), :] = ref[part]
-
-    for group, first in ((mine, core), (other, 1 - core)):
-        place(group[0], 0, first)
-        place(group[1], 1, first)
-        place(group[2], 3, first)
-
-        @pl.when(i < 2)
-        def _():
-            place(group[3], 2, first)
-
-        @pl.when(i >= 2)
-        def _():
-            place(group[4], 2, first)
+            z = 2 * i + part
+            place(group[0], z, part, 0, first)
+            place(group[1], z, part, 1, first)
+            place(group[2], z, part, 3, first)
+
+            @pl.when(z < near)
+            def _():
+                place(group[3], jnp.minimum(z, near - 1), part, 2, first)
+
+            @pl.when(z >= near)
+            def _():
+                place(group[4], jnp.maximum(z - near, 0), part, 2, first)
 
     rows = mom.shape[0]
-    both = dot_halves(halves(left[...]), halves(full[...]), 1, 1)
+    both = dot_halves((high[...], low[...]), halves(full[...]), 1, 1)
     coeff = step_rate * math.sqrt(D / RANK) / math.sqrt(FF)
     keep = 1.0 - step_rate * weight_decay
     summed = mom[...] + grad[...].astype(jnp.float32)
@@ -308,20 +314,19 @@
 def update(pos, left, gradient, momentum, weight, mine, other):
     rows, cols = momentum.shape
     wide = 2 * cols // NZ
-    half = mine[0].shape[1]
     block = pl.BlockSpec((rows, wide), lambda i: (0, i))
-    piece = pl.BlockSpec((2, half, RANK), lambda i: (i, 0, 0))
-    early = pl.BlockSpec((2, half, RANK), lambda i: (jnp.minimum(i, 1), 0, 0))
-    late = pl.BlockSpec((2, half, RANK), lambda i: (jnp.maximum(i - 2, 0), 0, 0))
-    pieces = [piece] * 3 + [early, late]
-    whole = pl.BlockSpec(left.shape, lambda i: (0, 0))
+    whole = pl.BlockSpec(memory_space=pltpu.VMEM)
     return pl.pallas_call(
         update_kernel,
         grid=(NZ // 2,),
-        in_specs=[smem(), whole, block, block, block] + pieces + pieces,
+        in_specs=[smem(), whole, block, block, block] + [whole] * 10,
         out_specs=[block, block],
         out_shape=[jax.ShapeDtypeStruct(momentum.shape, jnp.float32)] * 2,
-        scratch_shapes=[pltpu.VMEM((wide, RANK), jnp.float32)],
+        scratch_shapes=[
+            pltpu.VMEM((wide, RANK), jnp.float32),
+            pltpu.VMEM(left.shape, jnp.bfloat16),
+            pltpu.VMEM(left.shape, jnp.bfloat16),
+        ],
         compiler_params=params(48),
         cost_estimate=cost(12 * rows * cols * RANK, rows * cols * 18),
     )(pos, left, gradient, momentum, weight, *mine, *other)

time: 183 us -> 182 us (level)
  no operation moved by 1% of the time
where the time goes in v3:
time: 182 us
  blocking collectives  67.2 us (37%)
  starting transfers between devices  56.6 us (31%)
  Pallas kernels  28.2 us (15%)
  waiting for transfers between devices  24.6 us (14%)
  local copies, waits for them, and re-layouts  2.62 us (1%)
    all_to_all x1, blocking collectives, scatter_sum(): return jnp.sum(lax.all_to_all(blocks, axes, 0, 0), axis=0)  29.6 us
    all_gather x1, blocking collectives, body(): basis_z = lax.all_gather(basis, 'z', axis=0)  27.1 us
    ppermute x19, starting transfers between devices, shift(): lax.ppermute(block, axis, [(i, (i + step) % size) for i in range(size)])  26.3 us
    ppermute x8, starting transfers between devices, swap(): return lax.ppermute(block, 'c', [(0, 1), (1, 0)])  21.6 us
    ppermute x19, waiting for transfers between devices, shift(): lax.ppermute(block, axis, [(i, (i + step) % size) for i in range(size)])  15.8 us
    all_to_all x1, blocking collectives, gather(): return lax.all_to_all(copies, axes, 0, 0)  10.5 us
    pallas_call x1, Pallas kernels, factor_inverse(): pl.pallas_call(inverse_kernel, in_specs=[pl.BlockSpec(memory_space=pltpu....  10.4 us
    pallas_call x1, Pallas kernels, update(): pl.pallas_call(update_kernel, grid=(NZ // 2,), in_specs=[smem(), whole, b...  7.64 us
  transfers between devices with their start and end apart: 29, of which 16 were waited for; matrix products, arithmetic and copies ran while one was open for 2% of the time, Pallas kernels for 6%

profile of v3, /device:TPU:1, one launch (start us, length us, event | category | flops | bytes accessed | tf_op | source)
XLA Modules:
  0.0 182.0 jit_solution(6207057291559586720)
XLA Ops:
  0.6 3.8 %shard_map.67 = f32[4,8,176,128]{3,2,1,0:T(8,128)} custom-call(bf16[128,5632]{1,0:T(8,128)(2,1)} %grad.3, f32[128,5632]{1,0:T(8,128)} %mom.3), custom_call_target="tpu_custom_call" | custom-call | bytes 7208960 | tf_op jit(solution)/shard_map/pallas_call | solution.py:99
  4.4 5.1 %all-to-all-start = ((f32[4,8,176,128]{3,2,1,0:T(8,128)}), f32[4,8,176,128]{3,2,1,0:T(8,128)S(1)}, u32[]{:S(2)}, u32[]{:S(2)}) async-start(f32[4,8,176,128]{3,2,1,0:T(8,128)} %shard_map.67), calls=%async_computation | async-start | bytes 5767168 | tf_op jit(solution)/shard_map/all_to_all | solution.py:342
  9.6 27.1 %all-gather = f32[704,256]{1,0:T(8,128)} all-gather(f32[88,256]{1,0:T(8,128)S(1)} %copy-done), channel_id=2, replica_groups=mesh['z'=8,'y'=4,'c'=2,'x'=4] {'z'}, dimensions={0}, use_global_device_ids=true | all-gather | bytes 811008 | tf_op jit(solution)/shard_map/all_gather | solution.py:343
  36.6 5.4 %collective-permute-start = (f32[8,88,256]{2,1,0:T(8,128)}, f32[8,88,256]{2,1,0:T(8,128)}, u32[]{:S(2)}, u32[]{:S(2)}) collective-permute-start(f32[8,88,256]{2,1,0:T(8,128)} %bitcast.4.mine), channel_id=1, source_target_pairs={{0,4},{4,0},{1,5},{5,1},{2,6},{6,2},{3,7},{7,3},{8,12},{12,8},{9,1... | collective-permute-start | bytes 2162696 | tf_op jit(solution)/shard_map/ppermute | solution.py:46
  42.1 0.1 pad_add_fusion.pos
  42.1 2.1 %collective-permute-done.other = f32[8,88,256]{2,1,0:T(8,128)} collective-permute-done((f32[8,88,256]{2,1,0:T(8,128)}, f32[8,88,256]{2,1,0:T(8,128)}, u32[]{:S(2)}, u32[]{:S(2)}) %collective-permute-start) | collective-permute-done | bytes 720928 | tf_op jit(solution)/shard_map/ppermute | solution.py:46
  44.2 0.0 all-to-all-done.strips
  44.2 2.9 %shard_map.68 = (f32[128,256]{1,0:T(8,128)S(1)}, f32[128,256]{1,0:T(8,128)S(1)}, f32[128,256]{1,0:T(8,128)S(1)}, f32[128,256]{1,0:T(8,128)S(1)}) custom-call(s32[3]{0:T(128)S(1)} %pad_add_fusion.pos, f32[4,1408,128]{2,1,0:T(8,128)S(1)} %bitcast.46, f32[8,88,256]{2,1,0:T(8,128)} %bitcast.4.mine, f32[8,88,256]{2,1,0:T(8,128)} %collective-permute-done.other), custom_call_target="tpu_custom_call" | custom-call | flops 1107296256 | bytes 5767168 | tf_op jit(solution)/shard_map/pallas_call | solution.py:126
  47.1 3.5 %collective-permute-start.3 = (f32[128,256]{1,0:T(8,128)S(1)}, f32[128,256]{1,0:T(8,128)S(1)}, u32[]{:S(2)}, u32[]{:S(2)}) collective-permute-start(f32[128,256]{1,0:T(8,128)S(1)} %get-tuple-element.19), channel_id=1, source_target_pairs={{0,16},{8,24},{16,0},{24,8},{1,17},{9,25},{17,1},{25,9},{2,18},{10... | collective-permute-start | bytes 393224 | tf_op jit(solution)/shard_map/ppermute | solution.py:50
  50.6 0.1 collective-permute-start.2
  50.7 2.6 %collective-permute-start.1 = (f32[128,256]{1,0:T(8,128)S(1)}, f32[128,256]{1,0:T(8,128)S(1)}, u32[]{:S(2)}, u32[]{:S(2)}) collective-permute-start(f32[128,256]{1,0:T(8,128)S(1)} %get-tuple-element.17), channel_id=1, source_target_pairs={{0,24},{8,0},{16,8},{24,16},{1,25},{9,1},{17,9},{25,17},{2,26},{10... | collective-permute-start | bytes 393224 | tf_op jit(solution)/shard_map/ppermute | solution.py:50
  53.3 0.3 collective-permute-done.3
  53.5 3.5 %collective-permute-done.2 = f32[128,256]{1,0:T(8,128)S(1)} collective-permute-done((f32[128,256]{1,0:T(8,128)S(1)}, f32[128,256]{1,0:T(8,128)S(1)}, u32[]{:S(2)}, u32[]{:S(2)}) %collective-permute-start.2) | collective-permute-done | bytes 131104 | tf_op jit(solution)/shard_map/ppermute | solution.py:50
  57.1 0.0 collective-permute-done.1
  57.1 2.6 %collective-permute-start.6 = (f32[128,256]{1,0:T(8,128)S(1)}, f32[128,256]{1,0:T(8,128)S(1)}, u32[]{:S(2)}, u32[]{:S(2)}) collective-permute-start(f32[128,256]{1,0:T(8,128)S(1)} %add_add_fusion.1), channel_id=1, source_target_pairs={{0,3},{1,0},{2,1},{3,2},{4,7},{5,4},{6,5},{7,6},{8,11},{9,8},{10,9... | collective-permute-start | bytes 393224 | tf_op jit(solution)/shard_map/ppermute | solution.py:50
  59.7 1.7 collective-permute-start.5
  61.4 0.2 collective-permute-done.6
  61.6 5.2 %collective-permute-done.4 = f32[128,256]{1,0:T(8,128)S(1)} collective-permute-done((f32[128,256]{1,0:T(8,128)S(1)}, f32[128,256]{1,0:T(8,128)S(1)}, u32[]{:S(2)}, u32[]{:S(2)}) %collective-permute-start.4) | collective-permute-done | bytes 131104 | tf_op jit(solution)/shard_map/ppermute | solution.py:50
  66.9 1.9 %collective-permute-start.7 = (f32[128,256]{1,0:T(8,128)S(1)}, f32[128,256]{1,0:T(8,128)S(1)}, u32[]{:S(2)}, u32[]{:S(2)}) collective-permute-start(f32[128,256]{1,0:T(8,128)S(1)} %add_add_fusion.p0), channel_id=1, source_target_pairs={{0,8},{8,16},{16,24},{24,0},{1,9},{9,17},{17,25},{25,1},{2,10},{10... | collective-permute-start | bytes 393224 | tf_op jit(solution)/shard_map/ppermute | solution.py:50
  68.8 1.6 collective-permute-start.8
  70.3 0.9 collective-permute-start.9
  71.3 0.7 collective-permute-done.7.p1
  72.0 2.1 %collective-permute-done.8.p2 = f32[128,256]{1,0:T(8,128)S(1)} collective-permute-done((f32[128,256]{1,0:T(8,128)S(1)}, f32[128,256]{1,0:T(8,128)S(1)}, u32[]{:S(2)}, u32[]{:S(2)}) %collective-permute-start.8) | collective-permute-done | bytes 131104 | tf_op jit(solution)/shard_map/ppermute | solution.py:50
  74.1 0.3 collective-permute-done.9.p3
  74.5 3.5 %shard_map.69 = (f32[8,104,256]{2,1,0:T(8,128)S(1)}, f32[8,104,256]{2,1,0:T(8,128)S(1)}) custom-call(s32[3]{0:T(128)S(1)} %pad_add_fusion.pos, f32[4,8,176,128]{3,2,1,0:T(8,128)S(1)} %all-to-all-done.strips, f32[128,256]{1,0:T(8,128)S(1)} %add_add_fusion.p0, f32[128,256]{1,0:T(8,128)S(1)} %collective-permute-done.7.p1, ...), custom_call_target="tpu_custom_call" | custom-call | flops 1107296256 | bytes 4325376 | tf_op jit(solution)/shard_map/pallas_call | solution.py:170
  78.0 4.3 %collective-permute-start.10 = (f32[8,104,256]{2,1,0:T(8,128)S(1)}, f32[8,104,256]{2,1,0:T(8,128)S(1)}, u32[]{:S(2)}, u32[]{:S(2)}) collective-permute-start(f32[8,104,256]{2,1,0:T(8,128)S(1)} %get-tuple-element.21), channel_id=1, source_target_pairs={{0,4},{4,0},{1,5},{5,1},{2,6},{6,2},{3,7},{7,3},{8,12},{12,8},{9,1... | collective-permute-start | bytes 2555912 | tf_op jit(solution)/shard_map/ppermute | solution.py:46
  82.3 2.0 %collective-permute-done.10 = f32[8,104,256]{2,1,0:T(8,128)S(1)} collective-permute-done((f32[8,104,256]{2,1,0:T(8,128)S(1)}, f32[8,104,256]{2,1,0:T(8,128)S(1)}, u32[]{:S(2)}, u32[]{:S(2)}) %collective-permute-start.10) | collective-permute-done | bytes 852000 | tf_op jit(solution)/shard_map/ppermute | solution.py:46
  84.3 0.1 add.52
  84.4 29.6 %all_to_all.20 = f32[8,104,256]{2,1,0:T(8,128)S(1)} all-to-all(f32[8,104,256]{2,1,0:T(8,128)S(1)} %add.52), channel_id=1, replica_groups=mesh['z'=8,'y'=4,'c'=2,'x'=4] {'z'}, dimensions={0} | all-to-all | bytes 1703936 | tf_op jit(solution)/shard_map/all_to_all | solution.py:42
  114.0 0.1 reduce_sum.29
  114.0 2.3 %collective-permute-start.13 = (f32[16,256]{1,0:T(8,128)S(1)}, f32[16,256]{1,0:T(8,128)S(1)}, u32[]{:S(2)}, u32[]{:S(2)}) collective-permute-start(f32[16,256]{1,0:T(8,128)S(1)} %get-tuple-element.30), channel_id=1, source_target_pairs={{0,24},{8,0},{16,8},{24,16},{1,25},{9,1},{17,9},{25,17},{2,26},{10... | collective-permute-start | bytes 49160 | tf_op jit(solution)/shard_map/ppermute | solution.py:50
  116.3 0.0 collective-permute-start.12
  116.3 0.9 collective-permute-start.11
  117.2 0.9 broadcast_in_dim.8
  118.1 3.5 %all-to-all-start.2 = ((f32[8,88,256]{2,1,0:T(8,128)}), f32[8,88,256]{2,1,0:T(8,128)S(1)}, u32[]{:S(2)}, u32[]{:S(2)}) async-start(f32[8,88,256]{2,1,0:T(8,128)} %broadcast_in_dim.8), calls=%async_computation.2 | async-start | bytes 1441792 | tf_op jit(solution)/shard_map/all_to_all | solution.py:38
  121.7 0.0 collective-permute-done.12
  121.7 0.1 collective-permute-start.14
  121.8 2.6 %collective-permute-start.15 = (f32[4,16,256]{2,1,0:T(8,128)S(1)}, f32[4,16,256]{2,1,0:T(8,128)S(1)}, u32[]{:S(2)}, u32[]{:S(2)}) collective-permute-start(f32[4,16,256]{2,1,0:T(8,128)S(1)} %pad_maximum_fusion.2), channel_id=1, source_target_pairs={{0,2},{1,3},{2,0},{3,1},{4,6},{5,7},{6,4},{7,5},{8,10},{9,11},{10,... | collective-permute-start | bytes 196616 | tf_op jit(solution)/shard_map/ppermute | solution.py:50
  124.4 0.2 collective-permute-start.16
  124.6 1.5 collective-permute-done.14
  126.1 0.7 collective-permute-done.15
  126.8 1.0 collective-permute-done.16
  128.0 0.1 pad_maximum_fusion
  128.1 10.4 %shard_map.70 = f32[256,256]{1,0:T(8,128)S(1)} custom-call(f32[256,256]{1,0:T(8,128)S(1)} %bitcast.52), custom_call_target="tpu_custom_call" | custom-call | flops 100000000 | bytes 1000000 | tf_op jit(solution)/shard_map/pallas_call | solution.py:264
  138.5 3.6 %all-to-all-done.2 = f32[8,88,256]{2,1,0:T(8,128)S(1)} async-done(((f32[8,88,256]{2,1,0:T(8,128)}), f32[8,88,256]{2,1,0:T(8,128)S(1)}, u32[]{:S(2)}, u32[]{:S(2)}) %all-to-all-start.2) | async-done | bytes 720928 | tf_op jit(solution)/shard_map/all_to_all | solution.py:38
  142.0 0.5 multiply_reduce_fusion
  142.5 1.3 collective-permute-start.18
  143.9 1.4 collective-permute-start.19
  145.3 2.8 %collective-permute-start.17 = (f32[1,256]{1,0:T(1,128)S(1)}, f32[1,256]{1,0:T(1,128)S(1)}, u32[]{:S(2)}, u32[]{:S(2)}) collective-permute-start(f32[1,256]{1,0:T(1,128)S(1)} %bitcast.65), channel_id=1, source_target_pairs={{0,4},{4,0},{1,5},{5,1},{2,6},{6,2},{3,7},{7,3},{8,12},{12,8},{9,1... | collective-permute-start | bytes 3080 | tf_op jit(solution)/shard_map/ppermute | solution.py:46
  148.1 0.8 collective-permute-done.17
  148.9 10.5 %all_to_all.21 = f32[16,1,256]{2,1,0:T(1,128)S(1)} all-to-all(f32[16,1,256]{2,1,0:T(1,128)S(1)} %broadcast_in_dim.20), channel_id=1, replica_groups=mesh['z'=8,'y'=4,'c'=2,'x'=4] {'y','x'}, dimensions={0} | all-to-all | bytes 32768 | tf_op jit(solution)/shard_map/all_to_all | solution.py:38
  159.5 0.8 slice.14
  160.3 0.6 collective-permute-start.20
  160.8 0.8 slice.15
  161.6 2.1 %collective-permute-start.21 = (f32[4,88,256]{2,1,0:T(8,128)}, f32[4,88,256]{2,1,0:T(8,128)S(1)}, u32[]{:S(2)}, u32[]{:S(2)}) collective-permute-start(f32[4,88,256]{2,1,0:T(8,128)} %slice.15), channel_id=1, source_target_pairs={{0,24},{8,0},{16,8},{24,16},{1,25},{9,1},{17,9},{25,17},{2,26},{10... | collective-permute-start | bytes 1081352 | tf_op jit(solution)/shard_map/ppermute | solution.py:50
  163.7 3.9 %collective-permute-start.22 = (f32[8,88,256]{2,1,0:T(8,128)S(1)}, f32[8,88,256]{2,1,0:T(8,128)S(1)}, u32[]{:S(2)}, u32[]{:S(2)}) collective-permute-start(f32[8,88,256]{2,1,0:T(8,128)S(1)} %bitcast.49), channel_id=1, source_target_pairs={{0,4},{4,0},{1,5},{5,1},{2,6},{6,2},{3,7},{7,3},{8,12},{12,8},{9,1... | collective-permute-start | bytes 2162696 | tf_op jit(solution)/shard_map/ppermute | solution.py:46
  167.6 0.5 collective-permute-start.24
  168.1 0.2 collective-permute-done.20.refs_3_
  168.3 4.2 %collective-permute-start.25 = (f32[4,88,256]{2,1,0:T(8,128)S(1)}, f32[4,88,256]{2,1,0:T(8,128)S(1)}, u32[]{:S(2)}, u32[]{:S(2)}) collective-permute-start(f32[4,88,256]{2,1,0:T(8,128)S(1)} %collective-permute-done.20.refs_3_), channel_id=1, source_target_pairs={{0,4},{4,0},{1,5},{5,1},{2,6},{6,2},{3,7},{7,3},{8,12},{12,8},{9,1... | collective-permute-start | bytes 1081352 | tf_op jit(solution)/shard_map/ppermute | solution.py:46
  172.5 0.6 collective-permute-start.26
  173.1 0.4 broadcast_multiply_fusion
  173.5 0.7 bitcast_multiply_fusion
  174.2 0.2 collective-permute-done.26.refs_9_
  174.4 7.6 %shard_map.71 = (f32[128,5632]{1,0:T(8,128)}, f32[128,5632]{1,0:T(8,128)}) custom-call(s32[3]{0:T(128)S(1)} %pad_add_fusion.pos, f32[256,256]{1,0:T(8,128)S(1)} %pad_maximum_fusion.1.left, bf16[128,5632]{1,0:T(8,128)(2,1)} %grad.3, f32[128,5632]{1,0:T(8,128)} %mom.3, f32[128,5632]{1,0:T(8,128)} %wgt.1, f32[8,88,256]{2,1,0:T(8,128)S(1)} %bitcast.51, ...), custom_call_target="tpu_custom_call" | custom-call | flops 2214592512 | bytes 12976128 | tf_op jit(solution)/shard_map/pallas_call | solution.py:319
  (36 shorter events, 0.4 us)
Async XLA Ops:
  4.4 5.1 %copy-start = (f32[88,256]{1,0:T(8,128)S(1)}, f32[88,256]{1,0:T(8,128)}, u32[]{:S(2)}) copy-start(f32[88,256]{1,0:T(8,128)} %param.7) | copy-start | bytes 270340
  4.4 39.8 %all-to-all-start = ((f32[4,8,176,128]{3,2,1,0:T(8,128)}), f32[4,8,176,128]{3,2,1,0:T(8,128)S(1)}, u32[]{:S(2)}, u32[]{:S(2)}) async-start(f32[4,8,176,128]{3,2,1,0:T(8,128)} %shard_map.67), calls=%async_computation | async-start | bytes 5767168 | tf_op jit(solution)/shard_map/all_to_all | solution.py:342
  36.6 7.6 %collective-permute-start = (f32[8,88,256]{2,1,0:T(8,128)}, f32[8,88,256]{2,1,0:T(8,128)}, u32[]{:S(2)}, u32[]{:S(2)}) collective-permute-start(f32[8,88,256]{2,1,0:T(8,128)} %bitcast.4.mine), channel_id=1, source_target_pairs={{0,4},{4,0},{1,5},{5,1},{2,6},{6,2},{3,7},{7,3},{8,12},{12,8},{9,1... | collective-permute-start | bytes 2162696 | tf_op jit(solution)/shard_map/ppermute | solution.py:46
  47.1 6.4 %collective-permute-start.3 = (f32[128,256]{1,0:T(8,128)S(1)}, f32[128,256]{1,0:T(8,128)S(1)}, u32[]{:S(2)}, u32[]{:S(2)}) collective-permute-start(f32[128,256]{1,0:T(8,128)S(1)} %get-tuple-element.19), channel_id=1, source_target_pairs={{0,16},{8,24},{16,0},{24,8},{1,17},{9,25},{17,1},{25,9},{2,18},{10... | collective-permute-start | bytes 393224 | tf_op jit(solution)/shard_map/ppermute | solution.py:50
  50.6 6.5 %collective-permute-start.2 = (f32[128,256]{1,0:T(8,128)S(1)}, f32[128,256]{1,0:T(8,128)S(1)}, u32[]{:S(2)}, u32[]{:S(2)}) collective-permute-start(f32[128,256]{1,0:T(8,128)S(1)} %get-tuple-element.18), channel_id=1, source_target_pairs={{0,8},{8,16},{16,24},{24,0},{1,9},{9,17},{17,25},{25,1},{2,10},{10... | collective-permute-start | bytes 393224 | tf_op jit(solution)/shard_map/ppermute | solution.py:50
  50.7 6.4 %collective-permute-start.1 = (f32[128,256]{1,0:T(8,128)S(1)}, f32[128,256]{1,0:T(8,128)S(1)}, u32[]{:S(2)}, u32[]{:S(2)}) collective-permute-start(f32[128,256]{1,0:T(8,128)S(1)} %get-tuple-element.17), channel_id=1, source_target_pairs={{0,24},{8,0},{16,8},{24,16},{1,25},{9,1},{17,9},{25,17},{2,26},{10... | collective-permute-start | bytes 393224 | tf_op jit(solution)/shard_map/ppermute | solution.py:50
  57.1 4.5 %collective-permute-start.6 = (f32[128,256]{1,0:T(8,128)S(1)}, f32[128,256]{1,0:T(8,128)S(1)}, u32[]{:S(2)}, u32[]{:S(2)}) collective-permute-start(f32[128,256]{1,0:T(8,128)S(1)} %add_add_fusion.1), channel_id=1, source_target_pairs={{0,3},{1,0},{2,1},{3,2},{4,7},{5,4},{6,5},{7,6},{8,11},{9,8},{10,9... | collective-permute-start | bytes 393224 | tf_op jit(solution)/shard_map/ppermute | solution.py:50
  59.7 7.2 %collective-permute-start.4 = (f32[128,256]{1,0:T(8,128)S(1)}, f32[128,256]{1,0:T(8,128)S(1)}, u32[]{:S(2)}, u32[]{:S(2)}) collective-permute-start(f32[128,256]{1,0:T(8,128)S(1)} %add_add_fusion.1), channel_id=1, source_target_pairs={{0,1},{1,2},{2,3},{3,0},{4,5},{5,6},{6,7},{7,4},{8,9},{9,10},{10,1... | collective-permute-start | bytes 393224 | tf_op jit(solution)/shard_map/ppermute | solution.py:50
  59.7 7.2 %collective-permute-start.5 = (f32[128,256]{1,0:T(8,128)S(1)}, f32[128,256]{1,0:T(8,128)S(1)}, u32[]{:S(2)}, u32[]{:S(2)}) collective-permute-start(f32[128,256]{1,0:T(8,128)S(1)} %add_add_fusion.1), channel_id=1, source_target_pairs={{0,2},{1,3},{2,0},{3,1},{4,6},{5,7},{6,4},{7,5},{8,10},{9,11},{10,... | collective-permute-start | bytes 393224 | tf_op jit(solution)/shard_map/ppermute | solution.py:50
  66.9 5.1 %collective-permute-start.7 = (f32[128,256]{1,0:T(8,128)S(1)}, f32[128,256]{1,0:T(8,128)S(1)}, u32[]{:S(2)}, u32[]{:S(2)}) collective-permute-start(f32[128,256]{1,0:T(8,128)S(1)} %add_add_fusion.p0), channel_id=1, source_target_pairs={{0,8},{8,16},{16,24},{24,0},{1,9},{9,17},{17,25},{25,1},{2,10},{10... | collective-permute-start | bytes 393224 | tf_op jit(solution)/shard_map/ppermute | solution.py:50
  68.8 5.3 %collective-permute-start.8 = (f32[128,256]{1,0:T(8,128)S(1)}, f32[128,256]{1,0:T(8,128)S(1)}, u32[]{:S(2)}, u32[]{:S(2)}) collective-permute-start(f32[128,256]{1,0:T(8,128)S(1)} %add_add_fusion.p0), channel_id=1, source_target_pairs={{0,16},{8,24},{16,0},{24,8},{1,17},{9,25},{17,1},{25,9},{2,18},{10... | collective-permute-start | bytes 393224 | tf_op jit(solution)/shard_map/ppermute | solution.py:50
  70.3 4.1 %collective-permute-start.9 = (f32[128,256]{1,0:T(8,128)S(1)}, f32[128,256]{1,0:T(8,128)S(1)}, u32[]{:S(2)}, u32[]{:S(2)}) collective-permute-start(f32[128,256]{1,0:T(8,128)S(1)} %add_add_fusion.p0), channel_id=1, source_target_pairs={{0,24},{8,0},{16,8},{24,16},{1,25},{9,1},{17,9},{25,17},{2,26},{10... | collective-permute-start | bytes 393224 | tf_op jit(solution)/shard_map/ppermute | solution.py:50
  78.0 6.3 %collective-permute-start.10 = (f32[8,104,256]{2,1,0:T(8,128)S(1)}, f32[8,104,256]{2,1,0:T(8,128)S(1)}, u32[]{:S(2)}, u32[]{:S(2)}) collective-permute-start(f32[8,104,256]{2,1,0:T(8,128)S(1)} %get-tuple-element.21), channel_id=1, source_target_pairs={{0,4},{4,0},{1,5},{5,1},{2,6},{6,2},{3,7},{7,3},{8,12},{12,8},{9,1... | collective-permute-start | bytes 2555912 | tf_op jit(solution)/shard_map/ppermute | solution.py:46
  114.0 7.6 %collective-permute-start.13 = (f32[16,256]{1,0:T(8,128)S(1)}, f32[16,256]{1,0:T(8,128)S(1)}, u32[]{:S(2)}, u32[]{:S(2)}) collective-permute-start(f32[16,256]{1,0:T(8,128)S(1)} %get-tuple-element.30), channel_id=1, source_target_pairs={{0,24},{8,0},{16,8},{24,16},{1,25},{9,1},{17,9},{25,17},{2,26},{10... | collective-permute-start | bytes 49160 | tf_op jit(solution)/shard_map/ppermute | solution.py:50
  116.3 5.3 %collective-permute-start.12 = (f32[16,256]{1,0:T(8,128)S(1)}, f32[16,256]{1,0:T(8,128)S(1)}, u32[]{:S(2)}, u32[]{:S(2)}) collective-permute-start(f32[16,256]{1,0:T(8,128)S(1)} %get-tuple-element.30), channel_id=1, source_target_pairs={{0,16},{8,24},{16,0},{24,8},{1,17},{9,25},{17,1},{25,9},{2,18},{10... | collective-permute-start | bytes 49160 | tf_op jit(solution)/shard_map/ppermute | solution.py:50
  116.3 5.3 %collective-permute-start.11 = (f32[16,256]{1,0:T(8,128)S(1)}, f32[16,256]{1,0:T(8,128)S(1)}, u32[]{:S(2)}, u32[]{:S(2)}) collective-permute-start(f32[16,256]{1,0:T(8,128)S(1)} %get-tuple-element.30), channel_id=1, source_target_pairs={{0,8},{8,16},{16,24},{24,0},{1,9},{9,17},{17,25},{25,1},{2,10},{10... | collective-permute-start | bytes 49160 | tf_op jit(solution)/shard_map/ppermute | solution.py:50
  118.1 23.9 %all-to-all-start.2 = ((f32[8,88,256]{2,1,0:T(8,128)}), f32[8,88,256]{2,1,0:T(8,128)S(1)}, u32[]{:S(2)}, u32[]{:S(2)}) async-start(f32[8,88,256]{2,1,0:T(8,128)} %broadcast_in_dim.8), calls=%async_computation.2 | async-start | bytes 1441792 | tf_op jit(solution)/shard_map/all_to_all | solution.py:38
  121.7 4.4 %collective-permute-start.14 = (f32[4,16,256]{2,1,0:T(8,128)S(1)}, f32[4,16,256]{2,1,0:T(8,128)S(1)}, u32[]{:S(2)}, u32[]{:S(2)}) collective-permute-start(f32[4,16,256]{2,1,0:T(8,128)S(1)} %pad_maximum_fusion.2), channel_id=1, source_target_pairs={{0,1},{1,2},{2,3},{3,0},{4,5},{5,6},{6,7},{7,4},{8,9},{9,10},{10,1... | collective-permute-start | bytes 196616 | tf_op jit(solution)/shard_map/ppermute | solution.py:50
  121.8 5.0 %collective-permute-start.15 = (f32[4,16,256]{2,1,0:T(8,128)S(1)}, f32[4,16,256]{2,1,0:T(8,128)S(1)}, u32[]{:S(2)}, u32[]{:S(2)}) collective-permute-start(f32[4,16,256]{2,1,0:T(8,128)S(1)} %pad_maximum_fusion.2), channel_id=1, source_target_pairs={{0,2},{1,3},{2,0},{3,1},{4,6},{5,7},{6,4},{7,5},{8,10},{9,11},{10,... | collective-permute-start | bytes 196616 | tf_op jit(solution)/shard_map/ppermute | solution.py:50
  124.4 3.4 %collective-permute-start.16 = (f32[4,16,256]{2,1,0:T(8,128)S(1)}, f32[4,16,256]{2,1,0:T(8,128)S(1)}, u32[]{:S(2)}, u32[]{:S(2)}) collective-permute-start(f32[4,16,256]{2,1,0:T(8,128)S(1)} %pad_maximum_fusion.2), channel_id=1, source_target_pairs={{0,3},{1,0},{2,1},{3,2},{4,7},{5,4},{6,5},{7,6},{8,11},{9,8},{10,9... | collective-permute-start | bytes 196616 | tf_op jit(solution)/shard_map/ppermute | solution.py:50
  142.5 16.9 %collective-permute-start.18 = (f32[8,88,256]{2,1,0:T(8,128)S(1)}, f32[8,88,256]{2,1,0:T(8,128)S(1)}, u32[]{:S(2)}, u32[]{:S(2)}) collective-permute-start(f32[8,88,256]{2,1,0:T(8,128)S(1)} %bitcast.47), channel_id=1, source_target_pairs={{0,8},{8,16},{16,24},{24,0},{1,9},{9,17},{17,25},{25,1},{2,10},{10... | collective-permute-start | bytes 2162696 | tf_op jit(solution)/shard_map/ppermute | solution.py:50
  143.9 15.6 %collective-permute-start.19 = (f32[8,88,256]{2,1,0:T(8,128)S(1)}, f32[8,88,256]{2,1,0:T(8,128)S(1)}, u32[]{:S(2)}, u32[]{:S(2)}) collective-permute-start(f32[8,88,256]{2,1,0:T(8,128)S(1)} %bitcast.48), channel_id=1, source_target_pairs={{0,24},{8,0},{16,8},{24,16},{1,25},{9,1},{17,9},{25,17},{2,26},{10... | collective-permute-start | bytes 2162696 | tf_op jit(solution)/shard_map/ppermute | solution.py:50
  145.3 3.6 %collective-permute-start.17 = (f32[1,256]{1,0:T(1,128)S(1)}, f32[1,256]{1,0:T(1,128)S(1)}, u32[]{:S(2)}, u32[]{:S(2)}) collective-permute-start(f32[1,256]{1,0:T(1,128)S(1)} %bitcast.65), channel_id=1, source_target_pairs={{0,4},{4,0},{1,5},{5,1},{2,6},{6,2},{3,7},{7,3},{8,12},{12,8},{9,1... | collective-permute-start | bytes 3080 | tf_op jit(solution)/shard_map/ppermute | solution.py:46
  160.3 8.0 %collective-permute-start.20 = (f32[4,88,256]{2,1,0:T(8,128)}, f32[4,88,256]{2,1,0:T(8,128)S(1)}, u32[]{:S(2)}, u32[]{:S(2)}) collective-permute-start(f32[4,88,256]{2,1,0:T(8,128)} %slice.14), channel_id=1, source_target_pairs={{0,8},{8,16},{16,24},{24,0},{1,9},{9,17},{17,25},{25,1},{2,10},{10... | collective-permute-start | bytes 1081352 | tf_op jit(solution)/shard_map/ppermute | solution.py:50
  161.6 10.9 %collective-permute-start.21 = (f32[4,88,256]{2,1,0:T(8,128)}, f32[4,88,256]{2,1,0:T(8,128)S(1)}, u32[]{:S(2)}, u32[]{:S(2)}) collective-permute-start(f32[4,88,256]{2,1,0:T(8,128)} %slice.15), channel_id=1, source_target_pairs={{0,24},{8,0},{16,8},{24,16},{1,25},{9,1},{17,9},{25,17},{2,26},{10... | collective-permute-start | bytes 1081352 | tf_op jit(solution)/shard_map/ppermute | solution.py:50
  163.7 10.5 %collective-permute-start.22 = (f32[8,88,256]{2,1,0:T(8,128)S(1)}, f32[8,88,256]{2,1,0:T(8,128)S(1)}, u32[]{:S(2)}, u32[]{:S(2)}) collective-permute-start(f32[8,88,256]{2,1,0:T(8,128)S(1)} %bitcast.49), channel_id=1, source_target_pairs={{0,4},{4,0},{1,5},{5,1},{2,6},{6,2},{3,7},{7,3},{8,12},{12,8},{9,1... | collective-permute-start | bytes 2162696 | tf_op jit(solution)/shard_map/ppermute | solution.py:46
  167.6 6.8 %collective-permute-start.23 = (f32[8,88,256]{2,1,0:T(8,128)S(1)}, f32[8,88,256]{2,1,0:T(8,128)S(1)}, u32[]{:S(2)}, u32[]{:S(2)}) collective-permute-start(f32[8,88,256]{2,1,0:T(8,128)S(1)} %collective-permute-done.18.refs_1_), channel_id=1, source_target_pairs={{0,4},{4,0},{1,5},{5,1},{2,6},{6,2},{3,7},{7,3},{8,12},{12,8},{9,1... | collective-permute-start | bytes 2162696 | tf_op jit(solution)/shard_map/ppermute | solution.py:46
  167.6 6.8 %collective-permute-start.24 = (f32[8,88,256]{2,1,0:T(8,128)S(1)}, f32[8,88,256]{2,1,0:T(8,128)S(1)}, u32[]{:S(2)}, u32[]{:S(2)}) collective-permute-start(f32[8,88,256]{2,1,0:T(8,128)S(1)} %collective-permute-done.19.refs_2_), channel_id=1, source_target_pairs={{0,4},{4,0},{1,5},{5,1},{2,6},{6,2},{3,7},{7,3},{8,12},{12,8},{9,1... | collective-permute-start | bytes 2162696 | tf_op jit(solution)/shard_map/ppermute | solution.py:46
  168.3 5.9 %collective-permute-start.25 = (f32[4,88,256]{2,1,0:T(8,128)S(1)}, f32[4,88,256]{2,1,0:T(8,128)S(1)}, u32[]{:S(2)}, u32[]{:S(2)}) collective-permute-start(f32[4,88,256]{2,1,0:T(8,128)S(1)} %collective-permute-done.20.refs_3_), channel_id=1, source_target_pairs={{0,4},{4,0},{1,5},{5,1},{2,6},{6,2},{3,7},{7,3},{8,12},{12,8},{9,1... | collective-permute-start | bytes 1081352 | tf_op jit(solution)/shard_map/ppermute | solution.py:46
  172.5 1.9 %collective-permute-start.26 = (f32[4,88,256]{2,1,0:T(8,128)S(1)}, f32[4,88,256]{2,1,0:T(8,128)S(1)}, u32[]{:S(2)}, u32[]{:S(2)}) collective-permute-start(f32[4,88,256]{2,1,0:T(8,128)S(1)} %collective-permute-done.21.refs_4_), channel_id=1, source_target_pairs={{0,4},{4,0},{1,5},{5,1},{2,6},{6,2},{3,7},{7,3},{8,12},{12,8},{9,1... | collective-permute-start | bytes 1081352 | tf_op jit(solution)/shard_map/ppermute | solution.py:46

commit v4 on v3

--- a/solution.py
+++ b/solution.py
@@ -36,10 +36,6 @@
 def gather(block, axes, count):
     copies = jnp.broadcast_to(block[None], (count,) + block.shape)
     return lax.all_to_all(copies, axes, 0, 0)
-
-
-def scatter_sum(blocks, axes):
-    return jnp.sum(lax.all_to_all(blocks, axes, 0, 0), axis=0)
 
 
 def swap(block):
@@ -163,7 +159,7 @@
 def raw_feedback(pos, strips, projs):
     _, _, size, rows = strips.shape
     part = RANK // (NY * NX)
-    steps = 2
+    steps = 4
     strip = pl.BlockSpec((NY, steps, size, rows), lambda z: (0, z, 0, 0))
     proj = pl.BlockSpec((rows, RANK), lambda z: (0, 0))
     out = pl.BlockSpec((steps, size // 2 + part, RANK), lambda z: (z, 0, 0))
@@ -182,6 +178,31 @@
         compiler_params=params(24),
         cost_estimate=cost(6 * NY * rows * NZ * size * RANK, NZ * size * rows * 24),
     )(pos, strips, *projs)
+
+
+def share_kernel(parts, copies, gram):
+    total = parts[0]
+    for k in range(1, parts.shape[0]):
+        total = total + parts[k]
+    shard = copies.shape[1]
+    for k in range(copies.shape[0]):
+        copies[k] = total[:shard]
+    gram[...] = total[shard:]
+
+
+def share(parts, shard):
+    count, rows, _ = parts.shape
+    return pl.pallas_call(
+        share_kernel,
+        in_specs=[pl.BlockSpec(memory_space=pltpu.VMEM)],
+        out_specs=[pl.BlockSpec(memory_space=pltpu.VMEM)] * 2,
+        out_shape=[
+            jax.ShapeDtypeStruct((count, shard, RANK), jnp.float32),
+            jax.ShapeDtypeStruct((rows - shard, RANK), jnp.float32),
+        ],
+        compiler_params=params(8),
+        cost_estimate=cost(count * rows * RANK, 2 * count * rows * RANK * 4),
+    )(parts)
 
 
 BLOCK = 64
@@ -353,9 +374,9 @@
     projs = [projected] + [shift(projected, "y", NY, d) for d in range(1, NY)]
 
     mine, other = raw_feedback(pos, strips, projs)
-    reduced = scatter_sum(mine + swap(other), "z")
-    raw_shard, gram_part = reduced[:shard], reduced[shard:]
-    raw = gather(raw_shard, "z", NZ)
+    parts = lax.all_to_all(mine + swap(other), "z", 0, 0)
+    copies, gram_part = share(parts, shard)
+    raw = lax.all_to_all(copies, "z", 0, 0)
 
     by_y = jnp.stack([gram_part] + [shift(gram_part, "y", NY, d) for d in range(1, NY)])
     by_x = jnp.stack([by_y] + [shift(by_y, "x", NX, d) for d in range(1, NX)])

time: 182 us -> 182 us (level)
  transfers between devices with their start and end apart: 29 -> 29, of which waited for: 16 -> 15; matrix products, arithmetic and copies ran while one was open for 2% -> 1% of each run, Pallas kernels for 6% -> 6%
where the time goes in v4:
time: 182 us; the launch traced here: 181 us
  blocking collectives  67.1 us (37%)
  starting transfers between devices  56.5 us (31%)
  Pallas kernels  28.7 us (16%)
  waiting for transfers between devices  24.4 us (13%)
    all_to_all x1, blocking collectives, body(): parts = lax.all_to_all(mine + swap(other), 'z', 0, 0)  29.6 us
    all_gather x1, blocking collectives, body(): basis_z = lax.all_gather(basis, 'z', axis=0)  27.1 us
    ppermute x19, starting transfers between devices, shift(): lax.ppermute(block, axis, [(i, (i + step) % size) for i in range(size)])  25.9 us
    ppermute x8, starting transfers between devices, swap(): return lax.ppermute(block, 'c', [(0, 1), (1, 0)])  21.9 us
    ppermute x19, waiting for transfers between devices, shift(): lax.ppermute(block, axis, [(i, (i + step) % size) for i in range(size)])  15.7 us
    all_to_all x1, blocking collectives, gather(): return lax.all_to_all(copies, axes, 0, 0)  10.5 us
    pallas_call x1, Pallas kernels, factor_inverse(): pl.pallas_call(inverse_kernel, in_specs=[pl.BlockSpec(memory_space=pltpu....  10.4 us
    pallas_call x1, Pallas kernels, update(): pl.pallas_call(update_kernel, grid=(NZ // 2,), in_specs=[smem(), whole, b...  7.64 us
  transfers between devices with their start and end apart: 29, of which 15 were waited for; matrix products, arithmetic and copies ran while one was open for 1% of the time, Pallas kernels for 6%

profile of v4, /device:TPU:1, one launch (start us, length us, event | category | flops | bytes accessed | tf_op | source)
XLA Modules:
  0.0 181.1 jit_solution(600455515127686104)
XLA Ops:
  0.6 3.8 %shard_map.67 = f32[4,8,176,128]{3,2,1,0:T(8,128)} custom-call(bf16[128,5632]{1,0:T(8,128)(2,1)} %grad.3, f32[128,5632]{1,0:T(8,128)} %mom.3), custom_call_target="tpu_custom_call" | custom-call | bytes 7208960 | tf_op jit(solution)/shard_map/pallas_call | solution.py:95
  4.4 5.1 %all-to-all-start = ((f32[4,8,176,128]{3,2,1,0:T(8,128)}), f32[4,8,176,128]{3,2,1,0:T(8,128)S(1)}, u32[]{:S(2)}, u32[]{:S(2)}) async-start(f32[4,8,176,128]{3,2,1,0:T(8,128)} %shard_map.67), calls=%async_computation | async-start | bytes 5767168 | tf_op jit(solution)/shard_map/all_to_all | solution.py:363
  9.6 27.1 %all-gather = f32[704,256]{1,0:T(8,128)} all-gather(f32[88,256]{1,0:T(8,128)S(1)} %copy-done), channel_id=2, replica_groups=mesh['z'=8,'y'=4,'c'=2,'x'=4] {'z'}, dimensions={0}, use_global_device_ids=true | all-gather | bytes 811008 | tf_op jit(solution)/shard_map/all_gather | solution.py:364
  36.6 5.4 %collective-permute-start = (f32[8,88,256]{2,1,0:T(8,128)}, f32[8,88,256]{2,1,0:T(8,128)}, u32[]{:S(2)}, u32[]{:S(2)}) collective-permute-start(f32[8,88,256]{2,1,0:T(8,128)} %bitcast.4.mine), channel_id=1, source_target_pairs={{0,4},{4,0},{1,5},{5,1},{2,6},{6,2},{3,7},{7,3},{8,12},{12,8},{9,1... | collective-permute-start | bytes 2162696 | tf_op jit(solution)/shard_map/ppermute | solution.py:42
  42.1 0.1 pad_add_fusion.pos
  42.1 2.1 %collective-permute-done.other = f32[8,88,256]{2,1,0:T(8,128)} collective-permute-done((f32[8,88,256]{2,1,0:T(8,128)}, f32[8,88,256]{2,1,0:T(8,128)}, u32[]{:S(2)}, u32[]{:S(2)}) %collective-permute-start) | collective-permute-done | bytes 720928 | tf_op jit(solution)/shard_map/ppermute | solution.py:42
  44.2 0.0 all-to-all-done.strips
  44.2 2.9 %shard_map.68 = (f32[128,256]{1,0:T(8,128)S(1)}, f32[128,256]{1,0:T(8,128)S(1)}, f32[128,256]{1,0:T(8,128)S(1)}, f32[128,256]{1,0:T(8,128)S(1)}) custom-call(s32[3]{0:T(128)S(1)} %pad_add_fusion.pos, f32[4,1408,128]{2,1,0:T(8,128)S(1)} %bitcast.36, f32[8,88,256]{2,1,0:T(8,128)} %bitcast.4.mine, f32[8,88,256]{2,1,0:T(8,128)} %collective-permute-done.other), custom_call_target="tpu_custom_call" | custom-call | flops 1107296256 | bytes 5767168 | tf_op jit(solution)/shard_map/pallas_call | solution.py:122
  47.1 3.5 %collective-permute-start.3 = (f32[128,256]{1,0:T(8,128)S(1)}, f32[128,256]{1,0:T(8,128)S(1)}, u32[]{:S(2)}, u32[]{:S(2)}) collective-permute-start(f32[128,256]{1,0:T(8,128)S(1)} %get-tuple-element.21), channel_id=1, source_target_pairs={{0,16},{8,24},{16,0},{24,8},{1,17},{9,25},{17,1},{25,9},{2,18},{10... | collective-permute-start | bytes 393224 | tf_op jit(solution)/shard_map/ppermute | solution.py:46
  50.6 0.1 collective-permute-start.2
  50.7 2.6 %collective-permute-start.1 = (f32[128,256]{1,0:T(8,128)S(1)}, f32[128,256]{1,0:T(8,128)S(1)}, u32[]{:S(2)}, u32[]{:S(2)}) collective-permute-start(f32[128,256]{1,0:T(8,128)S(1)} %get-tuple-element.19), channel_id=1, source_target_pairs={{0,24},{8,0},{16,8},{24,16},{1,25},{9,1},{17,9},{25,17},{2,26},{10... | collective-permute-start | bytes 393224 | tf_op jit(solution)/shard_map/ppermute | solution.py:46
  53.3 0.3 collective-permute-done.3
  53.5 3.5 %collective-permute-done.2 = f32[128,256]{1,0:T(8,128)S(1)} collective-permute-done((f32[128,256]{1,0:T(8,128)S(1)}, f32[128,256]{1,0:T(8,128)S(1)}, u32[]{:S(2)}, u32[]{:S(2)}) %collective-permute-start.2) | collective-permute-done | bytes 131104 | tf_op jit(solution)/shard_map/ppermute | solution.py:46
  57.1 0.0 collective-permute-done.1
  57.1 2.6 %collective-permute-start.6 = (f32[128,256]{1,0:T(8,128)S(1)}, f32[128,256]{1,0:T(8,128)S(1)}, u32[]{:S(2)}, u32[]{:S(2)}) collective-permute-start(f32[128,256]{1,0:T(8,128)S(1)} %add_add_fusion.1), channel_id=1, source_target_pairs={{0,3},{1,0},{2,1},{3,2},{4,7},{5,4},{6,5},{7,6},{8,11},{9,8},{10,9... | collective-permute-start | bytes 393224 | tf_op jit(solution)/shard_map/ppermute | solution.py:46
  59.7 1.7 collective-permute-start.5
  61.4 0.2 collective-permute-done.6
  61.6 5.2 %collective-permute-done.4 = f32[128,256]{1,0:T(8,128)S(1)} collective-permute-done((f32[128,256]{1,0:T(8,128)S(1)}, f32[128,256]{1,0:T(8,128)S(1)}, u32[]{:S(2)}, u32[]{:S(2)}) %collective-permute-start.4) | collective-permute-done | bytes 131104 | tf_op jit(solution)/shard_map/ppermute | solution.py:46
  66.9 1.9 %collective-permute-start.7 = (f32[128,256]{1,0:T(8,128)S(1)}, f32[128,256]{1,0:T(8,128)S(1)}, u32[]{:S(2)}, u32[]{:S(2)}) collective-permute-start(f32[128,256]{1,0:T(8,128)S(1)} %add_add_fusion.p0), channel_id=1, source_target_pairs={{0,8},{8,16},{16,24},{24,0},{1,9},{9,17},{17,25},{25,1},{2,10},{10... | collective-permute-start | bytes 393224 | tf_op jit(solution)/shard_map/ppermute | solution.py:46
  68.8 1.6 collective-permute-start.8
  70.3 0.9 collective-permute-start.9
  71.3 0.7 collective-permute-done.7.p1
  72.0 2.1 %collective-permute-done.8.p2 = f32[128,256]{1,0:T(8,128)S(1)} collective-permute-done((f32[128,256]{1,0:T(8,128)S(1)}, f32[128,256]{1,0:T(8,128)S(1)}, u32[]{:S(2)}, u32[]{:S(2)}) %collective-permute-start.8) | collective-permute-done | bytes 131104 | tf_op jit(solution)/shard_map/ppermute | solution.py:46
  74.1 0.3 collective-permute-done.9.p3
  74.5 3.1 %shard_map.69 = (f32[8,104,256]{2,1,0:T(8,128)S(1)}, f32[8,104,256]{2,1,0:T(8,128)S(1)}) custom-call(s32[3]{0:T(128)S(1)} %pad_add_fusion.pos, f32[4,8,176,128]{3,2,1,0:T(8,128)S(1)} %all-to-all-done.strips, f32[128,256]{1,0:T(8,128)S(1)} %add_add_fusion.p0, f32[128,256]{1,0:T(8,128)S(1)} %collective-permute-done.7.p1, ...), custom_call_target="tpu_custom_call" | custom-call | flops 1107296256 | bytes 4325376 | tf_op jit(solution)/shard_map/pallas_call | solution.py:166
  77.5 4.3 %collective-permute-start.10 = (f32[8,104,256]{2,1,0:T(8,128)S(1)}, f32[8,104,256]{2,1,0:T(8,128)S(1)}, u32[]{:S(2)}, u32[]{:S(2)}) collective-permute-start(f32[8,104,256]{2,1,0:T(8,128)S(1)} %get-tuple-element.23), channel_id=1, source_target_pairs={{0,4},{4,0},{1,5},{5,1},{2,6},{6,2},{3,7},{7,3},{8,12},{12,8},{9,1... | collective-permute-start | bytes 2555912 | tf_op jit(solution)/shard_map/ppermute | solution.py:42
  81.8 2.0 %collective-permute-done.10 = f32[8,104,256]{2,1,0:T(8,128)S(1)} collective-permute-done((f32[8,104,256]{2,1,0:T(8,128)S(1)}, f32[8,104,256]{2,1,0:T(8,128)S(1)}, u32[]{:S(2)}, u32[]{:S(2)}) %collective-permute-start.10) | collective-permute-done | bytes 852000 | tf_op jit(solution)/shard_map/ppermute | solution.py:42
  83.8 0.1 add.52
  83.9 29.6 %all_to_all.20.parts = f32[8,104,256]{2,1,0:T(8,128)S(1)} all-to-all(f32[8,104,256]{2,1,0:T(8,128)S(1)} %add.52), channel_id=1, replica_groups=mesh['z'=8,'y'=4,'c'=2,'x'=4] {'z'}, dimensions={0} | all-to-all | bytes 1703936 | tf_op jit(solution)/shard_map/all_to_all | solution.py:377
  113.5 0.9 shard_map.70
  114.4 2.2 %collective-permute-start.13 = (f32[16,256]{1,0:T(8,128)S(1)}, f32[16,256]{1,0:T(8,128)S(1)}, u32[]{:S(2)}, u32[]{:S(2)}) collective-permute-start(f32[16,256]{1,0:T(8,128)S(1)} %get-tuple-element.25), channel_id=1, source_target_pairs={{0,24},{8,0},{16,8},{24,16},{1,25},{9,1},{17,9},{25,17},{2,26},{10... | collective-permute-start | bytes 49160 | tf_op jit(solution)/shard_map/ppermute | solution.py:46
  116.6 0.0 collective-permute-start.12
  116.6 0.6 collective-permute-start.11
  117.2 3.5 %all-to-all-start.2 = ((f32[8,88,256]{2,1,0:T(8,128)}), f32[8,88,256]{2,1,0:T(8,128)S(1)}, u32[]{:S(2)}, u32[]{:S(2)}) async-start(f32[8,88,256]{2,1,0:T(8,128)} %get-tuple-element.24), calls=%async_computation.2 | async-start | bytes 1441792 | tf_op jit(solution)/shard_map/all_to_all | solution.py:379
  120.8 0.0 collective-permute-done.13
  120.8 0.0 collective-permute-done.12
  120.8 0.1 collective-permute-start.14
  120.9 2.6 %collective-permute-start.15 = (f32[4,16,256]{2,1,0:T(8,128)S(1)}, f32[4,16,256]{2,1,0:T(8,128)S(1)}, u32[]{:S(2)}, u32[]{:S(2)}) collective-permute-start(f32[4,16,256]{2,1,0:T(8,128)S(1)} %pad_maximum_fusion.2), channel_id=1, source_target_pairs={{0,2},{1,3},{2,0},{3,1},{4,6},{5,7},{6,4},{7,5},{8,10},{9,11},{10,... | collective-permute-start | bytes 196616 | tf_op jit(solution)/shard_map/ppermute | solution.py:46
  123.5 0.2 collective-permute-start.16
  123.7 1.5 collective-permute-done.14
  125.2 0.7 collective-permute-done.15
  125.9 1.0 collective-permute-done.16
  127.1 0.1 pad_maximum_fusion
  127.2 10.4 %shard_map.71 = f32[256,256]{1,0:T(8,128)S(1)} custom-call(f32[256,256]{1,0:T(8,128)S(1)} %bitcast.42), custom_call_target="tpu_custom_call" | custom-call | flops 100000000 | bytes 1000000 | tf_op jit(solution)/shard_map/pallas_call | solution.py:285
  137.6 3.5 %all-to-all-done.2 = f32[8,88,256]{2,1,0:T(8,128)S(1)} async-done(((f32[8,88,256]{2,1,0:T(8,128)}), f32[8,88,256]{2,1,0:T(8,128)S(1)}, u32[]{:S(2)}, u32[]{:S(2)}) %all-to-all-start.2) | async-done | bytes 720928 | tf_op jit(solution)/shard_map/all_to_all | solution.py:379
  141.1 0.5 multiply_reduce_fusion
  141.6 1.6 collective-permute-start.18
  143.3 1.1 collective-permute-start.19
  144.4 2.8 %collective-permute-start.17 = (f32[1,256]{1,0:T(1,128)S(1)}, f32[1,256]{1,0:T(1,128)S(1)}, u32[]{:S(2)}, u32[]{:S(2)}) collective-permute-start(f32[1,256]{1,0:T(1,128)S(1)} %bitcast.58), channel_id=1, source_target_pairs={{0,4},{4,0},{1,5},{5,1},{2,6},{6,2},{3,7},{7,3},{8,12},{12,8},{9,1... | collective-permute-start | bytes 3080 | tf_op jit(solution)/shard_map/ppermute | solution.py:42
  147.2 0.8 collective-permute-done.17
  148.0 10.5 %all_to_all.21 = f32[16,1,256]{2,1,0:T(1,128)S(1)} all-to-all(f32[16,1,256]{2,1,0:T(1,128)S(1)} %broadcast_in_dim.13), channel_id=1, replica_groups=mesh['z'=8,'y'=4,'c'=2,'x'=4] {'y','x'}, dimensions={0} | all-to-all | bytes 32768 | tf_op jit(solution)/shard_map/all_to_all | solution.py:38
  158.5 0.0 collective-permute-done.18.refs_1_
  158.5 0.8 slice.6
  159.3 0.3 collective-permute-start.20
  159.6 0.8 slice.7
  160.3 2.4 %collective-permute-start.21 = (f32[4,88,256]{2,1,0:T(8,128)}, f32[4,88,256]{2,1,0:T(8,128)S(1)}, u32[]{:S(2)}, u32[]{:S(2)}) collective-permute-start(f32[4,88,256]{2,1,0:T(8,128)} %slice.7), channel_id=1, source_target_pairs={{0,24},{8,0},{16,8},{24,16},{1,25},{9,1},{17,9},{25,17},{2,26},{10... | collective-permute-start | bytes 1081352 | tf_op jit(solution)/shard_map/ppermute | solution.py:46
  162.7 4.1 %collective-permute-start.22 = (f32[8,88,256]{2,1,0:T(8,128)S(1)}, f32[8,88,256]{2,1,0:T(8,128)S(1)}, u32[]{:S(2)}, u32[]{:S(2)}) collective-permute-start(f32[8,88,256]{2,1,0:T(8,128)S(1)} %bitcast.39), channel_id=1, source_target_pairs={{0,4},{4,0},{1,5},{5,1},{2,6},{6,2},{3,7},{7,3},{8,12},{12,8},{9,1... | collective-permute-start | bytes 2162696 | tf_op jit(solution)/shard_map/ppermute | solution.py:42
  166.8 0.5 collective-permute-start.24
  167.4 4.3 %collective-permute-start.25 = (f32[4,88,256]{2,1,0:T(8,128)S(1)}, f32[4,88,256]{2,1,0:T(8,128)S(1)}, u32[]{:S(2)}, u32[]{:S(2)}) collective-permute-start(f32[4,88,256]{2,1,0:T(8,128)S(1)} %collective-permute-done.20.refs_3_), channel_id=1, source_target_pairs={{0,4},{4,0},{1,5},{5,1},{2,6},{6,2},{3,7},{7,3},{8,12},{12,8},{9,1... | collective-permute-start | bytes 1081352 | tf_op jit(solution)/shard_map/ppermute | solution.py:42
  171.7 0.5 collective-permute-start.26
  172.2 0.4 broadcast_multiply_fusion
  172.6 0.7 bitcast_multiply_fusion
  173.2 0.2 collective-permute-done.26.refs_9_
  173.5 7.6 %shard_map.72 = (f32[128,5632]{1,0:T(8,128)}, f32[128,5632]{1,0:T(8,128)}) custom-call(s32[3]{0:T(128)S(1)} %pad_add_fusion.pos, f32[256,256]{1,0:T(8,128)S(1)} %pad_maximum_fusion.1.left, bf16[128,5632]{1,0:T(8,128)(2,1)} %grad.3, f32[128,5632]{1,0:T(8,128)} %mom.3, f32[128,5632]{1,0:T(8,128)} %wgt.1, f32[8,88,256]{2,1,0:T(8,128)S(1)} %bitcast.41, ...), custom_call_target="tpu_custom_call" | custom-call | flops 2214592512 | bytes 12976128 | tf_op jit(solution)/shard_map/pallas_call | solution.py:340
  (34 shorter events, 0.4 us)
Async XLA Ops:
  4.4 5.1 %copy-start = (f32[88,256]{1,0:T(8,128)S(1)}, f32[88,256]{1,0:T(8,128)}, u32[]{:S(2)}) copy-start(f32[88,256]{1,0:T(8,128)} %param.7) | copy-start | bytes 270340
  4.4 39.8 %all-to-all-start = ((f32[4,8,176,128]{3,2,1,0:T(8,128)}), f32[4,8,176,128]{3,2,1,0:T(8,128)S(1)}, u32[]{:S(2)}, u32[]{:S(2)}) async-start(f32[4,8,176,128]{3,2,1,0:T(8,128)} %shard_map.67), calls=%async_computation | async-start | bytes 5767168 | tf_op jit(solution)/shard_map/all_to_all | solution.py:363
  36.6 7.6 %collective-permute-start = (f32[8,88,256]{2,1,0:T(8,128)}, f32[8,88,256]{2,1,0:T(8,128)}, u32[]{:S(2)}, u32[]{:S(2)}) collective-permute-start(f32[8,88,256]{2,1,0:T(8,128)} %bitcast.4.mine), channel_id=1, source_target_pairs={{0,4},{4,0},{1,5},{5,1},{2,6},{6,2},{3,7},{7,3},{8,12},{12,8},{9,1... | collective-permute-start | bytes 2162696 | tf_op jit(solution)/shard_map/ppermute | solution.py:42
  47.1 6.4 %collective-permute-start.3 = (f32[128,256]{1,0:T(8,128)S(1)}, f32[128,256]{1,0:T(8,128)S(1)}, u32[]{:S(2)}, u32[]{:S(2)}) collective-permute-start(f32[128,256]{1,0:T(8,128)S(1)} %get-tuple-element.21), channel_id=1, source_target_pairs={{0,16},{8,24},{16,0},{24,8},{1,17},{9,25},{17,1},{25,9},{2,18},{10... | collective-permute-start | bytes 393224 | tf_op jit(solution)/shard_map/ppermute | solution.py:46
  50.6 6.5 %collective-permute-start.2 = (f32[128,256]{1,0:T(8,128)S(1)}, f32[128,256]{1,0:T(8,128)S(1)}, u32[]{:S(2)}, u32[]{:S(2)}) collective-permute-start(f32[128,256]{1,0:T(8,128)S(1)} %get-tuple-element.20), channel_id=1, source_target_pairs={{0,8},{8,16},{16,24},{24,0},{1,9},{9,17},{17,25},{25,1},{2,10},{10... | collective-permute-start | bytes 393224 | tf_op jit(solution)/shard_map/ppermute | solution.py:46
  50.7 6.4 %collective-permute-start.1 = (f32[128,256]{1,0:T(8,128)S(1)}, f32[128,256]{1,0:T(8,128)S(1)}, u32[]{:S(2)}, u32[]{:S(2)}) collective-permute-start(f32[128,256]{1,0:T(8,128)S(1)} %get-tuple-element.19), channel_id=1, source_target_pairs={{0,24},{8,0},{16,8},{24,16},{1,25},{9,1},{17,9},{25,17},{2,26},{10... | collective-permute-start | bytes 393224 | tf_op jit(solution)/shard_map/ppermute | solution.py:46
  57.1 4.5 %collective-permute-start.6 = (f32[128,256]{1,0:T(8,128)S(1)}, f32[128,256]{1,0:T(8,128)S(1)}, u32[]{:S(2)}, u32[]{:S(2)}) collective-permute-start(f32[128,256]{1,0:T(8,128)S(1)} %add_add_fusion.1), channel_id=1, source_target_pairs={{0,3},{1,0},{2,1},{3,2},{4,7},{5,4},{6,5},{7,6},{8,11},{9,8},{10,9... | collective-permute-start | bytes 393224 | tf_op jit(solution)/shard_map/ppermute | solution.py:46
  59.7 7.2 %collective-permute-start.4 = (f32[128,256]{1,0:T(8,128)S(1)}, f32[128,256]{1,0:T(8,128)S(1)}, u32[]{:S(2)}, u32[]{:S(2)}) collective-permute-start(f32[128,256]{1,0:T(8,128)S(1)} %add_add_fusion.1), channel_id=1, source_target_pairs={{0,1},{1,2},{2,3},{3,0},{4,5},{5,6},{6,7},{7,4},{8,9},{9,10},{10,1... | collective-permute-start | bytes 393224 | tf_op jit(solution)/shard_map/ppermute | solution.py:46
  59.7 7.2 %collective-permute-start.5 = (f32[128,256]{1,0:T(8,128)S(1)}, f32[128,256]{1,0:T(8,128)S(1)}, u32[]{:S(2)}, u32[]{:S(2)}) collective-permute-start(f32[128,256]{1,0:T(8,128)S(1)} %add_add_fusion.1), channel_id=1, source_target_pairs={{0,2},{1,3},{2,0},{3,1},{4,6},{5,7},{6,4},{7,5},{8,10},{9,11},{10,... | collective-permute-start | bytes 393224 | tf_op jit(solution)/shard_map/ppermute | solution.py:46
  66.9 5.1 %collective-permute-start.7 = (f32[128,256]{1,0:T(8,128)S(1)}, f32[128,256]{1,0:T(8,128)S(1)}, u32[]{:S(2)}, u32[]{:S(2)}) collective-permute-start(f32[128,256]{1,0:T(8,128)S(1)} %add_add_fusion.p0), channel_id=1, source_target_pairs={{0,8},{8,16},{16,24},{24,0},{1,9},{9,17},{17,25},{25,1},{2,10},{10... | collective-permute-start | bytes 393224 | tf_op jit(solution)/shard_map/ppermute | solution.py:46
  68.8 5.3 %collective-permute-start.8 = (f32[128,256]{1,0:T(8,128)S(1)}, f32[128,256]{1,0:T(8,128)S(1)}, u32[]{:S(2)}, u32[]{:S(2)}) collective-permute-start(f32[128,256]{1,0:T(8,128)S(1)} %add_add_fusion.p0), channel_id=1, source_target_pairs={{0,16},{8,24},{16,0},{24,8},{1,17},{9,25},{17,1},{25,9},{2,18},{10... | collective-permute-start | bytes 393224 | tf_op jit(solution)/shard_map/ppermute | solution.py:46
  70.3 4.1 %collective-permute-start.9 = (f32[128,256]{1,0:T(8,128)S(1)}, f32[128,256]{1,0:T(8,128)S(1)}, u32[]{:S(2)}, u32[]{:S(2)}) collective-permute-start(f32[128,256]{1,0:T(8,128)S(1)} %add_add_fusion.p0), channel_id=1, source_target_pairs={{0,24},{8,0},{16,8},{24,16},{1,25},{9,1},{17,9},{25,17},{2,26},{10... | collective-permute-start | bytes 393224 | tf_op jit(solution)/shard_map/ppermute | solution.py:46
  77.5 6.3 %collective-permute-start.10 = (f32[8,104,256]{2,1,0:T(8,128)S(1)}, f32[8,104,256]{2,1,0:T(8,128)S(1)}, u32[]{:S(2)}, u32[]{:S(2)}) collective-permute-start(f32[8,104,256]{2,1,0:T(8,128)S(1)} %get-tuple-element.23), channel_id=1, source_target_pairs={{0,4},{4,0},{1,5},{5,1},{2,6},{6,2},{3,7},{7,3},{8,12},{12,8},{9,1... | collective-permute-start | bytes 2555912 | tf_op jit(solution)/shard_map/ppermute | solution.py:42
  114.4 6.3 %collective-permute-start.13 = (f32[16,256]{1,0:T(8,128)S(1)}, f32[16,256]{1,0:T(8,128)S(1)}, u32[]{:S(2)}, u32[]{:S(2)}) collective-permute-start(f32[16,256]{1,0:T(8,128)S(1)} %get-tuple-element.25), channel_id=1, source_target_pairs={{0,24},{8,0},{16,8},{24,16},{1,25},{9,1},{17,9},{25,17},{2,26},{10... | collective-permute-start | bytes 49160 | tf_op jit(solution)/shard_map/ppermute | solution.py:46
  116.6 4.1 %collective-permute-start.12 = (f32[16,256]{1,0:T(8,128)S(1)}, f32[16,256]{1,0:T(8,128)S(1)}, u32[]{:S(2)}, u32[]{:S(2)}) collective-permute-start(f32[16,256]{1,0:T(8,128)S(1)} %get-tuple-element.25), channel_id=1, source_target_pairs={{0,16},{8,24},{16,0},{24,8},{1,17},{9,25},{17,1},{25,9},{2,18},{10... | collective-permute-start | bytes 49160 | tf_op jit(solution)/shard_map/ppermute | solution.py:46
  116.6 4.2 %collective-permute-start.11 = (f32[16,256]{1,0:T(8,128)S(1)}, f32[16,256]{1,0:T(8,128)S(1)}, u32[]{:S(2)}, u32[]{:S(2)}) collective-permute-start(f32[16,256]{1,0:T(8,128)S(1)} %get-tuple-element.25), channel_id=1, source_target_pairs={{0,8},{8,16},{16,24},{24,0},{1,9},{9,17},{17,25},{25,1},{2,10},{10... | collective-permute-start | bytes 49160 | tf_op jit(solution)/shard_map/ppermute | solution.py:46
  117.2 23.9 %all-to-all-start.2 = ((f32[8,88,256]{2,1,0:T(8,128)}), f32[8,88,256]{2,1,0:T(8,128)S(1)}, u32[]{:S(2)}, u32[]{:S(2)}) async-start(f32[8,88,256]{2,1,0:T(8,128)} %get-tuple-element.24), calls=%async_computation.2 | async-start | bytes 1441792 | tf_op jit(solution)/shard_map/all_to_all | solution.py:379
  120.8 4.4 %collective-permute-start.14 = (f32[4,16,256]{2,1,0:T(8,128)S(1)}, f32[4,16,256]{2,1,0:T(8,128)S(1)}, u32[]{:S(2)}, u32[]{:S(2)}) collective-permute-start(f32[4,16,256]{2,1,0:T(8,128)S(1)} %pad_maximum_fusion.2), channel_id=1, source_target_pairs={{0,1},{1,2},{2,3},{3,0},{4,5},{5,6},{6,7},{7,4},{8,9},{9,10},{10,1... | collective-permute-start | bytes 196616 | tf_op jit(solution)/shard_map/ppermute | solution.py:46
  120.9 5.0 %collective-permute-start.15 = (f32[4,16,256]{2,1,0:T(8,128)S(1)}, f32[4,16,256]{2,1,0:T(8,128)S(1)}, u32[]{:S(2)}, u32[]{:S(2)}) collective-permute-start(f32[4,16,256]{2,1,0:T(8,128)S(1)} %pad_maximum_fusion.2), channel_id=1, source_target_pairs={{0,2},{1,3},{2,0},{3,1},{4,6},{5,7},{6,4},{7,5},{8,10},{9,11},{10,... | collective-permute-start | bytes 196616 | tf_op jit(solution)/shard_map/ppermute | solution.py:46
  123.5 3.4 %collective-permute-start.16 = (f32[4,16,256]{2,1,0:T(8,128)S(1)}, f32[4,16,256]{2,1,0:T(8,128)S(1)}, u32[]{:S(2)}, u32[]{:S(2)}) collective-permute-start(f32[4,16,256]{2,1,0:T(8,128)S(1)} %pad_maximum_fusion.2), channel_id=1, source_target_pairs={{0,3},{1,0},{2,1},{3,2},{4,7},{5,4},{6,5},{7,6},{8,11},{9,8},{10,9... | collective-permute-start | bytes 196616 | tf_op jit(solution)/shard_map/ppermute | solution.py:46
  141.6 16.9 %collective-permute-start.18 = (f32[8,88,256]{2,1,0:T(8,128)S(1)}, f32[8,88,256]{2,1,0:T(8,128)S(1)}, u32[]{:S(2)}, u32[]{:S(2)}) collective-permute-start(f32[8,88,256]{2,1,0:T(8,128)S(1)} %bitcast.37), channel_id=1, source_target_pairs={{0,8},{8,16},{16,24},{24,0},{1,9},{9,17},{17,25},{25,1},{2,10},{10... | collective-permute-start | bytes 2162696 | tf_op jit(solution)/shard_map/ppermute | solution.py:46
  143.3 15.2 %collective-permute-start.19 = (f32[8,88,256]{2,1,0:T(8,128)S(1)}, f32[8,88,256]{2,1,0:T(8,128)S(1)}, u32[]{:S(2)}, u32[]{:S(2)}) collective-permute-start(f32[8,88,256]{2,1,0:T(8,128)S(1)} %bitcast.38), channel_id=1, source_target_pairs={{0,24},{8,0},{16,8},{24,16},{1,25},{9,1},{17,9},{25,17},{2,26},{10... | collective-permute-start | bytes 2162696 | tf_op jit(solution)/shard_map/ppermute | solution.py:46
  144.4 3.6 %collective-permute-start.17 = (f32[1,256]{1,0:T(1,128)S(1)}, f32[1,256]{1,0:T(1,128)S(1)}, u32[]{:S(2)}, u32[]{:S(2)}) collective-permute-start(f32[1,256]{1,0:T(1,128)S(1)} %bitcast.58), channel_id=1, source_target_pairs={{0,4},{4,0},{1,5},{5,1},{2,6},{6,2},{3,7},{7,3},{8,12},{12,8},{9,1... | collective-permute-start | bytes 3080 | tf_op jit(solution)/shard_map/ppermute | solution.py:42
  159.3 8.1 %collective-permute-start.20 = (f32[4,88,256]{2,1,0:T(8,128)}, f32[4,88,256]{2,1,0:T(8,128)S(1)}, u32[]{:S(2)}, u32[]{:S(2)}) collective-permute-start(f32[4,88,256]{2,1,0:T(8,128)} %slice.6), channel_id=1, source_target_pairs={{0,8},{8,16},{16,24},{24,0},{1,9},{9,17},{17,25},{25,1},{2,10},{10... | collective-permute-start | bytes 1081352 | tf_op jit(solution)/shard_map/ppermute | solution.py:46
  160.3 11.3 %collective-permute-start.21 = (f32[4,88,256]{2,1,0:T(8,128)}, f32[4,88,256]{2,1,0:T(8,128)S(1)}, u32[]{:S(2)}, u32[]{:S(2)}) collective-permute-start(f32[4,88,256]{2,1,0:T(8,128)} %slice.7), channel_id=1, source_target_pairs={{0,24},{8,0},{16,8},{24,16},{1,25},{9,1},{17,9},{25,17},{2,26},{10... | collective-permute-start | bytes 1081352 | tf_op jit(solution)/shard_map/ppermute | solution.py:46
  162.7 10.5 %collective-permute-start.22 = (f32[8,88,256]{2,1,0:T(8,128)S(1)}, f32[8,88,256]{2,1,0:T(8,128)S(1)}, u32[]{:S(2)}, u32[]{:S(2)}) collective-permute-start(f32[8,88,256]{2,1,0:T(8,128)S(1)} %bitcast.39), channel_id=1, source_target_pairs={{0,4},{4,0},{1,5},{5,1},{2,6},{6,2},{3,7},{7,3},{8,12},{12,8},{9,1... | collective-permute-start | bytes 2162696 | tf_op jit(solution)/shard_map/ppermute | solution.py:42
  166.8 6.7 %collective-permute-start.23 = (f32[8,88,256]{2,1,0:T(8,128)S(1)}, f32[8,88,256]{2,1,0:T(8,128)S(1)}, u32[]{:S(2)}, u32[]{:S(2)}) collective-permute-start(f32[8,88,256]{2,1,0:T(8,128)S(1)} %collective-permute-done.18.refs_1_), channel_id=1, source_target_pairs={{0,4},{4,0},{1,5},{5,1},{2,6},{6,2},{3,7},{7,3},{8,12},{12,8},{9,1... | collective-permute-start | bytes 2162696 | tf_op jit(solution)/shard_map/ppermute | solution.py:42
  166.8 6.7 %collective-permute-start.24 = (f32[8,88,256]{2,1,0:T(8,128)S(1)}, f32[8,88,256]{2,1,0:T(8,128)S(1)}, u32[]{:S(2)}, u32[]{:S(2)}) collective-permute-start(f32[8,88,256]{2,1,0:T(8,128)S(1)} %collective-permute-done.19.refs_2_), channel_id=1, source_target_pairs={{0,4},{4,0},{1,5},{5,1},{2,6},{6,2},{3,7},{7,3},{8,12},{12,8},{9,1... | collective-permute-start | bytes 2162696 | tf_op jit(solution)/shard_map/ppermute | solution.py:42
  167.4 5.9 %collective-permute-start.25 = (f32[4,88,256]{2,1,0:T(8,128)S(1)}, f32[4,88,256]{2,1,0:T(8,128)S(1)}, u32[]{:S(2)}, u32[]{:S(2)}) collective-permute-start(f32[4,88,256]{2,1,0:T(8,128)S(1)} %collective-permute-done.20.refs_3_), channel_id=1, source_target_pairs={{0,4},{4,0},{1,5},{5,1},{2,6},{6,2},{3,7},{7,3},{8,12},{12,8},{9,1... | collective-permute-start | bytes 1081352 | tf_op jit(solution)/shard_map/ppermute | solution.py:42
  171.7 1.8 %collective-permute-start.26 = (f32[4,88,256]{2,1,0:T(8,128)S(1)}, f32[4,88,256]{2,1,0:T(8,128)S(1)}, u32[]{:S(2)}, u32[]{:S(2)}) collective-permute-start(f32[4,88,256]{2,1,0:T(8,128)S(1)} %collective-permute-done.21.refs_4_), channel_id=1, source_target_pairs={{0,4},{4,0},{1,5},{5,1},{2,6},{6,2},{3,7},{7,3},{8,12},{12,8},{9,1... | collective-permute-start | bytes 1081352 | tf_op jit(solution)/shard_map/ppermute | solution.py:42
